TPU v7x, 128 devices: a whole 4x4x4 slice. The times are simulated.
128 devices in a mesh: grp: 8 (over z, core), ch: 16 (over y, x).
Axes of the slice: x: 4, y: 4, z: 4, core: 2. Of those that a mesh axis runs over, the one named last changes fastest.
Arguments:
- features: bfloat16 [256, 64, 512], P(('grp', 'ch')), may hold values from -6 to 6
- live_counts: int32 [128], P(('grp', 'ch')), may hold values from 1 to 2, as said below
- neighbours: int32 [256, 27], P(('grp', 'ch')), may hold values from -1 to 255, as said below
- w_first: bfloat16 [27, 64, 64], replicated, may hold values from -0.21875 to 0.21875
- w_second: bfloat16 [27, 64, 64], replicated, may hold values from -0.21875 to 0.21875
- w_middle: bfloat16 [27, 128, 64], replicated, may hold values from -0.3125 to 0.3125
- w_coarse: bfloat16 [27, 256, 128], P(None, 'ch'), may hold values from -0.21875 to 0.21875
- w_project: bfloat16 [256, 64], P('ch'), may hold values from -0.75 to 0.75
- w_output: bfloat16 [64, 128], replicated, may hold values from -0.5 to 0.5
Outputs:
- mixed_out: bfloat16 [256, 64, 512], P(('grp', 'ch'))
Inputs may be any that keep to these rules, and one draw needn't show every extreme that they name: Device d holds its live blocks in slots d * 2 to d * 2 + live_counts[d] - 1; the rest are padding. In every group of devices along ch one device holds exactly 2. `neighbours`: the live blocks occupy distinct positions of a lattice of 16 x 16 x (2 times the size of grp) positions; the devices with grp index g hold exactly the blocks of layers g * 2 to (g + 1) * 2 - 1 along z. Within a group, the device with ch index m (of n) holds blocks only in the tile of x from floor(2 m / n) * 8 to that plus 16 / 2 - 1 and y from (m mod (n / 2)) * 2 * 16 / n to that plus 2 * 16 / n - 1. For a live block b, entry 9 (dx + 1) + 3 (dy + 1) + dz + 1 is the block at b's position plus (dx, dy, dz), or -1 where that position is empty or off the lattice; entry 13 is b itself. Rows of padding slots are all -1, and no entry names a padding slot.
All inputs are finite; a program needn't handle non-finite values.
Results may differ from a plain program's by a relative error of at most 0.013.
Values may be sent and summed in bfloat16 or wider, within the bound.
No kernel may reach another device: no remote copies, remote signals or barrier semaphores. Data moves between devices by JAX's collectives and lax.ppermute only.
A program may use at most 128 MiB of HBM per device.

v0:
```python
import functools

import jax
import jax.numpy as jnp
import numpy as np
from jax import lax
from jax.experimental import pallas as pl
from jax.experimental.pallas import tpu as pltpu
from jax.sharding import PartitionSpec as P

AXES = ("grp", "ch")
BF = jnp.bfloat16
F32 = jnp.float32
VMEM = pl.BlockSpec(memory_space=pltpu.VMEM)
SMEM = pl.BlockSpec(memory_space=pltpu.SMEM)
ANY = pl.BlockSpec(memory_space=pl.ANY)
PARAMS = pltpu.CompilerParams(vmem_limit_bytes=48 * 2**20)

ATOM = (2, 16, 128)
ABSENT = 96


def tables():
    step = (-1, 0, 0, 1)
    half = (1, 0, 1, 0)
    atoms = np.zeros((4, 128, 54), np.int32)
    for b in range(2):
        for z in range(4):
            for x in range(4):
                for y in range(4):
                    a = ((b * 4 + z) * 4 + x) * 4 + y
                    n = b * 27 + 9 * (step[x] + 1) + 3 * (step[y] + 1) + step[z] + 1
                    atoms[:, a, n] = (1, half[z], half[y], half[x])
    taps = np.zeros((432, 54), np.int32)
    inner = np.zeros((432, 1), np.int32)
    for t in range(27):
        tx, ty, tz = t // 9, t // 3 % 3, t % 3
        for r in range(16):
            y, b, z, x = r // 8, r // 4 % 2, r // 2 % 2, r % 2
            pz, px, py = z + tz, x + tx, y + ty
            n = b * 27 + 9 * (step[px] + 1) + 3 * (step[py] + 1) + step[pz] + 1
            taps[t * 16 + r, n] = 1
            inner[t * 16 + r] = half[py] * 8 + half[pz] * 2 + half[px]
    return atoms, taps, inner


def pairs_for(step_h, step_j, step_g, sizes):
    groups, members = sizes
    tiles = members // 2
    found = []
    for g in range(groups):
        for m in range(members):
            h, j = m // tiles, m % tiles
            if 0 <= j + step_j < tiles and 0 <= g + step_g < groups:
                to = (1 - h if step_h else h) * tiles + j + step_j
                found.append((g * members + m, (g + step_g) * members + to))
    return found


def gelu(v):
    return jax.nn.gelu(v, approximate=True)


def halves(axis_size_lanes):
    return lax.broadcasted_iota(jnp.int32, (1, axis_size_lanes), 1) < 64


def dot(a, b):
    return jnp.dot(a, b, preferred_element_type=F32)


def pack_kernel(half_ref, features_ref, atoms_ref, send_ref, turned):
    h = half_ref[0]
    turned[...] = features_ref[...].astype(F32).reshape(128, 512).T
    low = halves(128)
    upper = lax.broadcasted_iota(jnp.int32, (1, 8, 1), 1) < 4
    for pair in range(4):
        even = turned[pl.ds(2 * pair, 64, stride=8), :]
        odd = turned[pl.ds(2 * pair + 1, 64, stride=8), :]
        first = jnp.where(low, even, pltpu.roll(odd, 64, 1))
        second = jnp.where(low, pltpu.roll(even, 64, 1), odd)
        for b, rows in enumerate((first, second)):
            rows = rows.reshape(4, 2, 8, 128)
            a, c = rows[:, 0], rows[:, 1]
            near = jnp.where(upper, a, pltpu.roll(c, 4, 1))
            far = jnp.where(upper, pltpu.roll(a, 4, 1), c)
            for yh, part in enumerate((near, far)):
                part = part.reshape(2, 16, 128).astype(BF)
                for xh in range(2):
                    atoms_ref[pair // 2, yh, xh, b, pair % 2] = part[xh]
                send_ref[pair // 2, yh, b, pair % 2] = jnp.where(h == 0, part[1], part[0])


def widen_kernel(weight_ref, out_ref, *, outs):
    zero = jnp.zeros((outs, 64), F32)
    for tx in range(3):
        for ty in range(3):
            w = [weight_ref[9 * tx + 3 * ty + tz].astype(F32) for tz in range(3)]
            for pair, blocks in enumerate(
                (((w[0], w[1]), (zero, w[0])), ((w[2], zero), (w[1], w[2])))
            ):
                wide = jnp.concatenate([jnp.concatenate(two, axis=1) for two in blocks], axis=0)
                row = tx * 256 + pair * 128
                out_ref[row : row + 128, ty * 2 * outs : (ty + 1) * 2 * outs] = wide.T.astype(BF)


def leaf_conv(source, b, k, length, weight_ref):
    parts = [
        source[b, k + dk, dx : dx + length].reshape(length * 16, 128)
        for dx in range(3)
        for dk in range(2)
    ]
    wide = dot(jnp.concatenate(parts, axis=1), weight_ref[...])
    return (
        wide[:, 128:256]
        + pltpu.roll(wide[:, :128], 1, 0)
        + pltpu.roll(wide[:, 256:], length * 16 - 1, 0)
    )


def main_kernel(
    atom_ref, present_ref, own, below_y, above_y, below_z, above_z, w1, w2, w3,
    skip_ref, coarse_ref,
    table, wide, first, second, masks, rows_a, middle_in, rows_b, turned, sems,
):
    copies = [
        pltpu.make_async_copy(
            own.at[zh, yh], table.at[pl.ds((zh * 4 + yh) * 6, 6)], sems.at[zh * 2 + yh]
        )
        for zh in range(2)
        for yh in range(2)
    ]
    for n, source in enumerate((below_y, above_y)):
        copies += [
            pltpu.make_async_copy(
                source.at[zh], table.at[pl.ds((zh * 4 + 2 + n) * 6, 6)], sems.at[4 + n * 2 + zh]
            )
            for zh in range(2)
        ]
    for n, source in enumerate((below_z, above_z)):
        copies.append(
            pltpu.make_async_copy(source, table.at[pl.ds(48 + n * 24, 24)], sems.at[8 + n])
        )
    for copy in copies:
        copy.start()
    table[ABSENT] = jnp.zeros(ATOM, BF)

    low = halves(128)
    y_row = lax.broadcasted_iota(jnp.int32, (16, 128), 0)
    for b in range(2):
        for dx in range(3):
            of_z = []
            for dz in range(3):
                p = [
                    present_ref[b * 27 + 9 * dx + 3 * dy + dz].astype(F32) for dy in range(3)
                ]
                of_z.append(jnp.where(y_row < 4, p[0], jnp.where(y_row < 12, p[1], p[2])))
            masks[b, 0, dx] = of_z[0]
            masks[b, 1, dx] = jnp.where(low, of_z[0], of_z[1])
            masks[b, 2, dx] = of_z[1]
            masks[b, 3, dx] = jnp.where(low, of_z[1], of_z[2])
            masks[b, 4, dx] = of_z[2]

    for copy in copies:
        copy.wait()

    upper = lax.broadcasted_iota(jnp.int32, (1, 1, 8, 1), 2) < 4
    for b in range(2):
        for z in range(4):
            for x in range(4):
                base = ((b * 4 + z) * 4 + x) * 4
                a = [
                    table[atom_ref[base + y]].astype(F32).reshape(2, 2, 8, 128) for y in range(4)
                ]
                r = [pltpu.roll(v.reshape(4, 8, 128), 4, 1).reshape(2, 2, 8, 128) for v in a]
                even = jnp.concatenate(
                    [jnp.where(upper, a[0], r[1]), jnp.where(upper, a[2], r[3])], axis=2
                ).astype(BF)
                odd = jnp.concatenate(
                    [jnp.where(upper, r[0], a[1]), jnp.where(upper, r[2], a[3])], axis=2
                ).astype(BF)
                for pair in range(2):
                    for k in range(2):
                        wide[b, 2 * z + pair, 4 * x + 2 * k] = even[pair, k]
                        wide[b, 2 * z + pair, 4 * x + 2 * k + 1] = odd[pair, k]

    def masked(value, b, pattern, edge):
        mask = [masks[b, pattern, dx][None] for dx in range(3)]
        value = value.reshape(8 + 2 * edge, 16, 128)
        return jnp.concatenate(
            [value[:edge] * mask[0], value[edge : edge + 8] * mask[1], value[edge + 8 :] * mask[2]],
            axis=0,
        )

    for b in range(2):

        def first_step(k, _, b=b):
            value = gelu(leaf_conv(wide, b, k, 14, w1))
            pattern = jnp.minimum(k, 2) + jnp.maximum(k - 4, 0)
            first[b, k] = masked(value, b, pattern, 3).astype(BF)
            return 0

        lax.fori_loop(0, 7, first_step, 0)

    for b in range(2):

        def second_step(k, _, b=b):
            value = gelu(leaf_conv(first, b, k, 12, w2))
            pattern = 2 * (jnp.minimum(k, 1) + jnp.maximum(k - 4, 0))
            second[b, k] = masked(value, b, pattern, 2).astype(BF)
            return 0

        lax.fori_loop(0, 6, second_step, 0)

    for b in range(2):
        layers = []
        for k in range(6):
            v = second[b, k].astype(F32)
            v = (v.reshape(6, 2, 16, 128)[:, 0] + v.reshape(6, 2, 16, 128)[:, 1]).reshape(96, 128)
            v = v + pltpu.roll(v, 64, 1)
            rows_a[b, k] = v + pltpu.roll(v, 95, 0)
            layers.append((rows_a[b, k, pl.ds(0, 48, stride=2), :] * 0.125).astype(BF).astype(F32))
        for pair in range(3):
            middle_in[b, pair] = jnp.where(low, layers[2 * pair], layers[2 * pair + 1])

    operands = []
    for b in range(2):
        for k in range(2):
            operands.append(
                jnp.concatenate(
                    [
                        middle_in[b, k + dk, dx * 8 : dx * 8 + 32]
                        for dx in range(3)
                        for dk in range(2)
                    ],
                    axis=1,
                )
            )
    deep = dot(jnp.concatenate(operands, axis=0).astype(BF), w3[...])
    deep = (
        deep[:, 256:512] + pltpu.roll(deep[:, :256], 1, 0) + pltpu.roll(deep[:, 512:], 127, 0)
    )
    deep = gelu(deep).astype(BF).astype(F32)
    deep = (deep[:, :128] + deep[:, 128:]).reshape(8, 2, 8, 128)
    deep = (deep[:, 0] + deep[:, 1]).reshape(64, 128)
    rows_b[...] = deep + pltpu.roll(deep, 63, 0)
    coarse_ref[...] = (
        jnp.concatenate(
            [rows_b[pl.ds(2, 8, stride=8), :], rows_b[pl.ds(4, 8, stride=8), :]], axis=0
        )
        * 0.125
    ).astype(BF)

    for pair in range(4):
        v = [
            second[b, 1 + pair, 2:10].astype(F32)[:, 4:12, :].reshape(64, 128) for b in range(2)
        ]
        turned[pl.ds(2 * pair, 64, stride=8), :] = jnp.where(low, v[0], pltpu.roll(v[1], 64, 1))
        turned[pl.ds(2 * pair + 1, 64, stride=8), :] = jnp.where(
            low, pltpu.roll(v[0], 64, 1), v[1]
        )
    skip_ref[...] = turned[...].T.astype(BF).reshape(2, 64, 512)


def last_kernel(live_ref, tap_ref, own, below, above, weights, w_output, skip_ref, out_ref):
    tiles = jnp.concatenate([r[...].reshape(96, 128) for r in (own, below, above)], axis=0)
    chosen = (tap_ref[...] == lax.broadcasted_iota(jnp.int32, (432, 288), 1)).astype(F32).astype(BF)
    taps = dot(chosen, tiles).astype(BF)
    total = jnp.zeros((16, 256), F32)
    for t in range(27):
        total = total + lax.dot_general(
            taps[t * 16 : (t + 1) * 16],
            weights[:, t].reshape(256, 128),
            (((1,), (1,)), ((), ())),
            preferred_element_type=F32,
        )
    hidden = gelu(total).astype(BF)
    coarse = dot(hidden, weights[:, 27].reshape(256, 128)).astype(BF).astype(F32)
    coarse = coarse.T[:64].astype(BF)
    row = lax.broadcasted_iota(jnp.int32, (16, 512), 0)
    voxel = lax.broadcasted_iota(jnp.int32, (16, 512), 1)
    place = ((voxel >> 5) & 1) * 8 + ((voxel >> 2) & 1) * 2 + ((voxel >> 8) & 1)
    for b in range(2):
        spread = (row == place + b * 4).astype(F32).astype(BF)
        widened = dot(coarse, spread).astype(BF)
        mixed = dot(w_output[...], jnp.concatenate([skip_ref[b], widened], axis=0))
        mixed = jnp.where(b < live_ref[0], mixed, 0.0)
        out_ref[b] = mixed.astype(BF)


def shape(dims, kind=BF):
    return jax.ShapeDtypeStruct(dims, kind)


def widened_weight(weight, outs):
    return pl.pallas_call(
        functools.partial(widen_kernel, outs=outs),
        out_shape=shape((768, 6 * outs)),
        in_specs=[VMEM],
        out_specs=VMEM,
        compiler_params=PARAMS,
    )(weight)


def shards(
    features, live_counts, neighbours, w_first, w_second, w_middle, w_coarse, w_project, w_output
):
    sizes = (lax.axis_size("grp"), lax.axis_size("ch"))
    g, m = lax.axis_index("grp"), lax.axis_index("ch")
    h, j = m // 8, m % 8

    def moved(value, step_h, step_j, step_g):
        return lax.ppermute(value, AXES, pairs_for(step_h, step_j, step_g, sizes))

    shard = jnp.concatenate(
        [w_coarse, jnp.pad(w_project, ((0, 0), (0, 64)))[None]], axis=0
    )
    weights = lax.all_gather(shard, "ch", axis=0)

    atoms, send = pl.pallas_call(
        pack_kernel,
        out_shape=(shape((2, 2, 2, 2) + ATOM), shape((2, 2, 2) + ATOM)),
        in_specs=[SMEM, VMEM],
        out_specs=(VMEM, VMEM),
        scratch_shapes=[pltpu.VMEM((512, 128), F32)],
        compiler_params=PARAMS,
    )(h[None].astype(jnp.int32), features)
    beside = moved(send, 1, 0, 0)
    own = jnp.concatenate([atoms, beside[:, :, None]], axis=2)
    below_y = moved(own[:, 1], 0, 1, 0)
    above_y = moved(own[:, 0], 0, -1, 0)
    whole = [jnp.concatenate([own[z], below_y[z][None], above_y[z][None]], axis=0) for z in (0, 1)]
    below_z = moved(whole[1], 0, 0, 1)
    above_z = moved(whole[0], 0, 0, -1)

    atom_table, tap_table, inner = tables()
    entry = neighbours.reshape(54)
    present = entry >= 0
    group = entry // 32 - g
    member = entry % 32 // 2
    slot = entry % 2
    other = member // 8 != h
    tile = member % 8 - j
    base = (
        jnp.where(group == 0, 0, jnp.where(group < 0, 48, 72))
        + jnp.where(tile == 0, 0, jnp.where(tile < 0, 12, 18))
        + jnp.where(other, 4, 0)
        + slot
    )
    kept = jnp.stack(
        [
            jnp.where(present, base, ABSENT),
            jnp.where(present & (group == 0), 24, 0),
            jnp.where(present & (tile == 0), 6, 0),
            jnp.where(present & ~other, 2, 0),
        ]
    )
    atom_rows = jnp.sum(jnp.asarray(atom_table) * kept[:, None, :], axis=(0, 2))
    code = (
        jnp.where(group == 0, 0, jnp.where(group < 0, 6, 12))
        + jnp.where(tile == 0, 0, jnp.where(tile < 0, 2, 4))
        + jnp.where(other, 1, 0)
    ) * 16 + slot * 4
    code = jnp.where(present, code, -4096)
    tap_rows = jnp.sum(jnp.asarray(tap_table) * code[None], axis=1, keepdims=True) + inner

    w1 = widened_weight(w_first, 64)
    w2 = widened_weight(w_second, 64)
    w3 = widened_weight(w_middle, 128)
    skip, coarse = pl.pallas_call(
        main_kernel,
        out_shape=(shape((2, 64, 512)), shape((16, 128))),
        in_specs=[SMEM] * 2 + [ANY] * 5 + [VMEM] * 3,
        out_specs=(VMEM, VMEM),
        scratch_shapes=[
            pltpu.VMEM((97,) + ATOM, BF),
            pltpu.VMEM((2, 8, 16, 16, 128), BF),
            pltpu.VMEM((2, 7, 14, 16, 128), BF),
            pltpu.VMEM((2, 6, 12, 16, 128), BF),
            pltpu.VMEM((2, 5, 3, 16, 128), F32),
            pltpu.VMEM((2, 6, 96, 128), F32),
            pltpu.VMEM((2, 3, 48, 128), F32),
            pltpu.VMEM((64, 128), F32),
            pltpu.VMEM((512, 128), F32),
            pltpu.SemaphoreType.DMA((10,)),
        ],
        compiler_params=PARAMS,
    )(
        atom_rows,
        present.astype(jnp.int32),
        own.reshape((2, 2, 6) + ATOM),
        below_y.reshape((2, 6) + ATOM),
        above_y.reshape((2, 6) + ATOM),
        below_z.reshape((24,) + ATOM),
        above_z.reshape((24,) + ATOM),
        w1,
        w2,
        w3,
    )

    both = jnp.stack([coarse, moved(coarse, 1, 0, 0)])
    layer = jnp.concatenate([both, moved(both, 0, 1, 0), moved(both, 0, -1, 0)], axis=0)
    below, above = moved(layer, 0, 0, 1), moved(layer, 0, 0, -1)
    return pl.pallas_call(
        last_kernel,
        out_shape=shape((2, 64, 512)),
        in_specs=[SMEM] + [VMEM] * 7,
        out_specs=VMEM,
        compiler_params=PARAMS,
    )(live_counts, tap_rows, layer, below, above, weights, w_output, skip)


def solution(mesh):
    return jax.shard_map(
        shards,
        mesh=mesh,
        in_specs=(
            P(AXES, None, None),
            P(AXES),
            P(AXES, None),
            P(),
            P(),
            P(),
            P(None, "ch", None),
            P("ch", None),
            P(),
        ),
        out_specs=P(AXES, None, None),
        check_vma=False,
    )
```

profile of v0, /device:TPU:1, one launch (start us, length us, event | category | flops | bytes accessed | tf_op | source)
XLA Modules:
  0.0 84.4 jit_solution(2745056941289962198)
XLA Ops:
  6.5 0.7 pad_bitcast_fusion
  7.2 1.6 %pad_maximum_fusion.3 = bf16[28,16,128]{2,1,0:T(8,128)(2,1)} fusion(bf16[1,16,128]{2,1,0:T(8,128)(2,1)S(1)} %pad_bitcast_fusion, bf16[27,16,128]{2,1,0:T(8,128)(2,1)} %param.18), kind=kLoop, calls=%fused_computation.11 | loop fusion | flops 57344 | bytes 229376 | tf_op jit(solution)/shard_map/concatenate | solution.py:315
  8.8 0.9 %copy-done.3 = bf16[2,64,512]{2,1,0:T(8,128)(2,1)S(1)} copy-done((bf16[2,64,512]{2,1,0:T(8,128)(2,1)S(1)}, bf16[2,64,512]{2,1,0:T(8,128)(2,1)}, u32[]{:S(2)}) %copy-start.3) | copy-done | bytes 131096
  9.8 0.2 shard_map.118
  10.0 3.8 %collective-permute-start = (bf16[2,2,2,2,16,128]{5,4,3,2,1,0:T(8,128)(2,1)S(1)}, bf16[2,2,2,2,16,128]{5,4,3,2,1,0:T(8,128)(2,1)S(1)}, u32[]{:S(2)}, u32[]{:S(2)}) collective-permute-start(bf16[2,2,2,2,16,128]{5,4,3,2,1,0:T(8,128)(2,1)S(1)} %get-tuple-element.10), channel_id=1, source_target_pairs={{0,8},{1,9},{2,10},{3,11},{4,12},{5,13},{6,14},{7,15},{8,0},{9,1},... | collective-permute-start | bytes 196616 | tf_op jit(solution)/shard_map/ppermute | solution.py:313
  13.9 0.8 reshape.413
  14.6 0.8 reshape.412
  15.5 1.4 %copy.31.weight_ref = bf16[27,128,64]{2,1,0:T(8,128)(2,1)S(1)} copy(bf16[27,128,64]{1,2,0:T(8,128)(2,1)} %param.17) | data formatting | bytes 884736 | tf_op args[5]
  17.0 0.6 shard_map.121.w3
  17.7 0.6 shard_map.119.w1
  18.3 0.6 shard_map.120.w2
  18.9 3.1 %collective-permute-start.1 = (bf16[2,3,2,2,16,128]{5,4,3,2,1,0:T(8,128)(2,1)S(1)}, bf16[2,3,2,2,16,128]{5,4,3,2,1,0:T(8,128)(2,1)S(1)}, u32[]{:S(2)}, u32[]{:S(2)}) collective-permute-start(bf16[2,3,2,2,16,128]{5,4,3,2,1,0:T(8,128)(2,1)S(1)} %get-tuple-element.20), channel_id=1, source_target_pairs={{0,1},{1,2},{2,3},{3,4},{4,5},{5,6},{6,7},{8,9},{9,10},{10,11},{11... | collective-permute-start | bytes 294920 | tf_op jit(solution)/shard_map/ppermute | solution.py:313
  22.0 1.3 %collective-permute-start.2 = (bf16[2,3,2,2,16,128]{5,4,3,2,1,0:T(8,128)(2,1)S(1)}, bf16[2,3,2,2,16,128]{5,4,3,2,1,0:T(8,128)(2,1)S(1)}, u32[]{:S(2)}, u32[]{:S(2)}) collective-permute-start(bf16[2,3,2,2,16,128]{5,4,3,2,1,0:T(8,128)(2,1)S(1)} %get-tuple-element.19), channel_id=1, source_target_pairs={{1,0},{2,1},{3,2},{4,3},{5,4},{6,5},{7,6},{9,8},{10,9},{11,10},{12... | collective-permute-start | bytes 294920 | tf_op jit(solution)/shard_map/ppermute | solution.py:313
  23.3 0.3 collective-permute-done.1
  23.6 4.1 %collective-permute-done.2 = bf16[2,3,2,2,16,128]{5,4,3,2,1,0:T(8,128)(2,1)S(1)} collective-permute-done((bf16[2,3,2,2,16,128]{5,4,3,2,1,0:T(8,128)(2,1)S(1)}, bf16[2,3,2,2,16,128]{5,4,3,2,1,0:T(8,128)(2,1)S(1)}, u32[]{:S(2)}, u32[]{:S(2)}) %collective-permute-start.2) | collective-permute-done | bytes 98336 | tf_op jit(solution)/shard_map/ppermute | solution.py:313
  27.8 4.1 %collective-permute-start.4 = (bf16[4,3,2,2,16,128]{5,4,3,2,1,0:T(8,128)(2,1)S(1)}, bf16[4,3,2,2,16,128]{5,4,3,2,1,0:T(8,128)(2,1)S(1)}, u32[]{:S(2)}, u32[]{:S(2)}) collective-permute-start(bf16[4,3,2,2,16,128]{5,4,3,2,1,0:T(8,128)(2,1)S(1)} %pad_maximum_fusion.2), channel_id=1, source_target_pairs={{16,0},{17,1},{18,2},{19,3},{20,4},{21,5},{22,6},{23,7},{24,8},{25... | collective-permute-start | bytes 589832 | tf_op jit(solution)/shard_map/ppermute | solution.py:313
  32.0 3.5 %collective-permute-start.3 = (bf16[4,3,2,2,16,128]{5,4,3,2,1,0:T(8,128)(2,1)S(1)}, bf16[4,3,2,2,16,128]{5,4,3,2,1,0:T(8,128)(2,1)S(1)}, u32[]{:S(2)}, u32[]{:S(2)}) collective-permute-start(bf16[4,3,2,2,16,128]{5,4,3,2,1,0:T(8,128)(2,1)S(1)} %pad_maximum_fusion.1), channel_id=1, source_target_pairs={{0,16},{1,17},{2,18},{3,19},{4,20},{5,21},{6,22},{7,23},{8,24},{9,... | collective-permute-start | bytes 589832 | tf_op jit(solution)/shard_map/ppermute | solution.py:313
  35.5 0.1 multiply_reduce_fusion.1.atom_ref
  35.7 1.2 %collective-permute-done.4 = bf16[4,3,2,2,16,128]{5,4,3,2,1,0:T(8,128)(2,1)S(1)} collective-permute-done((bf16[4,3,2,2,16,128]{5,4,3,2,1,0:T(8,128)(2,1)S(1)}, bf16[4,3,2,2,16,128]{5,4,3,2,1,0:T(8,128)(2,1)S(1)}, u32[]{:S(2)}, u32[]{:S(2)}) %collective-permute-start.4) | collective-permute-done | bytes 196640 | tf_op jit(solution)/shard_map/ppermute | solution.py:313
  36.9 1.2 %collective-permute-done.3 = bf16[4,3,2,2,16,128]{5,4,3,2,1,0:T(8,128)(2,1)S(1)} collective-permute-done((bf16[4,3,2,2,16,128]{5,4,3,2,1,0:T(8,128)(2,1)S(1)}, bf16[4,3,2,2,16,128]{5,4,3,2,1,0:T(8,128)(2,1)S(1)}, u32[]{:S(2)}, u32[]{:S(2)}) %collective-permute-start.3) | collective-permute-done | bytes 196640 | tf_op jit(solution)/shard_map/ppermute | solution.py:313
  38.1 11.8 %shard_map.122 = (bf16[2,64,512]{2,1,0:T(8,128)(2,1)S(1)}, bf16[16,128]{1,0:T(8,128)(2,1)S(1)}) custom-call(s32[128]{0:T(128)S(1)} %multiply_reduce_fusion.1.atom_ref, s32[54]{0:T(128)S(1)} %compare_convert_fusion.present_ref, bf16[2,2,6,2,16,128]{5,4,3,2,1,0:T(8,128)(2,1)S(1)} %bitcast.28, bf16[2,6,2,16,128]{4,3,2,1,0:T(8,128)(2,1)S(1)} %bitcast.29, ...), custom_call_target="tpu_custom_call" | custom-call | tf_op jit(solution)/shard_map/pallas_call | solution.py:370
  49.9 0.3 collective-permute-start.5
  50.1 3.9 %collective-permute-done.5 = bf16[16,128]{1,0:T(8,128)(2,1)S(1)} collective-permute-done((bf16[16,128]{1,0:T(8,128)(2,1)S(1)}, bf16[16,128]{1,0:T(8,128)(2,1)S(1)}, u32[]{:S(2)}, u32[]{:S(2)}) %collective-permute-start.5) | collective-permute-done | bytes 4128 | tf_op jit(solution)/shard_map/ppermute | solution.py:313
  54.0 3.1 %collective-permute-start.6 = (bf16[2,16,128]{2,1,0:T(8,128)(2,1)S(1)}, bf16[2,16,128]{2,1,0:T(8,128)(2,1)S(1)}, u32[]{:S(2)}, u32[]{:S(2)}) collective-permute-start(bf16[2,16,128]{2,1,0:T(8,128)(2,1)S(1)} %pad_maximum_fusion.5), channel_id=1, source_target_pairs={{0,1},{1,2},{2,3},{3,4},{4,5},{5,6},{6,7},{8,9},{9,10},{10,11},{11... | collective-permute-start | bytes 24584 | tf_op jit(solution)/shard_map/ppermute | solution.py:313
  57.2 1.3 %collective-permute-start.7 = (bf16[2,16,128]{2,1,0:T(8,128)(2,1)S(1)}, bf16[2,16,128]{2,1,0:T(8,128)(2,1)S(1)}, u32[]{:S(2)}, u32[]{:S(2)}) collective-permute-start(bf16[2,16,128]{2,1,0:T(8,128)(2,1)S(1)} %pad_maximum_fusion.5), channel_id=1, source_target_pairs={{1,0},{2,1},{3,2},{4,3},{5,4},{6,5},{7,6},{9,8},{10,9},{11,10},{12... | collective-permute-start | bytes 24584 | tf_op jit(solution)/shard_map/ppermute | solution.py:313
  58.5 3.0 %collective-permute-done.7 = bf16[2,16,128]{2,1,0:T(8,128)(2,1)S(1)} collective-permute-done((bf16[2,16,128]{2,1,0:T(8,128)(2,1)S(1)}, bf16[2,16,128]{2,1,0:T(8,128)(2,1)S(1)}, u32[]{:S(2)}, u32[]{:S(2)}) %collective-permute-start.7) | collective-permute-done | bytes 8224 | tf_op jit(solution)/shard_map/ppermute | solution.py:313
  61.6 6.9 %collective-permute-start.8 = (bf16[6,16,128]{2,1,0:T(8,128)(2,1)S(1)}, bf16[6,16,128]{2,1,0:T(8,128)(2,1)S(1)}, u32[]{:S(2)}, u32[]{:S(2)}) collective-permute-start(bf16[6,16,128]{2,1,0:T(8,128)(2,1)S(1)} %pad_maximum_fusion.4.own), channel_id=1, source_target_pairs={{0,16},{1,17},{2,18},{3,19},{4,20},{5,21},{6,22},{7,23},{8,24},{9,... | collective-permute-start | bytes 73736 | tf_op jit(solution)/shard_map/ppermute | solution.py:313
  68.5 1.9 %collective-permute-start.9 = (bf16[6,16,128]{2,1,0:T(8,128)(2,1)S(1)}, bf16[6,16,128]{2,1,0:T(8,128)(2,1)S(1)}, u32[]{:S(2)}, u32[]{:S(2)}) collective-permute-start(bf16[6,16,128]{2,1,0:T(8,128)(2,1)S(1)} %pad_maximum_fusion.4.own), channel_id=1, source_target_pairs={{16,0},{17,1},{18,2},{19,3},{20,4},{21,5},{22,6},{23,7},{24,8},{25... | collective-permute-start | bytes 73736 | tf_op jit(solution)/shard_map/ppermute | solution.py:313
  70.6 0.1 copy.32.tap_ref
  71.4 2.3 %collective-permute-done.9.above = bf16[6,16,128]{2,1,0:T(8,128)(2,1)S(1)} collective-permute-done((bf16[6,16,128]{2,1,0:T(8,128)(2,1)S(1)}, bf16[6,16,128]{2,1,0:T(8,128)(2,1)S(1)}, u32[]{:S(2)}, u32[]{:S(2)}) %collective-permute-start.9) | collective-permute-done | bytes 24608 | tf_op jit(solution)/shard_map/ppermute | solution.py:313
  73.7 1.5 %copy-done = bf16[448,16,128]{2,1,0:T(8,128)(2,1)S(1)} copy-done((bf16[448,16,128]{2,1,0:T(8,128)(2,1)S(1)}, bf16[448,16,128]{2,1,0:T(8,128)(2,1)}, u32[]{:S(2)}) %copy-start) | copy-done | bytes 1835032
  75.2 2.4 %shard_map.123 = bf16[2,64,512]{2,1,0:T(8,128)(2,1)} custom-call(s32[1]{0:T(128)S(6)} %copy.35.live_ref, s32[432,1]{1,0:T(8,128)S(1)} %copy.32.tap_ref, bf16[6,16,128]{2,1,0:T(8,128)(2,1)S(1)} %pad_maximum_fusion.4.own, bf16[6,16,128]{2,1,0:T(8,128)(2,1)S(1)} %collective-permute-done.8.below, bf16[6,16,128]{2,1,0:T(8,128)(2,1)S(1)} %collective-permute-done.9.above, ...), custom_call_target="tpu_custom_call" | custom-call | tf_op jit(solution)/shard_map/pallas_call | solution.py:404
  (37 shorter events, 0.5 us)
Async XLA Ops:
  6.5 67.1 %all-gather.3.cloned.1.call-start = ((), (), s32[]{:S(2)}) async-start(), calls=%async_computation | async-start | bytes 1949696 | tf_op jit(solution)/shard_map/all_gather | solution.py:318
  8.8 8.8 %copy-start.1 = (bf16[27,64,64]{2,1,0:T(8,128)(2,1)S(1)}, bf16[27,64,64]{2,1,0:T(8,128)(2,1)}, u32[]{:S(2)}) copy-start(bf16[27,64,64]{2,1,0:T(8,128)(2,1)} %weight_ref.3) | copy-start | bytes 663556
  8.8 1.0 %copy-start.3 = (bf16[2,64,512]{2,1,0:T(8,128)(2,1)S(1)}, bf16[2,64,512]{2,1,0:T(8,128)(2,1)}, u32[]{:S(2)}) copy-start(bf16[2,64,512]{2,1,0:T(8,128)(2,1)} %features_ref.1) | copy-start | bytes 393220
  10.0 8.8 %collective-permute-start = (bf16[2,2,2,2,16,128]{5,4,3,2,1,0:T(8,128)(2,1)S(1)}, bf16[2,2,2,2,16,128]{5,4,3,2,1,0:T(8,128)(2,1)S(1)}, u32[]{:S(2)}, u32[]{:S(2)}) collective-permute-start(bf16[2,2,2,2,16,128]{5,4,3,2,1,0:T(8,128)(2,1)S(1)} %get-tuple-element.10), channel_id=1, source_target_pairs={{0,8},{1,9},{2,10},{3,11},{4,12},{5,13},{6,14},{7,15},{8,0},{9,1},... | collective-permute-start | bytes 196616 | tf_op jit(solution)/shard_map/ppermute | solution.py:313
  17.0 1.3 %copy-start.2 = (bf16[27,64,64]{2,1,0:T(8,128)(2,1)S(1)}, bf16[27,64,64]{2,1,0:T(8,128)(2,1)}, u32[]{:S(2)}) copy-start(bf16[27,64,64]{2,1,0:T(8,128)(2,1)} %weight_ref.4) | copy-start | bytes 663556
  17.7 17.9 %copy-start.6 = (s32[4,128,54]{1,0,2:T(4,128)S(1)}, s32[4,128,54]{1,0,2:T(4,128)}, u32[]{:S(2)}) copy-start(s32[4,128,54]{1,0,2:T(4,128)} %constant.122.clone) | copy-start | bytes 331780
  18.9 4.7 %collective-permute-start.1 = (bf16[2,3,2,2,16,128]{5,4,3,2,1,0:T(8,128)(2,1)S(1)}, bf16[2,3,2,2,16,128]{5,4,3,2,1,0:T(8,128)(2,1)S(1)}, u32[]{:S(2)}, u32[]{:S(2)}) collective-permute-start(bf16[2,3,2,2,16,128]{5,4,3,2,1,0:T(8,128)(2,1)S(1)} %get-tuple-element.20), channel_id=1, source_target_pairs={{0,1},{1,2},{2,3},{3,4},{4,5},{5,6},{6,7},{8,9},{9,10},{10,11},{11... | collective-permute-start | bytes 294920 | tf_op jit(solution)/shard_map/ppermute | solution.py:313
  22.0 5.8 %collective-permute-start.2 = (bf16[2,3,2,2,16,128]{5,4,3,2,1,0:T(8,128)(2,1)S(1)}, bf16[2,3,2,2,16,128]{5,4,3,2,1,0:T(8,128)(2,1)S(1)}, u32[]{:S(2)}, u32[]{:S(2)}) collective-permute-start(bf16[2,3,2,2,16,128]{5,4,3,2,1,0:T(8,128)(2,1)S(1)} %get-tuple-element.19), channel_id=1, source_target_pairs={{1,0},{2,1},{3,2},{4,3},{5,4},{6,5},{7,6},{9,8},{10,9},{11,10},{12... | collective-permute-start | bytes 294920 | tf_op jit(solution)/shard_map/ppermute | solution.py:313
  27.8 9.1 %collective-permute-start.4 = (bf16[4,3,2,2,16,128]{5,4,3,2,1,0:T(8,128)(2,1)S(1)}, bf16[4,3,2,2,16,128]{5,4,3,2,1,0:T(8,128)(2,1)S(1)}, u32[]{:S(2)}, u32[]{:S(2)}) collective-permute-start(bf16[4,3,2,2,16,128]{5,4,3,2,1,0:T(8,128)(2,1)S(1)} %pad_maximum_fusion.2), channel_id=1, source_target_pairs={{16,0},{17,1},{18,2},{19,3},{20,4},{21,5},{22,6},{23,7},{24,8},{25... | collective-permute-start | bytes 589832 | tf_op jit(solution)/shard_map/ppermute | solution.py:313
  32.0 6.1 %collective-permute-start.3 = (bf16[4,3,2,2,16,128]{5,4,3,2,1,0:T(8,128)(2,1)S(1)}, bf16[4,3,2,2,16,128]{5,4,3,2,1,0:T(8,128)(2,1)S(1)}, u32[]{:S(2)}, u32[]{:S(2)}) collective-permute-start(bf16[4,3,2,2,16,128]{5,4,3,2,1,0:T(8,128)(2,1)S(1)} %pad_maximum_fusion.1), channel_id=1, source_target_pairs={{0,16},{1,17},{2,18},{3,19},{4,20},{5,21},{6,22},{7,23},{8,24},{9,... | collective-permute-start | bytes 589832 | tf_op jit(solution)/shard_map/ppermute | solution.py:313
  35.7 34.8 %copy-start.5 = (s32[432,54]{0,1:T(8,128)S(1)}, s32[432,54]{0,1:T(8,128)}, u32[]{:S(2)}) copy-start(s32[432,54]{0,1:T(8,128)} %constant.123.clone) | copy-start | bytes 279940
  35.7 34.9 %copy-start.7 = (s32[432]{0:T(512)S(1)}, s32[432]{0:T(512)}, u32[]{:S(2)}) copy-start(s32[432]{0:T(512)} %constant.130) | copy-start | bytes 5188
  35.7 38.0 %copy-start.4 = (bf16[64,128]{1,0:T(8,128)(2,1)S(1)}, bf16[64,128]{1,0:T(8,128)(2,1)}, u32[]{:S(2)}) copy-start(bf16[64,128]{1,0:T(8,128)(2,1)} %w_output.1) | copy-start | bytes 49156
  49.9 4.1 %collective-permute-start.5 = (bf16[16,128]{1,0:T(8,128)(2,1)S(1)}, bf16[16,128]{1,0:T(8,128)(2,1)S(1)}, u32[]{:S(2)}, u32[]{:S(2)}) collective-permute-start(bf16[16,128]{1,0:T(8,128)(2,1)S(1)} %get-tuple-element.11), channel_id=1, source_target_pairs={{0,8},{1,9},{2,10},{3,11},{4,12},{5,13},{6,14},{7,15},{8,0},{9,1},... | collective-permute-start | bytes 12296 | tf_op jit(solution)/shard_map/ppermute | solution.py:313
  54.0 4.5 %collective-permute-start.6 = (bf16[2,16,128]{2,1,0:T(8,128)(2,1)S(1)}, bf16[2,16,128]{2,1,0:T(8,128)(2,1)S(1)}, u32[]{:S(2)}, u32[]{:S(2)}) collective-permute-start(bf16[2,16,128]{2,1,0:T(8,128)(2,1)S(1)} %pad_maximum_fusion.5), channel_id=1, source_target_pairs={{0,1},{1,2},{2,3},{3,4},{4,5},{5,6},{6,7},{8,9},{9,10},{10,11},{11... | collective-permute-start | bytes 24584 | tf_op jit(solution)/shard_map/ppermute | solution.py:313
  57.2 4.4 %collective-permute-start.7 = (bf16[2,16,128]{2,1,0:T(8,128)(2,1)S(1)}, bf16[2,16,128]{2,1,0:T(8,128)(2,1)S(1)}, u32[]{:S(2)}, u32[]{:S(2)}) collective-permute-start(bf16[2,16,128]{2,1,0:T(8,128)(2,1)S(1)} %pad_maximum_fusion.5), channel_id=1, source_target_pairs={{1,0},{2,1},{3,2},{4,3},{5,4},{6,5},{7,6},{9,8},{10,9},{11,10},{12... | collective-permute-start | bytes 24584 | tf_op jit(solution)/shard_map/ppermute | solution.py:313
  61.6 9.8 %collective-permute-start.8 = (bf16[6,16,128]{2,1,0:T(8,128)(2,1)S(1)}, bf16[6,16,128]{2,1,0:T(8,128)(2,1)S(1)}, u32[]{:S(2)}, u32[]{:S(2)}) collective-permute-start(bf16[6,16,128]{2,1,0:T(8,128)(2,1)S(1)} %pad_maximum_fusion.4.own), channel_id=1, source_target_pairs={{0,16},{1,17},{2,18},{3,19},{4,20},{5,21},{6,22},{7,23},{8,24},{9,... | collective-permute-start | bytes 73736 | tf_op jit(solution)/shard_map/ppermute | solution.py:313
  68.5 5.1 %collective-permute-start.9 = (bf16[6,16,128]{2,1,0:T(8,128)(2,1)S(1)}, bf16[6,16,128]{2,1,0:T(8,128)(2,1)S(1)}, u32[]{:S(2)}, u32[]{:S(2)}) collective-permute-start(bf16[6,16,128]{2,1,0:T(8,128)(2,1)S(1)} %pad_maximum_fusion.4.own), channel_id=1, source_target_pairs={{16,0},{17,1},{18,2},{19,3},{20,4},{21,5},{22,6},{23,7},{24,8},{25... | collective-permute-start | bytes 73736 | tf_op jit(solution)/shard_map/ppermute | solution.py:313
  73.7 1.5 %copy-start = (bf16[448,16,128]{2,1,0:T(8,128)(2,1)S(1)}, bf16[448,16,128]{2,1,0:T(8,128)(2,1)}, u32[]{:S(2)}) copy-start(bf16[448,16,128]{2,1,0:T(8,128)(2,1)} %all-gather.3.cloned.1.call-done) | copy-start | bytes 5505028
Sparse Core Ops, SparseCore 0:
  9.5 46.5 all-gather.2
where the time goes:
time: 85.8 us; the launch traced here: 84.4 us
  starting transfers between devices  29.4 us (34%)
  Pallas kernels  16.2 us (19%)
  waiting for transfers between devices  16 us (19%)
  between operations  14.4 us (17%)
  local copies, waits for them, and re-layouts  6.38 us (7%)
  other arithmetic  2.01 us (2%)
    ppermute x10, starting transfers between devices, moved(): return lax.ppermute(value, AXES, pairs_for(step_h, step_j, step_g, sizes))  29.4 us
    ppermute x10, waiting for transfers between devices, moved(): return lax.ppermute(value, AXES, pairs_for(step_h, step_j, step_g, sizes))  16 us
    pallas_call x1, Pallas kernels, shards(): pl.pallas_call(main_kernel, out_shape=(shape((2, 64, 512)), shape((16, 12...  11.8 us
    unnamed x17, local copies, waits for them, and re-layouts  3.92 us
    pallas_call x1, Pallas kernels, shards(): pl.pallas_call(last_kernel, out_shape=shape((2, 64, 512)), in_specs=[SMEM...  2.37 us
    pallas_call x3, Pallas kernels, widened_weight(): pl.pallas_call(functools.partial(widen_kernel, outs=outs), out_shape=shap...  1.79 us
  transfers between devices with their start and end apart: 11, of which 7 were waited for; matrix products, arithmetic and copies ran while one was open for 4% of the time, Pallas kernels for 16%

commit v1 on v0

--- a/solution.py
+++ b/solution.py
@@ -51,10 +51,19 @@
     for g in range(groups):
         for m in range(members):
             h, j = m // tiles, m % tiles
-            if 0 <= j + step_j < tiles and 0 <= g + step_g < groups:
-                to = (1 - h if step_h else h) * tiles + j + step_j
-                found.append((g * members + m, (g + step_g) * members + to))
+            to = (1 - h if step_h else h) * tiles + (j + step_j) % tiles
+            found.append((g * members + m, (g + step_g) % groups * members + to))
     return found
+
+
+def swapped(value, axis_mask, group_mask, sizes):
+    groups, members = sizes
+    pairs = [
+        (g * members + m, (g ^ group_mask) * members + (m ^ axis_mask))
+        for g in range(groups)
+        for m in range(members)
+    ]
+    return lax.ppermute(value, AXES, pairs)
 
 
 def gelu(v):
@@ -69,8 +78,21 @@
     return jnp.dot(a, b, preferred_element_type=F32)
 
 
-def pack_kernel(half_ref, features_ref, atoms_ref, send_ref, turned):
-    h = half_ref[0]
+def pack_kernel(
+    place_ref, features_ref, w_coarse_ref, w_project_ref, atoms_ref, send_ref, share_ref, turned
+):
+    h, core = place_ref[0], place_ref[1]
+
+    @pl.when(core == 0)
+    def _():
+        share_ref[...] = w_coarse_ref[0:14]
+
+    @pl.when(core == 1)
+    def _():
+        share_ref[0:13] = w_coarse_ref[14:27]
+        project = w_project_ref[...].astype(F32)
+        share_ref[13] = jnp.concatenate([project, jnp.zeros_like(project)], axis=1).astype(BF)
+
     turned[...] = features_ref[...].astype(F32).reshape(128, 512).T
     low = halves(128)
     upper = lax.broadcasted_iota(jnp.int32, (1, 8, 1), 1) < 4
@@ -262,20 +284,32 @@
     skip_ref[...] = turned[...].T.astype(BF).reshape(2, 64, 512)
 
 
-def last_kernel(live_ref, tap_ref, own, below, above, weights, w_output, skip_ref, out_ref):
+def last_kernel(
+    live_ref, core_ref, tap_ref, own, below, above, mine, theirs, w_output, skip_ref, out_ref,
+    weights, sems,
+):
+    core = core_ref[0]
+    copies = [
+        pltpu.make_async_copy(mine, weights.at[core], sems.at[0]),
+        pltpu.make_async_copy(theirs, weights.at[1 - core], sems.at[1]),
+    ]
+    for copy in copies:
+        copy.start()
     tiles = jnp.concatenate([r[...].reshape(96, 128) for r in (own, below, above)], axis=0)
     chosen = (tap_ref[...] == lax.broadcasted_iota(jnp.int32, (432, 288), 1)).astype(F32).astype(BF)
     taps = dot(chosen, tiles).astype(BF)
+    for copy in copies:
+        copy.wait()
     total = jnp.zeros((16, 256), F32)
     for t in range(27):
         total = total + lax.dot_general(
             taps[t * 16 : (t + 1) * 16],
-            weights[:, t].reshape(256, 128),
+            weights[t // 14, :, t % 14].reshape(256, 128),
             (((1,), (1,)), ((), ())),
             preferred_element_type=F32,
         )
     hidden = gelu(total).astype(BF)
-    coarse = dot(hidden, weights[:, 27].reshape(256, 128)).astype(BF).astype(F32)
+    coarse = dot(hidden, weights[1, :, 13].reshape(256, 128)).astype(BF).astype(F32)
     coarse = coarse.T[:64].astype(BF)
     row = lax.broadcasted_iota(jnp.int32, (16, 512), 0)
     voxel = lax.broadcasted_iota(jnp.int32, (16, 512), 1)
@@ -312,26 +346,33 @@
     def moved(value, step_h, step_j, step_g):
         return lax.ppermute(value, AXES, pairs_for(step_h, step_j, step_g, sizes))
 
-    shard = jnp.concatenate(
-        [w_coarse, jnp.pad(w_project, ((0, 0), (0, 64)))[None]], axis=0
-    )
-    weights = lax.all_gather(shard, "ch", axis=0)
-
-    atoms, send = pl.pallas_call(
+    atoms, send, mine = pl.pallas_call(
         pack_kernel,
-        out_shape=(shape((2, 2, 2, 2) + ATOM), shape((2, 2, 2) + ATOM)),
-        in_specs=[SMEM, VMEM],
-        out_specs=(VMEM, VMEM),
+        out_shape=(shape((2, 2, 2, 2) + ATOM), shape((2, 2, 2) + ATOM), shape((14, 16, 128))),
+        in_specs=[SMEM, VMEM, VMEM, VMEM],
+        out_specs=(VMEM, VMEM, VMEM),
         scratch_shapes=[pltpu.VMEM((512, 128), F32)],
         compiler_params=PARAMS,
-    )(h[None].astype(jnp.int32), features)
+    )(jnp.stack([h, g % 2]).astype(jnp.int32), features, w_coarse, w_project)
+    def doubled(value, mask):
+        return jnp.concatenate([value, swapped(value, mask, 0, sizes)], axis=0)
+
+    mine = doubled(mine[None], 2)
     beside = moved(send, 1, 0, 0)
     own = jnp.concatenate([atoms, beside[:, :, None]], axis=2)
-    below_y = moved(own[:, 1], 0, 1, 0)
-    above_y = moved(own[:, 0], 0, -1, 0)
+    near, far, mine, w_first, w_second, w_middle = lax.optimization_barrier(
+        (own[:, 1], own[:, 0], mine, w_first, w_second, w_middle)
+    )
+    below_y = moved(near, 0, 1, 0)
+    above_y = moved(far, 0, -1, 0)
+    mine = doubled(mine, 8)
     whole = [jnp.concatenate([own[z], below_y[z][None], above_y[z][None]], axis=0) for z in (0, 1)]
+    whole[0], whole[1], mine = lax.optimization_barrier((whole[0], whole[1], mine))
     below_z = moved(whole[1], 0, 0, 1)
     above_z = moved(whole[0], 0, 0, -1)
+    mine = doubled(mine, 1)
+    below_z, above_z, mine = lax.optimization_barrier((below_z, above_z, mine))
+    mine = doubled(mine, 4)
 
     atom_table, tap_table, inner = tables()
     entry = neighbours.reshape(54)
@@ -398,16 +439,33 @@
         w3,
     )
 
+    coarse, mine = lax.optimization_barrier((coarse, mine))
+    theirs = swapped(mine, 0, 1, sizes)
     both = jnp.stack([coarse, moved(coarse, 1, 0, 0)])
     layer = jnp.concatenate([both, moved(both, 0, 1, 0), moved(both, 0, -1, 0)], axis=0)
     below, above = moved(layer, 0, 0, 1), moved(layer, 0, 0, -1)
     return pl.pallas_call(
         last_kernel,
         out_shape=shape((2, 64, 512)),
-        in_specs=[SMEM] + [VMEM] * 7,
+        in_specs=[SMEM] * 2 + [VMEM] * 4 + [ANY] * 2 + [VMEM] * 2,
         out_specs=VMEM,
+        scratch_shapes=[
+            pltpu.VMEM((2, 16, 14, 16, 128), BF),
+            pltpu.SemaphoreType.DMA((2,)),
+        ],
         compiler_params=PARAMS,
-    )(live_counts, tap_rows, layer, below, above, weights, w_output, skip)
+    )(
+        live_counts,
+        (g % 2)[None].astype(jnp.int32),
+        tap_rows,
+        layer,
+        below,
+        above,
+        mine,
+        theirs,
+        w_output,
+        skip,
+    )
 
 
 def solution(mesh):

time: 85.8 us -> 64.2 us (0.75); the launches traced: 84.4 us -> 64 us
  between operations: 14.4 us -> 0.93 us
  waiting for transfers between devices: 16 us -> 11.9 us
  other arithmetic: 2.01 us -> 0.67 us
  starting transfers between devices: 29.4 us -> 28.1 us
  local copies, waits for them, and re-layouts: 6.38 us -> 5.09 us
  Pallas kernels: 16.2 us -> 17.3 us
    ppermute x10, starting transfers between devices: 29.4 us -> 23.4 us  [moved(): return lax.ppermute(value, AXES, pairs_for(step_h, step_j, step_g, sizes))]
    ppermute x0 -> x5, starting transfers between devices: none -> 4.65 us  [swapped(): return lax.ppermute(value, AXES, pairs)]
    ppermute x10, waiting for transfers between devices: 16 us -> 11.7 us  [moved(): return lax.ppermute(value, AXES, pairs_for(step_h, step_j, step_g, sizes))]
    concatenate x1 -> x4, other arithmetic: 1.55 us -> 0.16 us  [doubled(): return jnp.concatenate([value, swapped(value, mask, 0, sizes)], axis=0)]
    unnamed x17 -> x20, local copies, waits for them, and re-layouts: 3.92 us -> 2.88 us
  transfers between devices with their start and end apart: 11 -> 15, of which waited for: 7 -> 7; matrix products, arithmetic and copies ran while one was open for 4% -> 4% of each run, Pallas kernels for 16% -> 21%
where the time goes in v1:
time: 64.2 us; the launch traced here: 64 us
  starting transfers between devices  28.1 us (44%)
  Pallas kernels  17.3 us (27%)
  waiting for transfers between devices  11.9 us (19%)
  local copies, waits for them, and re-layouts  5.09 us (8%)
  between operations  0.93 us (1%)
  other arithmetic  0.67 us (1%)
    ppermute x10, starting transfers between devices, moved(): return lax.ppermute(value, AXES, pairs_for(step_h, step_j, step_g, sizes))  23.4 us
    pallas_call x1, Pallas kernels, shards(): pl.pallas_call(main_kernel, out_shape=(shape((2, 64, 512)), shape((16, 12...  11.8 us
    ppermute x10, waiting for transfers between devices, moved(): return lax.ppermute(value, AXES, pairs_for(step_h, step_j, step_g, sizes))  11.7 us
    ppermute x5, starting transfers between devices, swapped(): return lax.ppermute(value, AXES, pairs)  4.65 us
    pallas_call x1, Pallas kernels, shards(): pl.pallas_call(last_kernel, out_shape=shape((2, 64, 512)), in_specs=[SMEM...  2.94 us
    unnamed x20, local copies, waits for them, and re-layouts  2.88 us
    pallas_call x3, Pallas kernels, widened_weight(): pl.pallas_call(functools.partial(widen_kernel, outs=outs), out_shape=shap...  1.79 us
    reshape x2, local copies, waits for them, and re-layouts, shards(): entry = neighbours.reshape(54)  1.52 us
  transfers between devices with their start and end apart: 15, of which 7 were waited for; matrix products, arithmetic and copies ran while one was open for 4% of the time, Pallas kernels for 21%

profile of v1, /device:TPU:1, one launch (start us, length us, event | category | flops | bytes accessed | tf_op | source)
XLA Modules:
  0.0 64.0 jit_solution(8755861623349622947)
XLA Ops:
  0.1 0.9 %copy-done.2 = bf16[2,64,512]{2,1,0:T(8,128)(2,1)S(1)} copy-done((bf16[2,64,512]{2,1,0:T(8,128)(2,1)S(1)}, bf16[2,64,512]{2,1,0:T(8,128)(2,1)}, u32[]{:S(2)}) %copy-start.2) | copy-done | bytes 131096
  1.0 0.9 %copy-done.3 = bf16[27,16,128]{2,1,0:T(8,128)(2,1)S(1)} copy-done((bf16[27,16,128]{2,1,0:T(8,128)(2,1)S(1)}, bf16[27,16,128]{2,1,0:T(8,128)(2,1)}, u32[]{:S(2)}) %copy-start.3) | copy-done | bytes 110616
  1.9 0.7 %copy-done.5 = bf16[16,64]{1,0:T(8,128)(2,1)S(1)} copy-done((bf16[16,64]{1,0:T(8,128)(2,1)S(1)}, bf16[16,64]{1,0:T(8,128)(2,1)}, u32[]{:S(2)}) %copy-start.5) | copy-done | bytes 2072
  2.6 0.8 %shard_map.118 = (bf16[2,2,2,2,2,16,128]{6,5,4,3,2,1,0:T(8,128)(2,1)S(1)}, bf16[2,2,2,2,16,128]{5,4,3,2,1,0:T(8,128)(2,1)S(1)}, bf16[14,16,128]{2,1,0:T(8,128)(2,1)S(1)}) custom-call(s32[2]{0:T(128)S(1)} %pad_add_fusion.1.place_ref, bf16[2,64,512]{2,1,0:T(8,128)(2,1)S(1)} %copy-done.2, bf16[27,16,128]{2,1,0:T(8,128)(2,1)S(1)} %copy-done.3, ...), custom_call_target="tpu_custom_call" | custom-call | tf_op jit(solution)/shard_map/pallas_call | solution.py:349
  3.4 3.8 %collective-permute-start = (bf16[2,2,2,2,16,128]{5,4,3,2,1,0:T(8,128)(2,1)S(1)}, bf16[2,2,2,2,16,128]{5,4,3,2,1,0:T(8,128)(2,1)S(1)}, u32[]{:S(2)}, u32[]{:S(2)}) collective-permute-start(bf16[2,2,2,2,16,128]{5,4,3,2,1,0:T(8,128)(2,1)S(1)} %get-tuple-element.25), channel_id=1, source_target_pairs={{0,8},{1,9},{2,10},{3,11},{4,12},{5,13},{6,14},{7,15},{8,0},{9,1},... | collective-permute-start | bytes 196616 | tf_op jit(solution)/shard_map/ppermute | solution.py:347
  7.2 2.7 %collective-permute-start.1 = (bf16[1,14,16,128]{3,2,1,0:T(8,128)(2,1)S(1)}, bf16[1,14,16,128]{3,2,1,0:T(8,128)(2,1)S(1)}, u32[]{:S(2)}, u32[]{:S(2)}) collective-permute-start(bf16[1,14,16,128]{3,2,1,0:T(8,128)(2,1)S(1)} %bitcast.31), channel_id=1, source_target_pairs={{0,2},{1,3},{2,0},{3,1},{4,6},{5,7},{6,4},{7,5},{8,10},{9,11},{10,... | collective-permute-start | bytes 172040 | tf_op jit(solution)/shard_map/ppermute | solution.py:66
  9.9 0.8 %reshape.413 = s32[1,54]{1,0:T(1,128)S(1)} reshape(s32[2,27]{1,0:T(2,128)} %param.14) | data formatting | bytes 432 | tf_op jit(solution)/shard_map/reshape | solution.py:378
  10.7 0.8 %reshape.412 = s32[54]{0:T(128)S(1)} reshape(s32[2,27]{1,0:T(2,128)} %param.14) | data formatting | bytes 432 | tf_op jit(solution)/shard_map/reshape | solution.py:378
  11.5 0.2 collective-permute-done.1
  11.8 0.2 collective-permute-start.4
  11.9 1.2 %collective-permute-start.2 = (bf16[2,3,2,2,16,128]{5,4,3,2,1,0:T(8,128)(2,1)S(1)}, bf16[2,3,2,2,16,128]{5,4,3,2,1,0:T(8,128)(2,1)S(1)}, u32[]{:S(2)}, u32[]{:S(2)}) collective-permute-start(bf16[2,3,2,2,16,128]{5,4,3,2,1,0:T(8,128)(2,1)S(1)} %get-tuple-element.27), channel_id=1, source_target_pairs={{0,1},{1,2},{2,3},{3,4},{4,5},{5,6},{6,7},{7,0},{8,9},{9,10},{10,1... | collective-permute-start | bytes 294920 | tf_op jit(solution)/shard_map/ppermute | solution.py:347
  13.2 2.5 %collective-permute-start.3 = (bf16[2,3,2,2,16,128]{5,4,3,2,1,0:T(8,128)(2,1)S(1)}, bf16[2,3,2,2,16,128]{5,4,3,2,1,0:T(8,128)(2,1)S(1)}, u32[]{:S(2)}, u32[]{:S(2)}) collective-permute-start(bf16[2,3,2,2,16,128]{5,4,3,2,1,0:T(8,128)(2,1)S(1)} %get-tuple-element.28), channel_id=1, source_target_pairs={{0,7},{1,0},{2,1},{3,2},{4,3},{5,4},{6,5},{7,6},{8,15},{9,8},{10,9... | collective-permute-start | bytes 294920 | tf_op jit(solution)/shard_map/ppermute | solution.py:347
  15.7 2.1 %collective-permute-done.2 = bf16[2,3,2,2,16,128]{5,4,3,2,1,0:T(8,128)(2,1)S(1)} collective-permute-done((bf16[2,3,2,2,16,128]{5,4,3,2,1,0:T(8,128)(2,1)S(1)}, bf16[2,3,2,2,16,128]{5,4,3,2,1,0:T(8,128)(2,1)S(1)}, u32[]{:S(2)}, u32[]{:S(2)}) %collective-permute-start.2) | collective-permute-done | bytes 98336 | tf_op jit(solution)/shard_map/ppermute | solution.py:347
  18.0 0.4 collective-permute-start.7
  18.3 5.3 %collective-permute-start.5 = (bf16[4,3,2,2,16,128]{5,4,3,2,1,0:T(8,128)(2,1)S(1)}, bf16[4,3,2,2,16,128]{5,4,3,2,1,0:T(8,128)(2,1)S(1)}, u32[]{:S(2)}, u32[]{:S(2)}) collective-permute-start(bf16[4,3,2,2,16,128]{5,4,3,2,1,0:T(8,128)(2,1)S(1)} %get-tuple-element.30), channel_id=1, source_target_pairs={{0,16},{1,17},{2,18},{3,19},{4,20},{5,21},{6,22},{7,23},{8,24},{9,... | collective-permute-start | bytes 589832 | tf_op jit(solution)/shard_map/ppermute | solution.py:347
  23.8 2.4 %collective-permute-done.5 = bf16[4,3,2,2,16,128]{5,4,3,2,1,0:T(8,128)(2,1)S(1)} collective-permute-done((bf16[4,3,2,2,16,128]{5,4,3,2,1,0:T(8,128)(2,1)S(1)}, bf16[4,3,2,2,16,128]{5,4,3,2,1,0:T(8,128)(2,1)S(1)}, u32[]{:S(2)}, u32[]{:S(2)}) %collective-permute-start.5) | collective-permute-done | bytes 196640 | tf_op jit(solution)/shard_map/ppermute | solution.py:347
  26.2 2.5 %collective-permute-done.6 = bf16[4,3,2,2,16,128]{5,4,3,2,1,0:T(8,128)(2,1)S(1)} collective-permute-done((bf16[4,3,2,2,16,128]{5,4,3,2,1,0:T(8,128)(2,1)S(1)}, bf16[4,3,2,2,16,128]{5,4,3,2,1,0:T(8,128)(2,1)S(1)}, u32[]{:S(2)}, u32[]{:S(2)}) %collective-permute-start.6) | collective-permute-done | bytes 196640 | tf_op jit(solution)/shard_map/ppermute | solution.py:347
  28.7 1.3 %collective-permute-start.8 = (bf16[8,14,16,128]{3,2,1,0:T(8,128)(2,1)S(1)}, bf16[8,14,16,128]{3,2,1,0:T(8,128)(2,1)S(1)}, u32[]{:S(2)}, u32[]{:S(2)}) collective-permute-start(bf16[8,14,16,128]{3,2,1,0:T(8,128)(2,1)S(1)} %pad_maximum_fusion.1), channel_id=1, source_target_pairs={{0,4},{1,5},{2,6},{3,7},{4,0},{5,1},{6,2},{7,3},{8,12},{9,13},{10,... | collective-permute-start | bytes 1376264 | tf_op jit(solution)/shard_map/ppermute | solution.py:66
  30.2 0.4 copy.26.weight_ref
  30.6 0.6 %shard_map.121.w3 = bf16[768,768]{1,0:T(8,128)(2,1)S(1)} custom-call(bf16[27,128,64]{2,1,0:T(8,128)(2,1)S(1)} %copy.26.weight_ref), custom_call_target="tpu_custom_call" | custom-call | tf_op jit(solution)/shard_map/pallas_call | solution.py:330
  31.3 0.3 copy-done
  31.6 0.6 shard_map.119.w1
  32.2 0.6 shard_map.120.w2
  32.8 11.8 %shard_map.122 = (bf16[2,64,512]{2,1,0:T(8,128)(2,1)S(1)}, bf16[16,128]{1,0:T(8,128)(2,1)S(1)}) custom-call(s32[128]{0:T(128)S(1)} %multiply_reduce_fusion.1.atom_ref, s32[54]{0:T(128)S(1)} %compare_convert_fusion.present_ref, bf16[2,2,6,2,16,128]{5,4,3,2,1,0:T(8,128)(2,1)S(1)} %bitcast.26, bf16[2,6,2,16,128]{4,3,2,1,0:T(8,128)(2,1)S(1)} %bitcast.27, ...), custom_call_target="tpu_custom_call" | custom-call | tf_op jit(solution)/shard_map/pallas_call | solution.py:411
  44.9 2.7 %collective-permute-start.9 = (bf16[16,128]{1,0:T(8,128)(2,1)S(1)}, bf16[16,128]{1,0:T(8,128)(2,1)S(1)}, u32[]{:S(2)}, u32[]{:S(2)}) collective-permute-start(bf16[16,128]{1,0:T(8,128)(2,1)S(1)} %get-tuple-element.40), channel_id=1, source_target_pairs={{0,8},{1,9},{2,10},{3,11},{4,12},{5,13},{6,14},{7,15},{8,0},{9,1},... | collective-permute-start | bytes 12296 | tf_op jit(solution)/shard_map/ppermute | solution.py:347
  47.6 1.3 %collective-permute-done.9 = bf16[16,128]{1,0:T(8,128)(2,1)S(1)} collective-permute-done((bf16[16,128]{1,0:T(8,128)(2,1)S(1)}, bf16[16,128]{1,0:T(8,128)(2,1)S(1)}, u32[]{:S(2)}, u32[]{:S(2)}) %collective-permute-start.9) | collective-permute-done | bytes 4128 | tf_op jit(solution)/shard_map/ppermute | solution.py:347
  48.9 0.9 %collective-permute-start.10 = (bf16[2,16,128]{2,1,0:T(8,128)(2,1)S(1)}, bf16[2,16,128]{2,1,0:T(8,128)(2,1)S(1)}, u32[]{:S(2)}, u32[]{:S(2)}) collective-permute-start(bf16[2,16,128]{2,1,0:T(8,128)(2,1)S(1)} %pad_maximum_fusion.8), channel_id=1, source_target_pairs={{0,1},{1,2},{2,3},{3,4},{4,5},{5,6},{6,7},{7,0},{8,9},{9,10},{10,1... | collective-permute-start | bytes 24584 | tf_op jit(solution)/shard_map/ppermute | solution.py:347
  49.8 2.7 %collective-permute-start.11 = (bf16[2,16,128]{2,1,0:T(8,128)(2,1)S(1)}, bf16[2,16,128]{2,1,0:T(8,128)(2,1)S(1)}, u32[]{:S(2)}, u32[]{:S(2)}) collective-permute-start(bf16[2,16,128]{2,1,0:T(8,128)(2,1)S(1)} %pad_maximum_fusion.8), channel_id=1, source_target_pairs={{0,7},{1,0},{2,1},{3,2},{4,3},{5,4},{6,5},{7,6},{8,15},{9,8},{10,9... | collective-permute-start | bytes 24584 | tf_op jit(solution)/shard_map/ppermute | solution.py:347
  52.5 1.0 %collective-permute-done.10 = bf16[2,16,128]{2,1,0:T(8,128)(2,1)S(1)} collective-permute-done((bf16[2,16,128]{2,1,0:T(8,128)(2,1)S(1)}, bf16[2,16,128]{2,1,0:T(8,128)(2,1)S(1)}, u32[]{:S(2)}, u32[]{:S(2)}) %collective-permute-start.10) | collective-permute-done | bytes 8224 | tf_op jit(solution)/shard_map/ppermute | solution.py:347
  53.5 4.3 %collective-permute-start.12 = (bf16[6,16,128]{2,1,0:T(8,128)(2,1)S(1)}, bf16[6,16,128]{2,1,0:T(8,128)(2,1)S(1)}, u32[]{:S(2)}, u32[]{:S(2)}) collective-permute-start(bf16[6,16,128]{2,1,0:T(8,128)(2,1)S(1)} %pad_maximum_fusion.7.own), channel_id=1, source_target_pairs={{0,16},{1,17},{2,18},{3,19},{4,20},{5,21},{6,22},{7,23},{8,24},{9,... | collective-permute-start | bytes 73736 | tf_op jit(solution)/shard_map/ppermute | solution.py:347
  58.7 2.3 %collective-permute-done.13.above = bf16[6,16,128]{2,1,0:T(8,128)(2,1)S(1)} collective-permute-done((bf16[6,16,128]{2,1,0:T(8,128)(2,1)S(1)}, bf16[6,16,128]{2,1,0:T(8,128)(2,1)S(1)}, u32[]{:S(2)}, u32[]{:S(2)}) %collective-permute-start.13) | collective-permute-done | bytes 24608 | tf_op jit(solution)/shard_map/ppermute | solution.py:347
  61.0 2.9 %shard_map.123 = bf16[2,64,512]{2,1,0:T(8,128)(2,1)} custom-call(s32[1]{0:T(128)S(6)} %copy.30.live_ref, s32[1]{0:T(128)} %bitcast.core_ref, s32[432,1]{1,0:T(8,128)S(1)} %copy.27.tap_ref, bf16[6,16,128]{2,1,0:T(8,128)(2,1)S(1)} %pad_maximum_fusion.7.own, bf16[6,16,128]{2,1,0:T(8,128)(2,1)S(1)} %collective-permute-done.12.below, ...), custom_call_target="tpu_custom_call" | custom-call | tf_op jit(solution)/shard_map/pallas_call | solution.py:447
  (50 shorter events, 1.1 us)
Async XLA Ops:
  0.1 0.9 %copy-start.2 = (bf16[2,64,512]{2,1,0:T(8,128)(2,1)S(1)}, bf16[2,64,512]{2,1,0:T(8,128)(2,1)}, u32[]{:S(2)}) copy-start(bf16[2,64,512]{2,1,0:T(8,128)(2,1)} %features_ref.1) | copy-start | bytes 393220
  1.0 0.9 %copy-start.3 = (bf16[27,16,128]{2,1,0:T(8,128)(2,1)S(1)}, bf16[27,16,128]{2,1,0:T(8,128)(2,1)}, u32[]{:S(2)}) copy-start(bf16[27,16,128]{2,1,0:T(8,128)(2,1)} %w_coarse_ref.1) | copy-start | bytes 331780
  1.9 0.7 %copy-start.5 = (bf16[16,64]{1,0:T(8,128)(2,1)S(1)}, bf16[16,64]{1,0:T(8,128)(2,1)}, u32[]{:S(2)}) copy-start(bf16[16,64]{1,0:T(8,128)(2,1)} %w_project_ref.1) | copy-start | bytes 6148
  3.4 8.4 %collective-permute-start = (bf16[2,2,2,2,16,128]{5,4,3,2,1,0:T(8,128)(2,1)S(1)}, bf16[2,2,2,2,16,128]{5,4,3,2,1,0:T(8,128)(2,1)S(1)}, u32[]{:S(2)}, u32[]{:S(2)}) collective-permute-start(bf16[2,2,2,2,16,128]{5,4,3,2,1,0:T(8,128)(2,1)S(1)} %get-tuple-element.25), channel_id=1, source_target_pairs={{0,8},{1,9},{2,10},{3,11},{4,12},{5,13},{6,14},{7,15},{8,0},{9,1},... | collective-permute-start | bytes 196616 | tf_op jit(solution)/shard_map/ppermute | solution.py:347
  7.2 4.5 %collective-permute-start.1 = (bf16[1,14,16,128]{3,2,1,0:T(8,128)(2,1)S(1)}, bf16[1,14,16,128]{3,2,1,0:T(8,128)(2,1)S(1)}, u32[]{:S(2)}, u32[]{:S(2)}) collective-permute-start(bf16[1,14,16,128]{3,2,1,0:T(8,128)(2,1)S(1)} %bitcast.31), channel_id=1, source_target_pairs={{0,2},{1,3},{2,0},{3,1},{4,6},{5,7},{6,4},{7,5},{8,10},{9,11},{10,... | collective-permute-start | bytes 172040 | tf_op jit(solution)/shard_map/ppermute | solution.py:66
  11.8 6.1 %collective-permute-start.4 = (bf16[2,14,16,128]{3,2,1,0:T(8,128)(2,1)S(1)}, bf16[2,14,16,128]{3,2,1,0:T(8,128)(2,1)S(1)}, u32[]{:S(2)}, u32[]{:S(2)}) collective-permute-start(bf16[2,14,16,128]{3,2,1,0:T(8,128)(2,1)S(1)} %pad_maximum_fusion.6), channel_id=1, source_target_pairs={{0,8},{1,9},{2,10},{3,11},{4,12},{5,13},{6,14},{7,15},{8,0},{9,1},... | collective-permute-start | bytes 344072 | tf_op jit(solution)/shard_map/ppermute | solution.py:66
  11.9 5.9 %collective-permute-start.2 = (bf16[2,3,2,2,16,128]{5,4,3,2,1,0:T(8,128)(2,1)S(1)}, bf16[2,3,2,2,16,128]{5,4,3,2,1,0:T(8,128)(2,1)S(1)}, u32[]{:S(2)}, u32[]{:S(2)}) collective-permute-start(bf16[2,3,2,2,16,128]{5,4,3,2,1,0:T(8,128)(2,1)S(1)} %get-tuple-element.27), channel_id=1, source_target_pairs={{0,1},{1,2},{2,3},{3,4},{4,5},{5,6},{6,7},{7,0},{8,9},{9,10},{10,1... | collective-permute-start | bytes 294920 | tf_op jit(solution)/shard_map/ppermute | solution.py:347
  13.2 4.7 %collective-permute-start.3 = (bf16[2,3,2,2,16,128]{5,4,3,2,1,0:T(8,128)(2,1)S(1)}, bf16[2,3,2,2,16,128]{5,4,3,2,1,0:T(8,128)(2,1)S(1)}, u32[]{:S(2)}, u32[]{:S(2)}) collective-permute-start(bf16[2,3,2,2,16,128]{5,4,3,2,1,0:T(8,128)(2,1)S(1)} %get-tuple-element.28), channel_id=1, source_target_pairs={{0,7},{1,0},{2,1},{3,2},{4,3},{5,4},{6,5},{7,6},{8,15},{9,8},{10,9... | collective-permute-start | bytes 294920 | tf_op jit(solution)/shard_map/ppermute | solution.py:347
  17.8 12.2 %copy-start.8 = (s32[4,128,54]{1,0,2:T(4,128)S(1)}, s32[4,128,54]{1,0,2:T(4,128)}, u32[]{:S(2)}) copy-start(s32[4,128,54]{1,0,2:T(4,128)} %constant.126.clone) | copy-start | bytes 331780
  17.8 12.3 %copy-start.6 = (bf16[27,128,64]{1,2,0:T(8,128)(2,1)S(1)}, bf16[27,128,64]{1,2,0:T(8,128)(2,1)}, u32[]{:S(2)}) copy-start(bf16[27,128,64]{1,2,0:T(8,128)(2,1)} %param.17) | copy-start | bytes 1327108
  18.0 5.8 %collective-permute-start.7 = (bf16[4,14,16,128]{3,2,1,0:T(8,128)(2,1)S(1)}, bf16[4,14,16,128]{3,2,1,0:T(8,128)(2,1)S(1)}, u32[]{:S(2)}, u32[]{:S(2)}) collective-permute-start(bf16[4,14,16,128]{3,2,1,0:T(8,128)(2,1)S(1)} %pad_maximum_fusion.3), channel_id=1, source_target_pairs={{0,1},{1,0},{2,3},{3,2},{4,5},{5,4},{6,7},{7,6},{8,9},{9,8},{10,11... | collective-permute-start | bytes 688136 | tf_op jit(solution)/shard_map/ppermute | solution.py:66
  18.3 7.9 %collective-permute-start.5 = (bf16[4,3,2,2,16,128]{5,4,3,2,1,0:T(8,128)(2,1)S(1)}, bf16[4,3,2,2,16,128]{5,4,3,2,1,0:T(8,128)(2,1)S(1)}, u32[]{:S(2)}, u32[]{:S(2)}) collective-permute-start(bf16[4,3,2,2,16,128]{5,4,3,2,1,0:T(8,128)(2,1)S(1)} %get-tuple-element.30), channel_id=1, source_target_pairs={{0,16},{1,17},{2,18},{3,19},{4,20},{5,21},{6,22},{7,23},{8,24},{9,... | collective-permute-start | bytes 589832 | tf_op jit(solution)/shard_map/ppermute | solution.py:347
  23.6 5.1 %collective-permute-start.6 = (bf16[4,3,2,2,16,128]{5,4,3,2,1,0:T(8,128)(2,1)S(1)}, bf16[4,3,2,2,16,128]{5,4,3,2,1,0:T(8,128)(2,1)S(1)}, u32[]{:S(2)}, u32[]{:S(2)}) collective-permute-start(bf16[4,3,2,2,16,128]{5,4,3,2,1,0:T(8,128)(2,1)S(1)} %get-tuple-element.31), channel_id=1, source_target_pairs={{0,112},{1,113},{2,114},{3,115},{4,116},{5,117},{6,118},{7,119},{8... | collective-permute-start | bytes 589832 | tf_op jit(solution)/shard_map/ppermute | solution.py:347
  28.7 15.9 %collective-permute-start.8 = (bf16[8,14,16,128]{3,2,1,0:T(8,128)(2,1)S(1)}, bf16[8,14,16,128]{3,2,1,0:T(8,128)(2,1)S(1)}, u32[]{:S(2)}, u32[]{:S(2)}) collective-permute-start(bf16[8,14,16,128]{3,2,1,0:T(8,128)(2,1)S(1)} %pad_maximum_fusion.1), channel_id=1, source_target_pairs={{0,4},{1,5},{2,6},{3,7},{4,0},{5,1},{6,2},{7,3},{8,12},{9,13},{10,... | collective-permute-start | bytes 1376264 | tf_op jit(solution)/shard_map/ppermute | solution.py:66
  30.6 1.0 %copy-start = (bf16[27,64,64]{2,1,0:T(8,128)(2,1)S(1)}, bf16[27,64,64]{2,1,0:T(8,128)(2,1)}, u32[]{:S(2)}) copy-start(bf16[27,64,64]{2,1,0:T(8,128)(2,1)} %weight_ref) | copy-start | bytes 663556
  30.6 1.6 %copy-start.1 = (bf16[27,64,64]{2,1,0:T(8,128)(2,1)S(1)}, bf16[27,64,64]{2,1,0:T(8,128)(2,1)}, u32[]{:S(2)}) copy-start(bf16[27,64,64]{2,1,0:T(8,128)(2,1)} %weight_ref.1) | copy-start | bytes 663556
  44.6 13.2 %copy-start.7 = (s32[432,54]{0,1:T(8,128)S(1)}, s32[432,54]{0,1:T(8,128)}, u32[]{:S(2)}) copy-start(s32[432,54]{0,1:T(8,128)} %constant.127.clone) | copy-start | bytes 279940
  44.6 13.2 %copy-start.9 = (s32[432]{0:T(512)S(1)}, s32[432]{0:T(512)}, u32[]{:S(2)}) copy-start(s32[432]{0:T(512)} %constant.132) | copy-start | bytes 5188
  44.7 16.4 %copy-start.4 = (bf16[64,128]{1,0:T(8,128)(2,1)S(1)}, bf16[64,128]{1,0:T(8,128)(2,1)}, u32[]{:S(2)}) copy-start(bf16[64,128]{1,0:T(8,128)(2,1)} %w_output.1) | copy-start | bytes 49156
  44.8 16.3 %collective-permute-start.14 = (bf16[16,14,16,128]{3,2,1,0:T(8,128)(2,1)S(1)}, bf16[16,14,16,128]{3,2,1,0:T(8,128)(2,1)S(1)}, u32[]{:S(2)}, u32[]{:S(2)}) collective-permute-start(bf16[16,14,16,128]{3,2,1,0:T(8,128)(2,1)S(1)} %pad_maximum_fusion.mine), channel_id=1, source_target_pairs={{0,16},{1,17},{2,18},{3,19},{4,20},{5,21},{6,22},{7,23},{8,24},{9,... | collective-permute-start | bytes 2752520 | tf_op jit(solution)/shard_map/ppermute | solution.py:66
  44.9 4.0 %collective-permute-start.9 = (bf16[16,128]{1,0:T(8,128)(2,1)S(1)}, bf16[16,128]{1,0:T(8,128)(2,1)S(1)}, u32[]{:S(2)}, u32[]{:S(2)}) collective-permute-start(bf16[16,128]{1,0:T(8,128)(2,1)S(1)} %get-tuple-element.40), channel_id=1, source_target_pairs={{0,8},{1,9},{2,10},{3,11},{4,12},{5,13},{6,14},{7,15},{8,0},{9,1},... | collective-permute-start | bytes 12296 | tf_op jit(solution)/shard_map/ppermute | solution.py:347
  48.9 4.6 %collective-permute-start.10 = (bf16[2,16,128]{2,1,0:T(8,128)(2,1)S(1)}, bf16[2,16,128]{2,1,0:T(8,128)(2,1)S(1)}, u32[]{:S(2)}, u32[]{:S(2)}) collective-permute-start(bf16[2,16,128]{2,1,0:T(8,128)(2,1)S(1)} %pad_maximum_fusion.8), channel_id=1, source_target_pairs={{0,1},{1,2},{2,3},{3,4},{4,5},{5,6},{6,7},{7,0},{8,9},{9,10},{10,1... | collective-permute-start | bytes 24584 | tf_op jit(solution)/shard_map/ppermute | solution.py:347
  49.8 3.7 %collective-permute-start.11 = (bf16[2,16,128]{2,1,0:T(8,128)(2,1)S(1)}, bf16[2,16,128]{2,1,0:T(8,128)(2,1)S(1)}, u32[]{:S(2)}, u32[]{:S(2)}) collective-permute-start(bf16[2,16,128]{2,1,0:T(8,128)(2,1)S(1)} %pad_maximum_fusion.8), channel_id=1, source_target_pairs={{0,7},{1,0},{2,1},{3,2},{4,3},{5,4},{6,5},{7,6},{8,15},{9,8},{10,9... | collective-permute-start | bytes 24584 | tf_op jit(solution)/shard_map/ppermute | solution.py:347
  53.5 5.2 %collective-permute-start.12 = (bf16[6,16,128]{2,1,0:T(8,128)(2,1)S(1)}, bf16[6,16,128]{2,1,0:T(8,128)(2,1)S(1)}, u32[]{:S(2)}, u32[]{:S(2)}) collective-permute-start(bf16[6,16,128]{2,1,0:T(8,128)(2,1)S(1)} %pad_maximum_fusion.7.own), channel_id=1, source_target_pairs={{0,16},{1,17},{2,18},{3,19},{4,20},{5,21},{6,22},{7,23},{8,24},{9,... | collective-permute-start | bytes 73736 | tf_op jit(solution)/shard_map/ppermute | solution.py:347
  57.8 3.3 %collective-permute-start.13 = (bf16[6,16,128]{2,1,0:T(8,128)(2,1)S(1)}, bf16[6,16,128]{2,1,0:T(8,128)(2,1)S(1)}, u32[]{:S(2)}, u32[]{:S(2)}) collective-permute-start(bf16[6,16,128]{2,1,0:T(8,128)(2,1)S(1)} %pad_maximum_fusion.7.own), channel_id=1, source_target_pairs={{0,112},{1,113},{2,114},{3,115},{4,116},{5,117},{6,118},{7,119},{8... | collective-permute-start | bytes 73736 | tf_op jit(solution)/shard_map/ppermute | solution.py:347

commit v2 on v0

v2 whole, which is shorter than its diff:
```python
import functools

import jax
import jax.numpy as jnp
import numpy as np
from jax import lax
from jax.experimental import pallas as pl
from jax.experimental.pallas import tpu as pltpu
from jax.sharding import PartitionSpec as P

AXES = ("grp", "ch")
BF = jnp.bfloat16
F32 = jnp.float32
VMEM = pl.BlockSpec(memory_space=pltpu.VMEM)
SMEM = pl.BlockSpec(memory_space=pltpu.SMEM)
ANY = pl.BlockSpec(memory_space=pl.ANY)
HBM = pl.BlockSpec(memory_space=pltpu.HBM)


def params(mebibytes):
    return pltpu.CompilerParams(vmem_limit_bytes=mebibytes * 2**20)

ATOM = (2, 16, 128)
ABSENT = 96


OFFSETS = [(x, y, z) for x in (-1, 0, 1) for y in (-1, 0, 1) for z in (-1, 0, 1)]
STEP = (-1, 0, 0, 1)
HALF = (1, 0, 1, 0)


def tap_table():
    chosen = np.zeros((2, 432, 27), np.float32)
    voxel = np.zeros((432, 1), np.float32)
    for t in range(27):
        for r in range(16):
            y, b, z, x = r // 8, r // 4 % 2, r // 2 % 2, r % 2
            x, y, z = x + t // 9, y + t // 3 % 3, z + t % 3
            chosen[b, t * 16 + r, 9 * STEP[x] + 3 * STEP[y] + STEP[z] + 13] = 1
            voxel[t * 16 + r] = HALF[y] * 8 + HALF[z] * 2 + HALF[x]
    return chosen, voxel


def position():
    m = lax.axis_index("ch")
    g = lax.axis_index("grp")
    return g, m >> 3, m & 7, g & 1


def pairs_for(step_h, step_j, step_g, sizes):
    groups, members = sizes
    tiles = members // 2
    found = []
    for g in range(groups):
        for m in range(members):
            h, j = m // tiles, m % tiles
            to = (1 - h if step_h else h) * tiles + (j + step_j) % tiles
            found.append((g * members + m, (g + step_g) % groups * members + to))
    return found


def exchanged(value, axis_masks, group_mask, sizes):
    groups, members = sizes
    pairs = [
        (g * members + m, (g ^ group_mask) * members + (m ^ axis_masks[g % 2]))
        for g in range(groups)
        for m in range(members)
    ]
    return lax.ppermute(value, AXES, pairs)


def after(value, *others):
    return lax.optimization_barrier((value, *others))[0]


def gelu(v):
    return jax.nn.gelu(v, approximate=True)


def halves(axis_size_lanes):
    return lax.broadcasted_iota(jnp.int32, (1, axis_size_lanes), 1) < 64


def dot(a, b):
    return jnp.dot(a, b, preferred_element_type=F32)


def pack_kernel(features_ref, atoms_ref, packet_ref, turned):
    h = position()[1]
    low = halves(128)
    upper = lax.broadcasted_iota(jnp.int32, (1, 8, 1), 1) < 4
    turned[...] = features_ref[...].astype(F32).reshape(128, 512).T
    for pair in range(4):
        even = turned[pl.ds(2 * pair, 64, stride=8), :]
        odd = turned[pl.ds(2 * pair + 1, 64, stride=8), :]
        first = jnp.where(low, even, pltpu.roll(odd, 64, 1))
        second = jnp.where(low, pltpu.roll(even, 64, 1), odd)
        for b, rows in enumerate((first, second)):
            rows = rows.reshape(4, 2, 8, 128)
            a, c = rows[:, 0], rows[:, 1]
            near = jnp.where(upper, a, pltpu.roll(c, 4, 1))
            far = jnp.where(upper, pltpu.roll(a, 4, 1), c)
            for yh, part in enumerate((near, far)):
                part = part.reshape(2, 16, 128).astype(BF)
                for xh in range(2):
                    atoms_ref[pair // 2, yh, xh, b, pair % 2] = part[xh]
                tile = ((pair // 2 * 2 + yh) * 2 + b) * 2 + pair % 2
                packet_ref[tile] = jnp.where(h == 0, part[1], part[0])


def share_kernel(w_coarse_ref, w_project_ref, packet_in, packet_ref):
    core = position()[3]
    packet_ref[0:16] = packet_in[0:16]

    @pl.when(core == 0)
    def _():
        packet_ref[16:30] = w_coarse_ref[0:14]

    @pl.when(core == 1)
    def _():
        packet_ref[16:29] = w_coarse_ref[14:27]
        project = w_project_ref[...].astype(F32)
        packet_ref[29] = jnp.concatenate([project, jnp.zeros_like(project)], axis=1).astype(BF)


def merge_kernel(atoms_ref, packet_ref, got_ref, far_ref, near_ref, share_ref):
    for yh, out in enumerate((far_ref, near_ref)):
        for zh in range(2):
            out[zh, 0:2] = atoms_ref[zh, yh]
            tile = (zh * 2 + yh) * 4
            out[zh, 2] = got_ref[tile : tile + 4].reshape((2,) + ATOM)
    share_ref[0] = packet_ref[16:30]
    share_ref[1] = got_ref[16:30]


def widen_kernel(
    first_hbm, second_hbm, middle_hbm, w1_ref, w2_ref, w3_ref, first_ref, second_ref, middle_ref, sems
):
    copies = [
        pltpu.make_async_copy(a, b, sems.at[n])
        for n, (a, b) in enumerate(
            ((first_hbm, first_ref), (second_hbm, second_ref), (middle_hbm, middle_ref))
        )
    ]
    for copy in copies:
        copy.start()
    zero = jnp.zeros((64, 64), F32)
    for copy, weight_ref, out_ref in zip(copies, (first_ref, second_ref), (w1_ref, w2_ref)):
        copy.wait()
        for tx in range(3):
            for ty in range(3):
                w = [weight_ref[9 * tx + 3 * ty + tz].astype(F32) for tz in range(3)]
                for pair, blocks in enumerate(
                    (((w[0], w[1]), (zero, w[0])), ((w[2], zero), (w[1], w[2])))
                ):
                    wide = jnp.concatenate([jnp.concatenate(p, axis=1) for p in blocks], axis=0)
                    row = tx * 256 + pair * 128
                    out_ref[row : row + 128, ty * 128 : ty * 128 + 128] = wide.T.astype(BF)
    copies[2].wait()
    w3_ref[...] = jnp.zeros_like(w3_ref)
    for tx in range(3):
        for ty in range(3):
            for tz in range(3):
                for zo in range(2):
                    row = tx * 256 + (tz + zo) * 64
                    column = (ty * 2 + zo) * 128
                    w3_ref[row : row + 64, column : column + 128] = middle_ref[
                        9 * tx + 3 * ty + tz
                    ]


def join_kernel(*refs):
    *sources, out = refs
    row = 0
    for source in sources:
        out[row : row + source.shape[0]] = source[...]
        row += source.shape[0]


def joined(*arrays):
    rows = sum(a.shape[0] for a in arrays)
    return pl.pallas_call(
        join_kernel,
        out_shape=shape((rows,) + arrays[0].shape[1:]),
        in_specs=[VMEM] * len(arrays),
        out_specs=VMEM,
        compiler_params=params(8),
    )(*arrays)


def stack_kernel(far, near, below, above, low_ref, high_ref):
    for z, out in enumerate((low_ref, high_ref)):
        for n, source in enumerate((far, near, below, above)):
            out[n] = source[z]


def leaf_conv(source, b, k, n, length, weight_ref):
    rows = n * length * 16
    parts = [
        source[b, k + dk : k + dk + n, dx : dx + length].reshape(rows, 128)
        for dx in range(3)
        for dk in range(2)
    ]
    wide = dot(jnp.concatenate(parts, axis=1), weight_ref[...])
    return (
        wide[:, 128:256]
        + pltpu.roll(wide[:, :128], 1, 0)
        + pltpu.roll(wide[:, 256:], rows - 1, 0)
    )


def main_kernel(
    neighbour_ref, far, near, below_y, above_y, below_z, above_z, w1, w2, w3,
    skip_ref, coarse_ref,
    table, wide, first, second, masks, rows_a, middle_in, rows_b, turned, sems,
):
    copies = []
    for n, source in enumerate((far, near, below_y, above_y)):
        copies += [
            pltpu.make_async_copy(
                source.at[zh], table.at[pl.ds((zh * 4 + n) * 6, 6)], sems.at[n * 2 + zh]
            )
            for zh in range(2)
        ]
    for n, source in enumerate((below_z, above_z)):
        copies.append(
            pltpu.make_async_copy(source, table.at[pl.ds(48 + n * 24, 24)], sems.at[8 + n])
        )
    for copy in copies:
        copy.start()
    table[ABSENT] = jnp.zeros(ATOM, BF)

    g, h, j, _ = position()
    present, atom_rows = {}, {}
    for b in range(2):
        for n, (dx, dy, dz) in enumerate(OFFSETS):
            entry = neighbour_ref[b, n]
            there = entry >= 0
            present[b, dx, dy, dz] = there.astype(F32)
            apart_g = (entry >> 5) - g
            apart_j = ((entry >> 1) & 7) - j
            other = ((entry >> 4) & 1) != h
            of_z = jnp.where(apart_g < 0, 48, 72)
            of_y = jnp.where(apart_j < 0, 12, 18)
            for z in range(4):
                for x in range(4):
                    for y in range(4):
                        if (STEP[x], STEP[y], STEP[z]) == (dx, dy, dz):
                            row = entry & 1
                            row += jnp.where(apart_g == 0, HALF[z] * 24, of_z) if dz else HALF[z] * 24
                            row += jnp.where(apart_j == 0, HALF[y] * 6, of_y) if dy else HALF[y] * 6
                            row += jnp.where(other, 4, HALF[x] * 2) if dx else HALF[x] * 2
                            atom_rows[b, z, x, y] = jnp.where(there, row, ABSENT)

    low = halves(128)
    y_row = lax.broadcasted_iota(jnp.int32, (16, 128), 0)
    for b in range(2):
        for dx in range(3):
            of_z = []
            for dz in range(3):
                p = [present[b, dx - 1, dy - 1, dz - 1] for dy in range(3)]
                of_z.append(jnp.where(y_row < 4, p[0], jnp.where(y_row < 12, p[1], p[2])))
            masks[b, 0, dx] = of_z[0]
            masks[b, 1, dx] = jnp.where(low, of_z[0], of_z[1])
            masks[b, 2, dx] = of_z[1]
            masks[b, 3, dx] = jnp.where(low, of_z[1], of_z[2])
            masks[b, 4, dx] = of_z[2]

    for copy in copies:
        copy.wait()

    upper = lax.broadcasted_iota(jnp.int32, (1, 1, 8, 1), 2) < 4
    for b in range(2):
        for z in range(4):
            for x in range(4):
                a = [
                    table[atom_rows[b, z, x, y]].astype(F32).reshape(2, 2, 8, 128) for y in range(4)
                ]
                r = [pltpu.roll(v.reshape(4, 8, 128), 4, 1).reshape(2, 2, 8, 128) for v in a]
                even = jnp.concatenate(
                    [jnp.where(upper, a[0], r[1]), jnp.where(upper, a[2], r[3])], axis=2
                ).astype(BF)
                odd = jnp.concatenate(
                    [jnp.where(upper, r[0], a[1]), jnp.where(upper, r[2], a[3])], axis=2
                ).astype(BF)
                for pair in range(2):
                    for k in range(2):
                        wide[b, 2 * z + pair, 4 * x + 2 * k] = even[pair, k]
                        wide[b, 2 * z + pair, 4 * x + 2 * k + 1] = odd[pair, k]

    def masked(value, b, pattern, edge):
        mask = [masks[b, pattern, dx][None] for dx in range(3)]
        value = value.reshape(8 + 2 * edge, 16, 128)
        return jnp.concatenate(
            [value[:edge] * mask[0], value[edge : edge + 8] * mask[1], value[edge + 8 :] * mask[2]],
            axis=0,
        )

    for b in range(2):
        for k, n in ((0, 2), (2, 2), (4, 2), (6, 1)):
            value = gelu(leaf_conv(wide, b, k, n, 14, w1)).reshape(n, 14 * 16, 128)
            for i in range(n):
                pattern = (0, 1, 2, 2, 2, 3, 4)[k + i]
                first[b, k + i] = masked(value[i], b, pattern, 3).astype(BF)
    for b in range(2):
        for k, n in ((0, 2), (2, 2), (4, 2)):
            value = gelu(leaf_conv(first, b, k, n, 12, w2)).reshape(n, 12 * 16, 128)
            for i in range(n):
                pattern = (0, 2, 2, 2, 2, 4)[k + i]
                second[b, k + i] = masked(value[i], b, pattern, 2).astype(BF)

    for b in range(2):
        layers = []
        for k in range(6):
            v = second[b, k].astype(F32)
            v = (v.reshape(6, 2, 16, 128)[:, 0] + v.reshape(6, 2, 16, 128)[:, 1]).reshape(96, 128)
            v = v + pltpu.roll(v, 64, 1)
            rows_a[b, k] = v + pltpu.roll(v, 95, 0)
            layers.append((rows_a[b, k, pl.ds(0, 48, stride=2), :] * 0.125).astype(BF).astype(F32))
        for pair in range(3):
            middle_in[b, pair] = jnp.where(low, layers[2 * pair], layers[2 * pair + 1])

    operands = []
    for b in range(2):
        for k in range(2):
            operands.append(
                jnp.concatenate(
                    [
                        middle_in[b, k + dk, dx * 8 : dx * 8 + 32]
                        for dx in range(3)
                        for dk in range(2)
                    ],
                    axis=1,
                )
            )
    deep = dot(jnp.concatenate(operands, axis=0).astype(BF), w3[...])
    deep = (
        deep[:, 256:512] + pltpu.roll(deep[:, :256], 1, 0) + pltpu.roll(deep[:, 512:], 127, 0)
    )
    deep = gelu(deep).astype(BF).astype(F32)
    deep = (deep[:, :128] + deep[:, 128:]).reshape(8, 2, 8, 128)
    deep = (deep[:, 0] + deep[:, 1]).reshape(64, 128)
    rows_b[...] = deep + pltpu.roll(deep, 63, 0)
    coarse_ref[...] = (
        jnp.concatenate(
            [rows_b[pl.ds(2, 8, stride=8), :], rows_b[pl.ds(4, 8, stride=8), :]], axis=0
        )
        * 0.125
    ).astype(BF)

    for pair in range(4):
        v = [
            second[b, 1 + pair, 2:10].astype(F32)[:, 4:12, :].reshape(64, 128) for b in range(2)
        ]
        turned[pl.ds(2 * pair, 64, stride=8), :] = jnp.where(low, v[0], pltpu.roll(v[1], 64, 1))
        turned[pl.ds(2 * pair + 1, 64, stride=8), :] = jnp.where(
            low, pltpu.roll(v[0], 64, 1), v[1]
        )
    skip_ref[...] = turned[...].T.astype(BF).reshape(2, 64, 512)


def last_kernel(
    live_ref, neighbour_ref, taps_ref, voxel_ref, own, below, above, mine_a, mine_b, theirs_a, theirs_b,
    w_output, skip_ref, out_ref, coarse_ref,
):
    g, h, j, core = position()
    entry = neighbour_ref[...]
    apart_g = (entry >> 5) - g
    apart_j = ((entry >> 1) & 7) - j
    code = (
        jnp.where(apart_g == 0, 0, jnp.where(apart_g < 0, 6, 12))
        + jnp.where(apart_j == 0, 0, jnp.where(apart_j < 0, 2, 4))
        + jnp.where(((entry >> 4) & 1) == h, 0, 1)
    ) * 16 + (entry & 1) * 4
    code = jnp.where(entry >= 0, code, -4096).astype(F32)
    rows = jnp.sum(taps_ref[0] * code[0:1] + taps_ref[1] * code[1:2], axis=1, keepdims=True)
    rows = (rows + voxel_ref[...]).astype(jnp.int32)
    tiles = jnp.concatenate([r[...].reshape(96, 128) for r in (own, below, above)], axis=0)
    chosen = (rows == lax.broadcasted_iota(jnp.int32, (432, 288), 1)).astype(F32).astype(BF)
    taps = dot(chosen, tiles).astype(BF)

    def weight(parts, t):
        if t < 14:
            chosen = [part[:, t] for part in parts]
        else:
            chosen = [part[k : k + 4, t - 14] for k in (0, 4) for part in parts]
        return jnp.concatenate(chosen, axis=0).reshape(256, 128)

    def deepest(early, late):
        total = jnp.zeros((16, 256), F32)
        for t in range(27):
            total = total + lax.dot_general(
                taps[t * 16 : (t + 1) * 16],
                weight(early if t < 14 else late, t),
                (((1,), (1,)), ((), ())),
                preferred_element_type=F32,
            )
        coarse_ref[...] = dot(gelu(total).astype(BF), weight(late, 27))

    @pl.when(core == 0)
    def _():
        deepest((mine_a, mine_b), (theirs_a, theirs_b))

    @pl.when(core == 1)
    def _():
        deepest((theirs_a, theirs_b), (mine_a, mine_b))

    coarse = coarse_ref[...].astype(BF).astype(F32).T[:64].astype(BF)
    row = lax.broadcasted_iota(jnp.int32, (16, 512), 0)
    voxel = lax.broadcasted_iota(jnp.int32, (16, 512), 1)
    place = ((voxel >> 5) & 1) * 8 + ((voxel >> 2) & 1) * 2 + ((voxel >> 8) & 1)
    for b in range(2):
        spread = (row == place + b * 4).astype(F32).astype(BF)
        widened = dot(coarse, spread).astype(BF)
        mixed = dot(w_output[...], jnp.concatenate([skip_ref[b], widened], axis=0))
        mixed = jnp.where(b < live_ref[0], mixed, 0.0)
        out_ref[b] = mixed.astype(BF)


def shape(dims, kind=BF):
    return jax.ShapeDtypeStruct(dims, kind)


def shards(
    features, live_counts, neighbours, w_first, w_second, w_middle, w_coarse, w_project, w_output
):
    sizes = (lax.axis_size("grp"), lax.axis_size("ch"))

    def moved(value, step_h, step_j, step_g):
        return lax.ppermute(value, AXES, pairs_for(step_h, step_j, step_g, sizes))

    atoms, packet = pl.pallas_call(
        pack_kernel,
        out_shape=(shape((2, 2, 2, 2) + ATOM), shape((16, 16, 128))),
        in_specs=[VMEM],
        out_specs=(VMEM, VMEM),
        scratch_shapes=[pltpu.VMEM((512, 128), F32)],
        compiler_params=params(8),
    )(features)
    packet = pl.pallas_call(
        share_kernel,
        out_shape=shape((30, 16, 128)),
        in_specs=[VMEM, VMEM, VMEM],
        out_specs=VMEM,
        compiler_params=params(8),
    )(w_coarse, w_project, packet)
    half_block = shape((2, 3, 2) + ATOM)
    far, near, share = pl.pallas_call(
        merge_kernel,
        out_shape=(half_block, half_block, shape((2, 14, 16, 128))),
        in_specs=[VMEM] * 3,
        out_specs=(VMEM,) * 3,
        compiler_params=params(8),
    )(atoms, packet, moved(packet, 1, 0, 0))
    below_y = moved(near, 0, 1, 0)
    above_y = moved(far, 0, -1, 0)
    share_more = exchanged(share, (2, 2), 0, sizes)
    w1, w2, w3 = pl.pallas_call(
        widen_kernel,
        out_shape=(shape((768, 384)), shape((768, 384)), shape((768, 768))),
        in_specs=[HBM] * 3,
        out_specs=(VMEM,) * 3,
        scratch_shapes=[
            pltpu.VMEM((27, 64, 64), BF),
            pltpu.VMEM((27, 64, 64), BF),
            pltpu.VMEM((27, 64, 128), BF),
            pltpu.SemaphoreType.DMA((3,)),
        ],
        compiler_params=params(8),
    )(after(w_first, near), after(w_second, near), after(jnp.swapaxes(w_middle, 1, 2), near))
    low_z, high_z = pl.pallas_call(
        stack_kernel,
        out_shape=(shape((4, 3, 2) + ATOM),) * 2,
        in_specs=[VMEM] * 4,
        out_specs=(VMEM,) * 2,
        compiler_params=params(8),
    )(far, near, after(below_y, w1), above_y)
    below_z = moved(high_z, 0, 0, 1)
    above_z = moved(low_z, 0, 0, -1)
    share = joined(share, after(share_more, low_z))
    share_more = exchanged(share, (1, 4), 0, sizes)
    mine_a = joined(share, after(share_more, below_z, above_z))
    mine_b = exchanged(mine_a, (4, 1), 0, sizes)
    theirs_a = exchanged(mine_a, (0, 0), 1, sizes)

    skip, coarse = pl.pallas_call(
        main_kernel,
        out_shape=(shape((2, 64, 512)), shape((16, 128))),
        in_specs=[SMEM] + [ANY] * 6 + [VMEM] * 3,
        out_specs=(VMEM, VMEM),
        scratch_shapes=[
            pltpu.VMEM((97,) + ATOM, BF),
            pltpu.VMEM((2, 8, 16, 16, 128), BF),
            pltpu.VMEM((2, 7, 14, 16, 128), BF),
            pltpu.VMEM((2, 6, 12, 16, 128), BF),
            pltpu.VMEM((2, 5, 3, 16, 128), F32),
            pltpu.VMEM((2, 6, 96, 128), F32),
            pltpu.VMEM((2, 3, 48, 128), F32),
            pltpu.VMEM((64, 128), F32),
            pltpu.VMEM((512, 128), F32),
            pltpu.SemaphoreType.DMA((10,)),
        ],
        compiler_params=params(20),
    )(
        after(neighbours, mine_a),
        far.reshape((2, 6) + ATOM),
        near.reshape((2, 6) + ATOM),
        below_y.reshape((2, 6) + ATOM),
        above_y.reshape((2, 6) + ATOM),
        below_z.reshape((24,) + ATOM),
        above_z.reshape((24,) + ATOM),
        w1,
        w2,
        w3,
    )

    theirs_b = exchanged(after(mine_b, coarse), (0, 0), 1, sizes)
    both = joined(coarse[None], moved(coarse, 1, 0, 0)[None])
    layer = joined(both, moved(both, 0, 1, 0), moved(both, 0, -1, 0))
    below, above = moved(layer, 0, 0, 1), moved(layer, 0, 0, -1)
    return pl.pallas_call(
        last_kernel,
        out_shape=shape((2, 64, 512)),
        in_specs=[SMEM] + [VMEM] * 12,
        out_specs=VMEM,
        scratch_shapes=[
            pltpu.VMEM((16, 128), F32),
        ],
        compiler_params=params(8),
    )(
        live_counts,
        neighbours,
        *(jnp.asarray(a) for a in tap_table()),
        layer,
        below,
        above,
        mine_a,
        mine_b,
        theirs_a,
        theirs_b,
        w_output,
        skip,
    )


def solution(mesh):
    return jax.shard_map(
        shards,
        mesh=mesh,
        in_specs=(
            P(AXES, None, None),
            P(AXES),
            P(AXES, None),
            P(),
            P(),
            P(),
            P(None, "ch", None),
            P("ch", None),
            P(),
        ),
        out_specs=P(AXES, None, None),
        check_vma=False,
    )
```

time: 85.8 us -> 58.5 us (0.68)
  between operations: 14.4 us -> 0.81 us
  starting transfers between devices: 29.4 us -> 25.2 us
  Pallas kernels: 16.2 us -> 12.1 us
  other arithmetic: 2.01 us -> 0 us
  waiting for transfers between devices: 16 us -> 14.2 us
    ppermute x10, starting transfers between devices: 29.4 us -> 18.6 us  [moved(): return lax.ppermute(value, AXES, pairs_for(step_h, step_j, step_g, sizes))]
    ppermute x0 -> x5, starting transfers between devices: none -> 6.58 us  [exchanged(): return lax.ppermute(value, AXES, pairs)]
    pallas_call x1, Pallas kernels: 11.8 us -> 7.2 us  [shards(): pl.pallas_call(main_kernel, out_shape=(shape((2, 64, 512)), shape((16, 12...]
    ppermute x10, waiting for transfers between devices: 16 us -> 14.2 us  [moved(): return lax.ppermute(value, AXES, pairs_for(step_h, step_j, step_g, sizes))]
    concatenate x5 -> x0, other arithmetic: 1.63 us -> none  [the longest x1 1.55 us: shards(): jnp.concatenate([w_coarse, jnp.pad(w_project, ((0, 0), (0, 64)))[None]],...]
    unnamed x17 -> x20, local copies, waits for them, and re-layouts: 3.92 us -> 5.54 us
    reshape x2 -> x0, local copies, waits for them, and re-layouts: 1.52 us -> none  [shards(): entry = neighbours.reshape(54)]
    pallas_call x3 -> x8, Pallas kernels: 1.79 us -> 2.23 us  [the longest x1 2.12 us: shards(): pl.pallas_call(widen_kernel, out_shape=(shape((768, 384)), shape((768, 38...]
  transfers between devices with their start and end apart: 11 -> 15, of which waited for: 7 -> 7; matrix products, arithmetic and copies ran while one was open for 4% -> 0% of each run, Pallas kernels for 16% -> 16%
where the time goes in v2:
time: 58.5 us; the launch traced here: 57.8 us
  starting transfers between devices  25.2 us (43%)
  waiting for transfers between devices  14.2 us (24%)
  Pallas kernels  12.1 us (21%)
  local copies, waits for them, and re-layouts  5.54 us (9%)
  between operations  0.81 us (1%)
    ppermute x10, starting transfers between devices, moved(): return lax.ppermute(value, AXES, pairs_for(step_h, step_j, step_g, sizes))  18.6 us
    ppermute x10, waiting for transfers between devices, moved(): return lax.ppermute(value, AXES, pairs_for(step_h, step_j, step_g, sizes))  14.2 us
    pallas_call x1, Pallas kernels, shards(): pl.pallas_call(main_kernel, out_shape=(shape((2, 64, 512)), shape((16, 12...  7.2 us
    ppermute x5, starting transfers between devices, exchanged(): return lax.ppermute(value, AXES, pairs)  6.58 us
    unnamed x20, local copies, waits for them, and re-layouts  5.54 us
    pallas_call x1, Pallas kernels, shards(): pl.pallas_call(last_kernel, out_shape=shape((2, 64, 512)), in_specs=[SMEM...  2.45 us
    pallas_call x1, Pallas kernels, shards(): pl.pallas_call(widen_kernel, out_shape=(shape((768, 384)), shape((768, 38...  2.12 us
  transfers between devices with their start and end apart: 15, of which 7 were waited for; matrix products, arithmetic and copies ran while one was open for 0% of the time, Pallas kernels for 16%

profile of v2, /device:TPU:1, one launch (start us, length us, event | category | flops | bytes accessed | tf_op | source)
XLA Modules:
  0.0 57.8 jit_solution(3745992321823076637)
XLA Ops:
  0.0 0.9 %copy-done.5 = bf16[2,64,512]{2,1,0:T(8,128)(2,1)S(1)} copy-done((bf16[2,64,512]{2,1,0:T(8,128)(2,1)S(1)}, bf16[2,64,512]{2,1,0:T(8,128)(2,1)}, u32[]{:S(2)}) %copy-start.5) | copy-done | bytes 131096
  0.9 0.2 shard_map.109
  1.1 0.0 copy-start.6
  1.2 0.9 %copy-done.6 = bf16[27,16,128]{2,1,0:T(8,128)(2,1)S(1)} copy-done((bf16[27,16,128]{2,1,0:T(8,128)(2,1)S(1)}, bf16[27,16,128]{2,1,0:T(8,128)(2,1)}, u32[]{:S(2)}) %copy-start.6) | copy-done | bytes 110616
  2.0 0.7 %copy-done.8 = bf16[16,64]{1,0:T(8,128)(2,1)S(1)} copy-done((bf16[16,64]{1,0:T(8,128)(2,1)S(1)}, bf16[16,64]{1,0:T(8,128)(2,1)}, u32[]{:S(2)}) %copy-start.8) | copy-done | bytes 2072
  2.7 3.8 %collective-permute-start = (bf16[30,16,128]{2,1,0:T(8,128)(2,1)S(1)}, bf16[30,16,128]{2,1,0:T(8,128)(2,1)S(1)}, u32[]{:S(2)}, u32[]{:S(2)}) collective-permute-start(bf16[30,16,128]{2,1,0:T(8,128)(2,1)S(1)} %shard_map.110.packet_ref), channel_id=1, source_target_pairs={{0,8},{1,9},{2,10},{3,11},{4,12},{5,13},{6,14},{7,15},{8,0},{9,1},... | collective-permute-start | bytes 368648 | tf_op jit(solution)/shard_map/ppermute | solution.py:430
  6.6 2.8 %collective-permute-done.got_ref = bf16[30,16,128]{2,1,0:T(8,128)(2,1)S(1)} collective-permute-done((bf16[30,16,128]{2,1,0:T(8,128)(2,1)S(1)}, bf16[30,16,128]{2,1,0:T(8,128)(2,1)S(1)}, u32[]{:S(2)}, u32[]{:S(2)}) %collective-permute-start) | collective-permute-done | bytes 122912 | tf_op jit(solution)/shard_map/ppermute | solution.py:430
  9.4 2.8 %collective-permute-start.1 = (bf16[2,14,16,128]{3,2,1,0:T(8,128)(2,1)S(1)}, bf16[2,14,16,128]{3,2,1,0:T(8,128)(2,1)S(1)}, u32[]{:S(2)}, u32[]{:S(2)}) collective-permute-start(bf16[2,14,16,128]{3,2,1,0:T(8,128)(2,1)S(1)} %get-tuple-element.27.refs_0_), channel_id=1, source_target_pairs={{0,2},{1,3},{2,0},{3,1},{4,6},{5,7},{6,4},{7,5},{8,10},{9,11},{10,... | collective-permute-start | bytes 344072 | tf_op jit(solution)/shard_map/ppermute | solution.py:69
  12.2 0.3 collective-permute-start.2
  12.5 3.3 %collective-permute-start.3 = (bf16[2,3,2,2,16,128]{5,4,3,2,1,0:T(8,128)(2,1)S(1)}, bf16[2,3,2,2,16,128]{5,4,3,2,1,0:T(8,128)(2,1)S(1)}, u32[]{:S(2)}, u32[]{:S(2)}) collective-permute-start(bf16[2,3,2,2,16,128]{5,4,3,2,1,0:T(8,128)(2,1)S(1)} %get-tuple-element.28.far), channel_id=1, source_target_pairs={{0,7},{1,0},{2,1},{3,2},{4,3},{5,4},{6,5},{7,6},{8,15},{9,8},{10,9... | collective-permute-start | bytes 294920 | tf_op jit(solution)/shard_map/ppermute | solution.py:430
  15.8 1.0 %copy-done = bf16[27,64,64]{2,1,0:T(8,128)(2,1)S(1)} copy-done((bf16[27,64,64]{2,1,0:T(8,128)(2,1)S(1)}, bf16[27,64,64]{2,1,0:T(8,128)(2,1)}, u32[]{:S(2)}) %copy-start) | copy-done | bytes 221208
  16.8 1.0 %copy-done.1 = bf16[27,64,64]{2,1,0:T(8,128)(2,1)S(1)} copy-done((bf16[27,64,64]{2,1,0:T(8,128)(2,1)S(1)}, bf16[27,64,64]{2,1,0:T(8,128)(2,1)}, u32[]{:S(2)}) %copy-start.1) | copy-done | bytes 221208
  17.8 1.0 %copy-done.2 = bf16[27,128,64]{1,2,0:T(8,128)(2,1)S(1)} copy-done((bf16[27,128,64]{1,2,0:T(8,128)(2,1)S(1)}, bf16[27,128,64]{1,2,0:T(8,128)(2,1)}, u32[]{:S(2)}) %copy-start.2) | copy-done | bytes 442392
  18.8 2.1 %shard_map.112 = (bf16[768,384]{1,0:T(8,128)(2,1)S(1)}, bf16[768,384]{1,0:T(8,128)(2,1)S(1)}, bf16[768,768]{1,0:T(8,128)(2,1)S(1)}) custom-call(bf16[27,64,64]{2,1,0:T(8,128)(2,1)S(1)} %copy-done, bf16[27,64,64]{2,1,0:T(8,128)(2,1)S(1)} %copy-done.1, bf16[27,64,128]{2,1,0:T(8,128)(2,1)S(1)} %bitcast.9), custom_call_target="tpu_custom_call" | custom-call | tf_op jit(solution)/shard_map/pallas_call | solution.py:458
  20.9 0.0 copy-start.9
  21.0 1.4 %collective-permute-start.4 = (bf16[4,14,16,128]{3,2,1,0:T(8,128)(2,1)S(1)}, bf16[4,14,16,128]{3,2,1,0:T(8,128)(2,1)S(1)}, u32[]{:S(2)}, u32[]{:S(2)}) collective-permute-start(bf16[4,14,16,128]{3,2,1,0:T(8,128)(2,1)S(1)} %shard_map.114.refs_0_), channel_id=1, source_target_pairs={{0,1},{1,0},{2,3},{3,2},{4,5},{5,4},{6,7},{7,6},{8,9},{9,8},{10,11... | collective-permute-start | bytes 688136 | tf_op jit(solution)/shard_map/ppermute | solution.py:69
  22.4 2.6 %collective-permute-start.5 = (bf16[4,3,2,2,16,128]{5,4,3,2,1,0:T(8,128)(2,1)S(1)}, bf16[4,3,2,2,16,128]{5,4,3,2,1,0:T(8,128)(2,1)S(1)}, u32[]{:S(2)}, u32[]{:S(2)}) collective-permute-start(bf16[4,3,2,2,16,128]{5,4,3,2,1,0:T(8,128)(2,1)S(1)} %get-tuple-element.37), channel_id=1, source_target_pairs={{0,16},{1,17},{2,18},{3,19},{4,20},{5,21},{6,22},{7,23},{8,24},{9,... | collective-permute-start | bytes 589832 | tf_op jit(solution)/shard_map/ppermute | solution.py:430
  25.1 2.6 %collective-permute-done.5 = bf16[4,3,2,2,16,128]{5,4,3,2,1,0:T(8,128)(2,1)S(1)} collective-permute-done((bf16[4,3,2,2,16,128]{5,4,3,2,1,0:T(8,128)(2,1)S(1)}, bf16[4,3,2,2,16,128]{5,4,3,2,1,0:T(8,128)(2,1)S(1)}, u32[]{:S(2)}, u32[]{:S(2)}) %collective-permute-start.5) | collective-permute-done | bytes 196640 | tf_op jit(solution)/shard_map/ppermute | solution.py:430
  27.7 2.5 %collective-permute-done.6 = bf16[4,3,2,2,16,128]{5,4,3,2,1,0:T(8,128)(2,1)S(1)} collective-permute-done((bf16[4,3,2,2,16,128]{5,4,3,2,1,0:T(8,128)(2,1)S(1)}, bf16[4,3,2,2,16,128]{5,4,3,2,1,0:T(8,128)(2,1)S(1)}, u32[]{:S(2)}, u32[]{:S(2)}) %collective-permute-start.6) | collective-permute-done | bytes 196640 | tf_op jit(solution)/shard_map/ppermute | solution.py:430
  30.2 1.8 %collective-permute-start.12 = (bf16[8,14,16,128]{3,2,1,0:T(8,128)(2,1)S(1)}, bf16[8,14,16,128]{3,2,1,0:T(8,128)(2,1)S(1)}, u32[]{:S(2)}, u32[]{:S(2)}) collective-permute-start(bf16[8,14,16,128]{3,2,1,0:T(8,128)(2,1)S(1)} %shard_map.115.mine_a), channel_id=1, source_target_pairs={{0,4},{1,5},{2,6},{3,7},{4,0},{5,1},{6,2},{7,3},{8,12},{9,13},{10,... | collective-permute-start | bytes 1376264 | tf_op jit(solution)/shard_map/ppermute | solution.py:69
  32.0 7.2 %shard_map.116 = (bf16[2,64,512]{2,1,0:T(8,128)(2,1)S(1)}, bf16[16,128]{1,0:T(8,128)(2,1)S(1)}) custom-call(s32[2,27]{1,0:T(2,128)S(1)} %copy-done.9, bf16[2,6,2,16,128]{4,3,2,1,0:T(8,128)(2,1)S(1)} %bitcast.10, bf16[2,6,2,16,128]{4,3,2,1,0:T(8,128)(2,1)S(1)} %bitcast.11, bf16[2,6,2,16,128]{4,3,2,1,0:T(8,128)(2,1)S(1)} %bitcast.12, ...), custom_call_target="tpu_custom_call" | custom-call | tf_op jit(solution)/shard_map/pallas_call | solution.py:486
  39.2 0.6 collective-permute-start.14
  39.8 2.9 %collective-permute-start.7 = (bf16[16,128]{1,0:T(8,128)(2,1)S(1)}, bf16[16,128]{1,0:T(8,128)(2,1)S(1)}, u32[]{:S(2)}, u32[]{:S(2)}) collective-permute-start(bf16[16,128]{1,0:T(8,128)(2,1)S(1)} %get-tuple-element.42), channel_id=1, source_target_pairs={{0,8},{1,9},{2,10},{3,11},{4,12},{5,13},{6,14},{7,15},{8,0},{9,1},... | collective-permute-start | bytes 12296 | tf_op jit(solution)/shard_map/ppermute | solution.py:430
  42.7 1.1 %collective-permute-done.7 = bf16[16,128]{1,0:T(8,128)(2,1)S(1)} collective-permute-done((bf16[16,128]{1,0:T(8,128)(2,1)S(1)}, bf16[16,128]{1,0:T(8,128)(2,1)S(1)}, u32[]{:S(2)}, u32[]{:S(2)}) %collective-permute-start.7) | collective-permute-done | bytes 4128 | tf_op jit(solution)/shard_map/ppermute | solution.py:430
  43.8 1.2 %collective-permute-start.9 = (bf16[2,16,128]{2,1,0:T(8,128)(2,1)S(1)}, bf16[2,16,128]{2,1,0:T(8,128)(2,1)S(1)}, u32[]{:S(2)}, u32[]{:S(2)}) collective-permute-start(bf16[2,16,128]{2,1,0:T(8,128)(2,1)S(1)} %shard_map.117.refs_0_), channel_id=1, source_target_pairs={{0,7},{1,0},{2,1},{3,2},{4,3},{5,4},{6,5},{7,6},{8,15},{9,8},{10,9... | collective-permute-start | bytes 24584 | tf_op jit(solution)/shard_map/ppermute | solution.py:430
  45.0 0.2 collective-permute-start.8
  45.3 1.0 %collective-permute-done.9.refs_2_ = bf16[2,16,128]{2,1,0:T(8,128)(2,1)S(1)} collective-permute-done((bf16[2,16,128]{2,1,0:T(8,128)(2,1)S(1)}, bf16[2,16,128]{2,1,0:T(8,128)(2,1)S(1)}, u32[]{:S(2)}, u32[]{:S(2)}) %collective-permute-start.9) | collective-permute-done | bytes 8224 | tf_op jit(solution)/shard_map/ppermute | solution.py:430
  46.3 3.3 %collective-permute-done.8.refs_1_ = bf16[2,16,128]{2,1,0:T(8,128)(2,1)S(1)} collective-permute-done((bf16[2,16,128]{2,1,0:T(8,128)(2,1)S(1)}, bf16[2,16,128]{2,1,0:T(8,128)(2,1)S(1)}, u32[]{:S(2)}, u32[]{:S(2)}) %collective-permute-start.8) | collective-permute-done | bytes 8224 | tf_op jit(solution)/shard_map/ppermute | solution.py:430
  49.6 2.7 %collective-permute-start.11 = (bf16[6,16,128]{2,1,0:T(8,128)(2,1)S(1)}, bf16[6,16,128]{2,1,0:T(8,128)(2,1)S(1)}, u32[]{:S(2)}, u32[]{:S(2)}) collective-permute-start(bf16[6,16,128]{2,1,0:T(8,128)(2,1)S(1)} %shard_map.118.own), channel_id=1, source_target_pairs={{0,112},{1,113},{2,114},{3,115},{4,116},{5,117},{6,118},{7,119},{8... | collective-permute-start | bytes 73736 | tf_op jit(solution)/shard_map/ppermute | solution.py:430
  52.3 1.5 %collective-permute-start.10 = (bf16[6,16,128]{2,1,0:T(8,128)(2,1)S(1)}, bf16[6,16,128]{2,1,0:T(8,128)(2,1)S(1)}, u32[]{:S(2)}, u32[]{:S(2)}) collective-permute-start(bf16[6,16,128]{2,1,0:T(8,128)(2,1)S(1)} %shard_map.118.own), channel_id=1, source_target_pairs={{0,16},{1,17},{2,18},{3,19},{4,20},{5,21},{6,22},{7,23},{8,24},{9,... | collective-permute-start | bytes 73736 | tf_op jit(solution)/shard_map/ppermute | solution.py:430
  54.5 0.9 %collective-permute-done.11.above = bf16[6,16,128]{2,1,0:T(8,128)(2,1)S(1)} collective-permute-done((bf16[6,16,128]{2,1,0:T(8,128)(2,1)S(1)}, bf16[6,16,128]{2,1,0:T(8,128)(2,1)S(1)}, u32[]{:S(2)}, u32[]{:S(2)}) %collective-permute-start.11) | collective-permute-done | bytes 24608 | tf_op jit(solution)/shard_map/ppermute | solution.py:430
  55.4 2.5 %shard_map.119 = bf16[2,64,512]{2,1,0:T(8,128)(2,1)} custom-call(s32[1]{0:T(128)S(6)} %copy.12.live_ref, s32[2,27]{1,0:T(2,128)S(1)} %copy-done.9, f32[2,432,27]{2,1,0:T(8,128)S(1)} %copy-done.3, f32[432,1]{1,0:T(8,128)S(1)} %copy-done.4, bf16[6,16,128]{2,1,0:T(8,128)(2,1)S(1)} %shard_map.118.own, bf16[6,16,128]{2,1,0:T(8,128)(2,1)S(1)} %collective-permute-done.10.below, ...), custom_call_target="tpu_custom_call" | custom-call | tf_op jit(solution)/shard_map/pallas_call | solution.py:521
  (29 shorter events, 0.2 us)
Async XLA Ops:
  0.0 0.9 %copy-start.5 = (bf16[2,64,512]{2,1,0:T(8,128)(2,1)S(1)}, bf16[2,64,512]{2,1,0:T(8,128)(2,1)}, u32[]{:S(2)}) copy-start(bf16[2,64,512]{2,1,0:T(8,128)(2,1)} %features_ref.1) | copy-start | bytes 393220
  1.1 0.9 %copy-start.6 = (bf16[27,16,128]{2,1,0:T(8,128)(2,1)S(1)}, bf16[27,16,128]{2,1,0:T(8,128)(2,1)}, u32[]{:S(2)}) copy-start(bf16[27,16,128]{2,1,0:T(8,128)(2,1)} %w_coarse_ref.1) | copy-start | bytes 331780
  2.0 0.7 %copy-start.8 = (bf16[16,64]{1,0:T(8,128)(2,1)S(1)}, bf16[16,64]{1,0:T(8,128)(2,1)}, u32[]{:S(2)}) copy-start(bf16[16,64]{1,0:T(8,128)(2,1)} %w_project_ref.1) | copy-start | bytes 6148
  2.7 6.6 %collective-permute-start = (bf16[30,16,128]{2,1,0:T(8,128)(2,1)S(1)}, bf16[30,16,128]{2,1,0:T(8,128)(2,1)S(1)}, u32[]{:S(2)}, u32[]{:S(2)}) collective-permute-start(bf16[30,16,128]{2,1,0:T(8,128)(2,1)S(1)} %shard_map.110.packet_ref), channel_id=1, source_target_pairs={{0,8},{1,9},{2,10},{3,11},{4,12},{5,13},{6,14},{7,15},{8,0},{9,1},... | collective-permute-start | bytes 368648 | tf_op jit(solution)/shard_map/ppermute | solution.py:430
  9.4 11.7 %collective-permute-start.1 = (bf16[2,14,16,128]{3,2,1,0:T(8,128)(2,1)S(1)}, bf16[2,14,16,128]{3,2,1,0:T(8,128)(2,1)S(1)}, u32[]{:S(2)}, u32[]{:S(2)}) collective-permute-start(bf16[2,14,16,128]{3,2,1,0:T(8,128)(2,1)S(1)} %get-tuple-element.27.refs_0_), channel_id=1, source_target_pairs={{0,2},{1,3},{2,0},{3,1},{4,6},{5,7},{6,4},{7,5},{8,10},{9,11},{10,... | collective-permute-start | bytes 344072 | tf_op jit(solution)/shard_map/ppermute | solution.py:69
  12.2 8.8 %collective-permute-start.2 = (bf16[2,3,2,2,16,128]{5,4,3,2,1,0:T(8,128)(2,1)S(1)}, bf16[2,3,2,2,16,128]{5,4,3,2,1,0:T(8,128)(2,1)S(1)}, u32[]{:S(2)}, u32[]{:S(2)}) collective-permute-start(bf16[2,3,2,2,16,128]{5,4,3,2,1,0:T(8,128)(2,1)S(1)} %get-tuple-element.29.near), channel_id=1, source_target_pairs={{0,1},{1,2},{2,3},{3,4},{4,5},{5,6},{6,7},{7,0},{8,9},{9,10},{10,1... | collective-permute-start | bytes 294920 | tf_op jit(solution)/shard_map/ppermute | solution.py:430
  12.5 8.5 %collective-permute-start.3 = (bf16[2,3,2,2,16,128]{5,4,3,2,1,0:T(8,128)(2,1)S(1)}, bf16[2,3,2,2,16,128]{5,4,3,2,1,0:T(8,128)(2,1)S(1)}, u32[]{:S(2)}, u32[]{:S(2)}) collective-permute-start(bf16[2,3,2,2,16,128]{5,4,3,2,1,0:T(8,128)(2,1)S(1)} %get-tuple-element.28.far), channel_id=1, source_target_pairs={{0,7},{1,0},{2,1},{3,2},{4,3},{5,4},{6,5},{7,6},{8,15},{9,8},{10,9... | collective-permute-start | bytes 294920 | tf_op jit(solution)/shard_map/ppermute | solution.py:430
  15.8 1.0 %copy-start = (bf16[27,64,64]{2,1,0:T(8,128)(2,1)S(1)}, bf16[27,64,64]{2,1,0:T(8,128)(2,1)}, u32[]{:S(2)}) copy-start(bf16[27,64,64]{2,1,0:T(8,128)(2,1)} %first_hbm) | copy-start | bytes 663556
  16.8 1.0 %copy-start.1 = (bf16[27,64,64]{2,1,0:T(8,128)(2,1)S(1)}, bf16[27,64,64]{2,1,0:T(8,128)(2,1)}, u32[]{:S(2)}) copy-start(bf16[27,64,64]{2,1,0:T(8,128)(2,1)} %second_hbm) | copy-start | bytes 663556
  17.8 1.0 %copy-start.2 = (bf16[27,128,64]{1,2,0:T(8,128)(2,1)S(1)}, bf16[27,128,64]{1,2,0:T(8,128)(2,1)}, u32[]{:S(2)}) copy-start(bf16[27,128,64]{1,2,0:T(8,128)(2,1)} %param.16) | copy-start | bytes 1327108
  20.9 11.1 %copy-start.9 = (s32[2,27]{1,0:T(2,128)S(1)}, s32[2,27]{1,0:T(2,128)}, u32[]{:S(2)}) copy-start(s32[2,27]{1,0:T(2,128)} %neighbour_ref.2) | copy-start | bytes 652
  21.0 9.1 %collective-permute-start.4 = (bf16[4,14,16,128]{3,2,1,0:T(8,128)(2,1)S(1)}, bf16[4,14,16,128]{3,2,1,0:T(8,128)(2,1)S(1)}, u32[]{:S(2)}, u32[]{:S(2)}) collective-permute-start(bf16[4,14,16,128]{3,2,1,0:T(8,128)(2,1)S(1)} %shard_map.114.refs_0_), channel_id=1, source_target_pairs={{0,1},{1,0},{2,3},{3,2},{4,5},{5,4},{6,7},{7,6},{8,9},{9,8},{10,11... | collective-permute-start | bytes 688136 | tf_op jit(solution)/shard_map/ppermute | solution.py:69
  22.4 5.3 %collective-permute-start.5 = (bf16[4,3,2,2,16,128]{5,4,3,2,1,0:T(8,128)(2,1)S(1)}, bf16[4,3,2,2,16,128]{5,4,3,2,1,0:T(8,128)(2,1)S(1)}, u32[]{:S(2)}, u32[]{:S(2)}) collective-permute-start(bf16[4,3,2,2,16,128]{5,4,3,2,1,0:T(8,128)(2,1)S(1)} %get-tuple-element.37), channel_id=1, source_target_pairs={{0,16},{1,17},{2,18},{3,19},{4,20},{5,21},{6,22},{7,23},{8,24},{9,... | collective-permute-start | bytes 589832 | tf_op jit(solution)/shard_map/ppermute | solution.py:430
  25.1 5.1 %collective-permute-start.6 = (bf16[4,3,2,2,16,128]{5,4,3,2,1,0:T(8,128)(2,1)S(1)}, bf16[4,3,2,2,16,128]{5,4,3,2,1,0:T(8,128)(2,1)S(1)}, u32[]{:S(2)}, u32[]{:S(2)}) collective-permute-start(bf16[4,3,2,2,16,128]{5,4,3,2,1,0:T(8,128)(2,1)S(1)} %get-tuple-element.35), channel_id=1, source_target_pairs={{0,112},{1,113},{2,114},{3,115},{4,116},{5,117},{6,118},{7,119},{8... | collective-permute-start | bytes 589832 | tf_op jit(solution)/shard_map/ppermute | solution.py:430
  30.2 9.0 %collective-permute-start.12 = (bf16[8,14,16,128]{3,2,1,0:T(8,128)(2,1)S(1)}, bf16[8,14,16,128]{3,2,1,0:T(8,128)(2,1)S(1)}, u32[]{:S(2)}, u32[]{:S(2)}) collective-permute-start(bf16[8,14,16,128]{3,2,1,0:T(8,128)(2,1)S(1)} %shard_map.115.mine_a), channel_id=1, source_target_pairs={{0,4},{1,5},{2,6},{3,7},{4,0},{5,1},{6,2},{7,3},{8,12},{9,13},{10,... | collective-permute-start | bytes 1376264 | tf_op jit(solution)/shard_map/ppermute | solution.py:69
  32.0 23.3 %collective-permute-start.13 = (bf16[8,14,16,128]{3,2,1,0:T(8,128)(2,1)S(1)}, bf16[8,14,16,128]{3,2,1,0:T(8,128)(2,1)S(1)}, u32[]{:S(2)}, u32[]{:S(2)}) collective-permute-start(bf16[8,14,16,128]{3,2,1,0:T(8,128)(2,1)S(1)} %shard_map.115.mine_a), channel_id=1, source_target_pairs={{0,16},{1,17},{2,18},{3,19},{4,20},{5,21},{6,22},{7,23},{8,24},{9,... | collective-permute-start | bytes 1376264 | tf_op jit(solution)/shard_map/ppermute | solution.py:69
  32.0 23.3 %copy-start.3 = (f32[2,432,27]{2,1,0:T(8,128)S(1)}, f32[2,432,27]{2,1,0:T(8,128)}, u32[]{:S(2)}) copy-start(f32[2,432,27]{2,1,0:T(8,128)} %constant.4.clone.taps_ref) | copy-start | bytes 279940
  32.0 23.3 %copy-start.4 = (f32[432,1]{1,0:T(8,128)S(1)}, f32[432,1]{1,0:T(8,128)}, u32[]{:S(2)}) copy-start(f32[432,1]{1,0:T(8,128)} %constant.5.clone.voxel_ref) | copy-start | bytes 5188
  32.0 23.4 %copy-start.7 = (bf16[64,128]{1,0:T(8,128)(2,1)S(1)}, bf16[64,128]{1,0:T(8,128)(2,1)}, u32[]{:S(2)}) copy-start(bf16[64,128]{1,0:T(8,128)(2,1)} %w_output.1) | copy-start | bytes 49156
  39.2 16.1 %collective-permute-start.14 = (bf16[8,14,16,128]{3,2,1,0:T(8,128)(2,1)S(1)}, bf16[8,14,16,128]{3,2,1,0:T(8,128)(2,1)S(1)}, u32[]{:S(2)}, u32[]{:S(2)}) collective-permute-start(bf16[8,14,16,128]{3,2,1,0:T(8,128)(2,1)S(1)} %collective-permute-done.12.mine_b), channel_id=1, source_target_pairs={{0,16},{1,17},{2,18},{3,19},{4,20},{5,21},{6,22},{7,23},{8,24},{9,... | collective-permute-start | bytes 1376264 | tf_op jit(solution)/shard_map/ppermute | solution.py:69
  39.8 4.0 %collective-permute-start.7 = (bf16[16,128]{1,0:T(8,128)(2,1)S(1)}, bf16[16,128]{1,0:T(8,128)(2,1)S(1)}, u32[]{:S(2)}, u32[]{:S(2)}) collective-permute-start(bf16[16,128]{1,0:T(8,128)(2,1)S(1)} %get-tuple-element.42), channel_id=1, source_target_pairs={{0,8},{1,9},{2,10},{3,11},{4,12},{5,13},{6,14},{7,15},{8,0},{9,1},... | collective-permute-start | bytes 12296 | tf_op jit(solution)/shard_map/ppermute | solution.py:430
  43.8 2.5 %collective-permute-start.9 = (bf16[2,16,128]{2,1,0:T(8,128)(2,1)S(1)}, bf16[2,16,128]{2,1,0:T(8,128)(2,1)S(1)}, u32[]{:S(2)}, u32[]{:S(2)}) collective-permute-start(bf16[2,16,128]{2,1,0:T(8,128)(2,1)S(1)} %shard_map.117.refs_0_), channel_id=1, source_target_pairs={{0,7},{1,0},{2,1},{3,2},{4,3},{5,4},{6,5},{7,6},{8,15},{9,8},{10,9... | collective-permute-start | bytes 24584 | tf_op jit(solution)/shard_map/ppermute | solution.py:430
  45.0 4.6 %collective-permute-start.8 = (bf16[2,16,128]{2,1,0:T(8,128)(2,1)S(1)}, bf16[2,16,128]{2,1,0:T(8,128)(2,1)S(1)}, u32[]{:S(2)}, u32[]{:S(2)}) collective-permute-start(bf16[2,16,128]{2,1,0:T(8,128)(2,1)S(1)} %shard_map.117.refs_0_), channel_id=1, source_target_pairs={{0,1},{1,2},{2,3},{3,4},{4,5},{5,6},{6,7},{7,0},{8,9},{9,10},{10,1... | collective-permute-start | bytes 24584 | tf_op jit(solution)/shard_map/ppermute | solution.py:430
  49.6 5.7 %collective-permute-start.11 = (bf16[6,16,128]{2,1,0:T(8,128)(2,1)S(1)}, bf16[6,16,128]{2,1,0:T(8,128)(2,1)S(1)}, u32[]{:S(2)}, u32[]{:S(2)}) collective-permute-start(bf16[6,16,128]{2,1,0:T(8,128)(2,1)S(1)} %shard_map.118.own), channel_id=1, source_target_pairs={{0,112},{1,113},{2,114},{3,115},{4,116},{5,117},{6,118},{7,119},{8... | collective-permute-start | bytes 73736 | tf_op jit(solution)/shard_map/ppermute | solution.py:430
  52.3 3.0 %collective-permute-start.10 = (bf16[6,16,128]{2,1,0:T(8,128)(2,1)S(1)}, bf16[6,16,128]{2,1,0:T(8,128)(2,1)S(1)}, u32[]{:S(2)}, u32[]{:S(2)}) collective-permute-start(bf16[6,16,128]{2,1,0:T(8,128)(2,1)S(1)} %shard_map.118.own), channel_id=1, source_target_pairs={{0,16},{1,17},{2,18},{3,19},{4,20},{5,21},{6,22},{7,23},{8,24},{9,... | collective-permute-start | bytes 73736 | tf_op jit(solution)/shard_map/ppermute | solution.py:430

commit v3 on v2

v3 whole, which is shorter than its diff:
```python
import functools

import jax
import jax.numpy as jnp
import numpy as np
from jax import lax
from jax.experimental import pallas as pl
from jax.experimental.pallas import tpu as pltpu
from jax.sharding import PartitionSpec as P

AXES = ("grp", "ch")
BF = jnp.bfloat16
F32 = jnp.float32
VMEM = pl.BlockSpec(memory_space=pltpu.VMEM)
SMEM = pl.BlockSpec(memory_space=pltpu.SMEM)
ANY = pl.BlockSpec(memory_space=pl.ANY)
HBM = pl.BlockSpec(memory_space=pltpu.HBM)


def params(mebibytes):
    return pltpu.CompilerParams(vmem_limit_bytes=mebibytes * 2**20)


def cost(microseconds):
    return pl.CostEstimate(flops=int(microseconds * 1.15e9), bytes_accessed=0, transcendentals=0)

ATOM = (2, 16, 128)
ABSENT = 96


OFFSETS = [(x, y, z) for x in (-1, 0, 1) for y in (-1, 0, 1) for z in (-1, 0, 1)]
STEP = (-1, 0, 0, 1)
HALF = (1, 0, 1, 0)


def tap_table():
    chosen = np.zeros((2, 432, 27), np.float32)
    voxel = np.zeros((432, 1), np.float32)
    for t in range(27):
        for r in range(16):
            y, b, z, x = r // 8, r // 4 % 2, r // 2 % 2, r % 2
            x, y, z = x + t // 9, y + t // 3 % 3, z + t % 3
            chosen[b, t * 16 + r, 9 * STEP[x] + 3 * STEP[y] + STEP[z] + 13] = 1
            voxel[t * 16 + r] = HALF[y] * 8 + HALF[z] * 2 + HALF[x]
    return chosen, voxel


def position():
    m = lax.axis_index("ch")
    g = lax.axis_index("grp")
    return g, m >> 3, m & 7, g & 1


def permuted(value, along_g, along_h, along_j, sizes):
    groups, members = sizes
    tiles = members // 2
    pairs = []
    for g in range(groups):
        for m in range(members):
            to = along_h(m // tiles) * tiles + along_j(m % tiles, tiles)
            pairs.append((g * members + m, along_g(g, groups) * members + to))
    return lax.ppermute(value, AXES, pairs)


def stay(i, n=0):
    return i


def flip(i, n=0):
    return i ^ 1


def flop(i, n):
    return (((i + 1) ^ 1) - 1) % n


def after(value, *others):
    return lax.optimization_barrier((value, *others))[0]


def gelu(v):
    return jax.nn.gelu(v, approximate=True)


def halves(axis_size_lanes):
    return lax.broadcasted_iota(jnp.int32, (1, axis_size_lanes), 1) < 64


def dot(a, b):
    return jnp.dot(a, b, preferred_element_type=F32)


def started(sources, targets, sems):
    copies = [
        pltpu.make_async_copy(source, target, sems.at[n])
        for n, (source, target) in enumerate(zip(sources, targets))
    ]
    for copy in copies:
        copy.start()
    return copies


def in_hbm(value):
    return pltpu.with_memory_space_constraint(value, pltpu.HBM)


def pack_kernel(
    features_hbm, w_coarse_hbm, w_project_hbm, atoms_ref, packet_ref,
    features_ref, w_coarse_ref, w_project_ref, turned, sems,
):
    copies = started(
        (features_hbm, w_coarse_hbm, w_project_hbm),
        (features_ref, w_coarse_ref, w_project_ref),
        sems,
    )
    copies[0].wait()
    h = position()[1]
    low = halves(128)
    upper = lax.broadcasted_iota(jnp.int32, (1, 8, 1), 1) < 4
    turned[...] = features_ref[...].astype(F32).reshape(128, 512).T
    for pair in range(4):
        even = turned[pl.ds(2 * pair, 64, stride=8), :]
        odd = turned[pl.ds(2 * pair + 1, 64, stride=8), :]
        first = jnp.where(low, even, pltpu.roll(odd, 64, 1))
        second = jnp.where(low, pltpu.roll(even, 64, 1), odd)
        for b, rows in enumerate((first, second)):
            rows = rows.reshape(4, 2, 8, 128)
            a, c = rows[:, 0], rows[:, 1]
            near = jnp.where(upper, a, pltpu.roll(c, 4, 1))
            far = jnp.where(upper, pltpu.roll(a, 4, 1), c)
            for yh, part in enumerate((near, far)):
                part = part.reshape(2, 16, 128).astype(BF)
                for xh in range(2):
                    atoms_ref[pair // 2, yh, xh, b, pair % 2] = part[xh]
                tile = ((pair // 2 * 2 + yh) * 2 + b) * 2 + pair % 2
                packet_ref[tile] = jnp.where(h == 0, part[1], part[0])


    for copy in copies[1:]:
        copy.wait()
    core = position()[3]

    @pl.when(core == 0)
    def _():
        packet_ref[16:30] = w_coarse_ref[0:14]

    @pl.when(core == 1)
    def _():
        packet_ref[16:29] = w_coarse_ref[14:27]
        project = w_project_ref[...].astype(F32)
        packet_ref[29] = jnp.concatenate([project, jnp.zeros_like(project)], axis=1).astype(BF)


def merge_kernel(atoms_ref, packet_ref, got_ref, flip_ref, flop_ref):
    j = position()[2]
    upper = 1 - (j & 1)
    for yh, out in ((upper, flip_ref), (1 - upper, flop_ref)):
        for zh in range(2):
            out[zh * 12 : zh * 12 + 8] = atoms_ref[zh, yh].reshape(8, 16, 128)
            out[zh * 12 + 8 : zh * 12 + 12] = got_ref[pl.ds((zh * 2 + yh) * 4, 4)]
        out[24:38] = packet_ref[16:30]
        out[38:52] = got_ref[16:30]


def widen_kernel(
    first_hbm, second_hbm, middle_hbm, _, w1_ref, w2_ref, w3_ref, first_ref, second_ref, middle_ref, sems
):
    copies = started(
        (first_hbm, second_hbm, middle_hbm), (first_ref, second_ref, middle_ref), sems
    )
    for copy in copies:
        copy.wait()
    zero = jnp.zeros((64, 64), F32)
    for weight_ref, out_ref in ((first_ref, w1_ref), (second_ref, w2_ref)):
        for tx in range(3):
            for ty in range(3):
                w = [weight_ref[9 * tx + 3 * ty + tz].astype(F32) for tz in range(3)]
                for pair, blocks in enumerate(
                    (((w[0], w[1]), (zero, w[0])), ((w[2], zero), (w[1], w[2])))
                ):
                    wide = jnp.concatenate([jnp.concatenate(p, axis=1) for p in blocks], axis=0)
                    row = tx * 256 + pair * 128
                    out_ref[row : row + 128, ty * 128 : ty * 128 + 128] = wide.T.astype(BF)
    w3_ref[...] = jnp.zeros_like(w3_ref)
    for tx in range(3):
        for ty in range(3):
            for tz in range(3):
                for zo in range(2):
                    row = tx * 256 + (tz + zo) * 64
                    column = (ty * 2 + zo) * 128
                    w3_ref[row : row + 64, column : column + 128] = middle_ref[
                        9 * tx + 3 * ty + tz
                    ]


def join_kernel(*refs):
    *sources, out = refs
    row = 0
    for source in sources:
        out[row : row + source.shape[0]] = source[...]
        row += source.shape[0]


def joined(*arrays):
    rows = sum(a.shape[0] for a in arrays)
    return pl.pallas_call(
        join_kernel,
        out_shape=shape((rows,) + arrays[0].shape[1:]),
        in_specs=[VMEM] * len(arrays),
        out_specs=VMEM,
        cost_estimate=cost(0.05),
        compiler_params=params(8),
    )(*arrays)


def stack_kernel(own_flip, own_flop, got_flip, got_flop, flip_ref, flop_ref):
    core = position()[3]
    for zh, out in ((1 - core, flip_ref), (core, flop_ref)):
        for n, source in enumerate((own_flip, own_flop, got_flip, got_flop)):
            out[n * 12 : n * 12 + 12] = source[pl.ds(zh * 12, 12)]


def gather_kernel(own_ref, got_flip, got_flop, three_ref, two_ref):
    j = position()[2]
    three_ref[0:28] = got_flip[24:52]
    three_ref[28:56] = own_ref[24:52]
    three_ref[56:84] = got_flop[24:52]
    two_ref[28:56] = own_ref[24:52]

    @pl.when((j & 1) == 1)
    def _():
        two_ref[0:28] = got_flip[24:52]

    @pl.when((j & 1) == 0)
    def _():
        two_ref[0:28] = got_flop[24:52]


def leaf_conv(source, b, k, n, length, weight_ref):
    rows = n * length * 16
    parts = [
        source[b, k + dk : k + dk + n, dx : dx + length].reshape(rows, 128)
        for dx in range(3)
        for dk in range(2)
    ]
    wide = dot(jnp.concatenate(parts, axis=1), weight_ref[...])
    return (
        wide[:, 128:256]
        + pltpu.roll(wide[:, :128], 1, 0)
        + pltpu.roll(wide[:, 256:], rows - 1, 0)
    )


def atom_rows(neighbour_ref, z_halves):
    g, h, j, _ = position()
    rows = {}
    for b in range(2):
        for n, (dx, dy, dz) in enumerate(OFFSETS):
            if dz not in [STEP[z] for z in z_halves]:
                continue
            entry = neighbour_ref[b, n]
            apart_g = (entry >> 5) ^ g
            apart_j = ((entry >> 1) & 7) ^ j
            other = ((entry >> 4) & 1) != h
            of_z = jnp.where(apart_g == 1, 48, 72)
            of_y = jnp.where(apart_j == 1, 12, 18)
            own_y = ((1 - (j & 1)) * 6, (j & 1) * 6)
            for z in z_halves:
                for x in range(4):
                    for y in range(4):
                        if (STEP[x], STEP[y], STEP[z]) == (dx, dy, dz):
                            row = entry & 1
                            row += jnp.where(apart_g == 0, HALF[z] * 24, of_z) if dz else HALF[z] * 24
                            row += jnp.where(apart_j == 0, own_y[HALF[y]], of_y) if dy else own_y[HALF[y]]
                            row += jnp.where(other, 4, HALF[x] * 2) if dx else HALF[x] * 2
                            rows[b, z, x, y] = jnp.where(entry >= 0, row, ABSENT)
    return rows


def mask_tile(neighbour_ref, b, dx, dz):
    p = [
        (neighbour_ref[b, 9 * dx + 3 * dy + dz] >= 0).astype(F32) for dy in range(3)
    ]
    y_row = lax.broadcasted_iota(jnp.int32, (16, 128), 0)
    return jnp.where(y_row < 4, p[0], jnp.where(y_row < 12, p[1], p[2]))


def assemble(table, rows, b, z, wide, at, first_pair):
    upper = lax.broadcasted_iota(jnp.int32, (1, 1, 8, 1), 2) < 4
    for x in range(4):
        a = [
            table[pl.ds(rows[b, z, x, y] * 2, 2)].astype(F32).reshape(2, 2, 8, 128)
            for y in range(4)
        ]
        r = [pltpu.roll(v.reshape(4, 8, 128), 4, 1).reshape(2, 2, 8, 128) for v in a]
        even = jnp.concatenate(
            [jnp.where(upper, a[0], r[1]), jnp.where(upper, a[2], r[3])], axis=2
        ).astype(BF)
        odd = jnp.concatenate(
            [jnp.where(upper, r[0], a[1]), jnp.where(upper, r[2], a[3])], axis=2
        ).astype(BF)
        for pair in range(2):
            for k in range(2):
                wide[at, first_pair + pair, 4 * x + 2 * k] = even[pair, k]
                wide[at, first_pair + pair, 4 * x + 2 * k + 1] = odd[pair, k]


def over_x(value, mask, edge):
    value = value.reshape(8 + 2 * edge, 16, 128)
    return jnp.concatenate(
        [
            value[:edge] * mask[0][None],
            value[edge : edge + 8] * mask[1][None],
            value[edge + 8 :] * mask[2][None],
        ],
        axis=0,
    )


def own_copies(facing_flip, facing_flop, table, sems):
    core = position()[3]
    return started(
        (facing_flip, facing_flop),
        (table.at[pl.ds((1 - core) * 48, 48)], table.at[pl.ds(core * 48, 48)]),
        sems,
    )


def early_kernel(neighbour_ref, facing_flip, facing_flop, w1, wide, first, table, sems):
    copies = own_copies(facing_flip, facing_flop, table, sems)
    rows = atom_rows(neighbour_ref, (1, 2))
    table[2 * ABSENT : 2 * ABSENT + 2] = jnp.zeros(ATOM, BF)
    for copy in copies:
        copy.wait()
    for b in range(2):
        for z in (1, 2):
            assemble(table, rows, b, z, wide, b, 2 * z - 2)
    for b in range(2):
        mask = [mask_tile(neighbour_ref, b, dx, 1) for dx in range(3)]
        value = gelu(leaf_conv(wide, b, 0, 3, 14, w1)).reshape(3, 14 * 16, 128)
        for i in range(3):
            first[b, i] = over_x(value[i], mask, 3).astype(BF)


def main_kernel(
    neighbour_ref, facing_flip, facing_flop, beside_flip, beside_flop, wide_mid, first_mid,
    w1, w2, w3,
    skip_ref, coarse_ref,
    table, wide, first, second, masks, rows_a, middle_in, rows_b, turned, sems,
):
    copies = own_copies(facing_flip, facing_flop, table, sems)
    for n, source in enumerate((beside_flip, beside_flop)):
        copies.append(
            pltpu.make_async_copy(source, table.at[pl.ds(96 + n * 48, 48)], sems.at[2 + n])
        )
        copies[-1].start()
    table[2 * ABSENT : 2 * ABSENT + 2] = jnp.zeros(ATOM, BF)
    rows = atom_rows(neighbour_ref, (0, 3))

    low = halves(128)
    for b in range(2):
        for dx in range(3):
            of_z = [mask_tile(neighbour_ref, b, dx, dz) for dz in range(3)]
            masks[b, 0, dx] = of_z[0]
            masks[b, 1, dx] = jnp.where(low, of_z[0], of_z[1])
            masks[b, 2, dx] = of_z[1]
            masks[b, 3, dx] = jnp.where(low, of_z[1], of_z[2])
            masks[b, 4, dx] = of_z[2]
        first[b, 2:5] = first_mid[b]
        wide[2 * b, 2] = wide_mid[b, 0]
        wide[2 * b + 1, 0] = wide_mid[b, 3]

    for copy in copies:
        copy.wait()

    for b in range(2):
        assemble(table, rows, b, 0, wide, 2 * b, 0)
        assemble(table, rows, b, 3, wide, 2 * b + 1, 1)

    def masked(value, b, pattern, edge):
        return over_x(value, [masks[b, pattern, dx] for dx in range(3)], edge)

    for b in range(2):
        for side in range(2):
            value = gelu(leaf_conv(wide, 2 * b + side, 0, 2, 14, w1)).reshape(2, 14 * 16, 128)
            for i in range(2):
                pattern = ((0, 1), (3, 4))[side][i]
                first[b, 5 * side + i] = masked(value[i], b, pattern, 3).astype(BF)
    for b in range(2):
        for k, n in ((0, 2), (2, 2), (4, 2)):
            value = gelu(leaf_conv(first, b, k, n, 12, w2)).reshape(n, 12 * 16, 128)
            for i in range(n):
                pattern = (0, 2, 2, 2, 2, 4)[k + i]
                second[b, k + i] = masked(value[i], b, pattern, 2).astype(BF)

    for b in range(2):
        layers = []
        for k in range(6):
            v = second[b, k].astype(F32)
            v = (v.reshape(6, 2, 16, 128)[:, 0] + v.reshape(6, 2, 16, 128)[:, 1]).reshape(96, 128)
            v = v + pltpu.roll(v, 64, 1)
            rows_a[b, k] = v + pltpu.roll(v, 95, 0)
            layers.append((rows_a[b, k, pl.ds(0, 48, stride=2), :] * 0.125).astype(BF).astype(F32))
        for pair in range(3):
            middle_in[b, pair] = jnp.where(low, layers[2 * pair], layers[2 * pair + 1])

    operands = []
    for b in range(2):
        for k in range(2):
            operands.append(
                jnp.concatenate(
                    [
                        middle_in[b, k + dk, dx * 8 : dx * 8 + 32]
                        for dx in range(3)
                        for dk in range(2)
                    ],
                    axis=1,
                )
            )
    deep = dot(jnp.concatenate(operands, axis=0).astype(BF), w3[...])
    deep = (
        deep[:, 256:512] + pltpu.roll(deep[:, :256], 1, 0) + pltpu.roll(deep[:, 512:], 127, 0)
    )
    deep = gelu(deep).astype(BF).astype(F32)
    deep = (deep[:, :128] + deep[:, 128:]).reshape(8, 2, 8, 128)
    deep = (deep[:, 0] + deep[:, 1]).reshape(64, 128)
    rows_b[...] = deep + pltpu.roll(deep, 63, 0)
    coarse_ref[...] = (
        jnp.concatenate(
            [rows_b[pl.ds(2, 8, stride=8), :], rows_b[pl.ds(4, 8, stride=8), :]], axis=0
        )
        * 0.125
    ).astype(BF)

    for pair in range(4):
        v = [
            second[b, 1 + pair, 2:10].astype(F32)[:, 4:12, :].reshape(64, 128) for b in range(2)
        ]
        turned[pl.ds(2 * pair, 64, stride=8), :] = jnp.where(low, v[0], pltpu.roll(v[1], 64, 1))
        turned[pl.ds(2 * pair + 1, 64, stride=8), :] = jnp.where(
            low, pltpu.roll(v[0], 64, 1), v[1]
        )
    skip_ref[...] = turned[...].T.astype(BF).reshape(2, 64, 512)


def last_kernel(
    live_ref, neighbour_ref, taps_ref, voxel_ref, own, below, above, mine_a, mine_b, mine_c,
    theirs_a, theirs_b, theirs_c, w_output, skip_ref, out_ref, coarse_ref,
):
    g, h, j, core = position()
    entry = neighbour_ref[...]
    apart_g = (entry >> 5) ^ g
    apart_j = ((entry >> 1) & 7) ^ j
    code = (
        jnp.where(apart_g == 0, 0, jnp.where(apart_g == 1, 6, 12))
        + jnp.where(apart_j == 0, 0, jnp.where(apart_j == 1, 2, 4))
        + jnp.where(((entry >> 4) & 1) == h, 0, 1)
    ) * 16 + (entry & 1) * 4
    code = jnp.where(entry >= 0, code, -4096).astype(F32)
    rows = jnp.sum(taps_ref[0] * code[0:1] + taps_ref[1] * code[1:2], axis=1, keepdims=True)
    rows = (rows + voxel_ref[...]).astype(jnp.int32)
    tiles = jnp.concatenate([r[...].reshape(96, 128) for r in (own, below, above)], axis=0)
    chosen = (rows == lax.broadcasted_iota(jnp.int32, (432, 288), 1)).astype(F32).astype(BF)
    taps = dot(chosen, tiles).astype(BF)

    def weight(parts, t):
        chosen = [part[:, t % 14] for part in parts]
        return jnp.concatenate(chosen, axis=0).reshape(256, 128)

    def deepest(early, late):
        total = jnp.zeros((16, 256), F32)
        for t in range(27):
            total = total + lax.dot_general(
                taps[t * 16 : (t + 1) * 16],
                weight(early if t < 14 else late, t),
                (((1,), (1,)), ((), ())),
                preferred_element_type=F32,
            )
        coarse_ref[...] = dot(gelu(total).astype(BF), weight(late, 27))

    @pl.when(core == 0)
    def _():
        deepest((mine_a, mine_b, mine_c), (theirs_a, theirs_b, theirs_c))

    @pl.when(core == 1)
    def _():
        deepest((theirs_a, theirs_b, theirs_c), (mine_a, mine_b, mine_c))

    coarse = coarse_ref[...].astype(BF).astype(F32).T[:64].astype(BF)
    row = lax.broadcasted_iota(jnp.int32, (16, 512), 0)
    voxel = lax.broadcasted_iota(jnp.int32, (16, 512), 1)
    place = ((voxel >> 5) & 1) * 8 + ((voxel >> 2) & 1) * 2 + ((voxel >> 8) & 1)
    for b in range(2):
        spread = (row == place + b * 4).astype(F32).astype(BF)
        widened = dot(coarse, spread).astype(BF)
        mixed = dot(w_output[...], jnp.concatenate([skip_ref[b], widened], axis=0))
        mixed = jnp.where(b < live_ref[0], mixed, 0.0)
        out_ref[b] = mixed.astype(BF)


def shape(dims, kind=BF):
    return jax.ShapeDtypeStruct(dims, kind)


def shards(
    features, live_counts, neighbours, w_first, w_second, w_middle, w_coarse, w_project, w_output
):
    sizes = (lax.axis_size("grp"), lax.axis_size("ch"))

    def to_x(value):
        return permuted(value, stay, flip, stay, sizes)

    def to_y(value, along):
        return permuted(value, stay, stay, along, sizes)

    def to_z(value, along):
        return permuted(value, along, stay, stay, sizes)

    atoms, packet = pl.pallas_call(
        pack_kernel,
        out_shape=(shape((2, 2, 2, 2) + ATOM), shape((30, 16, 128))),
        in_specs=[HBM] * 3,
        out_specs=(VMEM, VMEM),
        scratch_shapes=[
            pltpu.VMEM((2, 64, 512), BF),
            pltpu.VMEM((27, 16, 128), BF),
            pltpu.VMEM((16, 64), BF),
            pltpu.VMEM((512, 128), F32),
            pltpu.SemaphoreType.DMA((3,)),
        ],
        cost_estimate=cost(1),
        compiler_params=params(8),
    )(in_hbm(features), in_hbm(w_coarse), in_hbm(w_project))
    own_flip, own_flop = pl.pallas_call(
        merge_kernel,
        out_shape=(shape((52, 16, 128)),) * 2,
        in_specs=[VMEM] * 3,
        out_specs=(VMEM,) * 2,
        cost_estimate=cost(0.1),
        compiler_params=params(8),
    )(atoms, packet, to_x(packet))
    w1, w2, w3 = pl.pallas_call(
        widen_kernel,
        out_shape=(shape((768, 384)), shape((768, 384)), shape((768, 768))),
        in_specs=[HBM] * 3 + [ANY],
        out_specs=(VMEM,) * 3,
        scratch_shapes=[
            pltpu.VMEM((27, 64, 64), BF),
            pltpu.VMEM((27, 64, 64), BF),
            pltpu.VMEM((27, 64, 128), BF),
            pltpu.SemaphoreType.DMA((3,)),
        ],
        cost_estimate=cost(2.5),
        compiler_params=params(8),
    )(in_hbm(w_first), in_hbm(w_second), in_hbm(jnp.swapaxes(w_middle, 1, 2)), own_flip)
    got_flip, got_flop = to_y(own_flip, flip), to_y(own_flop, flop)
    facing_flip, facing_flop = pl.pallas_call(
        stack_kernel,
        out_shape=(shape((48, 16, 128)),) * 2,
        in_specs=[VMEM] * 4,
        out_specs=(VMEM,) * 2,
        cost_estimate=cost(0.05),
        compiler_params=params(8),
    )(own_flip, own_flop, after(got_flip, w1), got_flop)
    beside_flip, beside_flop = to_z(facing_flip, flip), to_z(facing_flop, flop)
    wide_mid, first_mid = pl.pallas_call(
        early_kernel,
        out_shape=(shape((2, 4, 16, 16, 128)), shape((2, 3, 14, 16, 128))),
        in_specs=[SMEM, ANY, ANY, VMEM],
        out_specs=(VMEM,) * 2,
        scratch_shapes=[pltpu.VMEM((194, 16, 128), BF), pltpu.SemaphoreType.DMA((2,))],
        cost_estimate=cost(2.6),
        compiler_params=params(14),
    )(neighbours, facing_flip, facing_flop, w1)
    three, two = pl.pallas_call(
        gather_kernel,
        out_shape=(shape((84, 16, 128)), shape((56, 16, 128))),
        in_specs=[VMEM] * 3,
        out_specs=(VMEM,) * 2,
        cost_estimate=cost(0.05),
        compiler_params=params(8),
    )(own_flip, after(got_flip, wide_mid), got_flop)
    mine = (
        three,
        to_y(three, lambda j, n: (j + 3) % n),
        to_y(two, lambda j, n: (j - 3) % n),
    )

    skip, coarse = pl.pallas_call(
        main_kernel,
        out_shape=(shape((2, 64, 512)), shape((16, 128))),
        in_specs=[SMEM] + [ANY] * 4 + [VMEM] * 5,
        out_specs=(VMEM, VMEM),
        scratch_shapes=[
            pltpu.VMEM((194, 16, 128), BF),
            pltpu.VMEM((4, 3, 16, 16, 128), BF),
            pltpu.VMEM((2, 7, 14, 16, 128), BF),
            pltpu.VMEM((2, 6, 12, 16, 128), BF),
            pltpu.VMEM((2, 5, 3, 16, 128), F32),
            pltpu.VMEM((2, 6, 96, 128), F32),
            pltpu.VMEM((2, 3, 48, 128), F32),
            pltpu.VMEM((64, 128), F32),
            pltpu.VMEM((512, 128), F32),
            pltpu.SemaphoreType.DMA((4,)),
        ],
        cost_estimate=cost(6),
        compiler_params=params(20),
    )(
        after(neighbours, three),
        facing_flip,
        facing_flop,
        beside_flip,
        beside_flop,
        wide_mid,
        first_mid,
        w1,
        w2,
        w3,
    )

    both = joined(coarse[None], to_x(coarse)[None])
    theirs = [to_z(after(part, both), flip) for part in mine]
    layer = joined(both, to_y(both, flip), to_y(both, flop))
    below, above = to_z(layer, flip), to_z(layer, flop)
    return pl.pallas_call(
        last_kernel,
        out_shape=shape((2, 64, 512)),
        in_specs=[SMEM] + [VMEM] * 14,
        out_specs=VMEM,
        scratch_shapes=[
            pltpu.VMEM((16, 128), F32),
        ],
        cost_estimate=cost(2.4),
        compiler_params=params(8),
    )(
        live_counts,
        neighbours,
        *(jnp.asarray(a) for a in tap_table()),
        layer,
        below,
        above,
        *(part.reshape(-1, 14, 16, 128) for part in (*mine, *theirs)),
        w_output,
        skip,
    )


def solution(mesh):
    return jax.shard_map(
        shards,
        mesh=mesh,
        in_specs=(
            P(AXES, None, None),
            P(AXES),
            P(AXES, None),
            P(),
            P(),
            P(),
            P(None, "ch", None),
            P("ch", None),
            P(),
        ),
        out_specs=P(AXES, None, None),
        check_vma=False,
    )
```

time: 58.5 us -> 53 us (0.906)
  local copies, waits for them, and re-layouts: 5.54 us -> 0.02 us
  waiting for transfers between devices: 14.2 us -> 10.2 us
  Pallas kernels: 12.1 us -> 14.8 us
  starting transfers between devices: 25.2 us -> 27.1 us
    unnamed x20 -> x8, local copies, waits for them, and re-layouts: 5.54 us -> 0.02 us
    ppermute x15, waiting for transfers between devices: 14.2 us -> 10.2 us  [permuted(): return lax.ppermute(value, AXES, pairs)]
    pallas_call x3 -> x4, Pallas kernels: 0.06 us -> 2.71 us  [the longest x1 2.58 us: shards(): pl.pallas_call(early_kernel, out_shape=(shape((2, 4, 16, 16, 128)), shape...]
    ppermute x15, starting transfers between devices: 25.2 us -> 27.1 us  [permuted(): return lax.ppermute(value, AXES, pairs)]
    pallas_call x1, Pallas kernels: 7.2 us -> 5.93 us  [shards(): pl.pallas_call(main_kernel, out_shape=(shape((2, 64, 512)), shape((16, 12...]
    pallas_call x1, Pallas kernels: 0.23 us -> 1.18 us  [shards(): pl.pallas_call(pack_kernel, out_shape=(shape((2, 2, 2, 2) + ATOM), shape(...]
  transfers between devices with their start and end apart: 15 -> 15, of which waited for: 7 -> 6; matrix products, arithmetic and copies ran while one was open for 0% -> 0% of each run, Pallas kernels for 16% -> 21%
where the time goes in v3:
time: 53 us; the launch traced here: 52.9 us
  starting transfers between devices  27.1 us (51%)
  Pallas kernels  14.8 us (28%)
  waiting for transfers between devices  10.2 us (19%)
  between operations  0.77 us (1%)
    ppermute x15, starting transfers between devices, permuted(): return lax.ppermute(value, AXES, pairs)  27.1 us
    ppermute x15, waiting for transfers between devices, permuted(): return lax.ppermute(value, AXES, pairs)  10.2 us
    pallas_call x1, Pallas kernels, shards(): pl.pallas_call(main_kernel, out_shape=(shape((2, 64, 512)), shape((16, 12...  5.93 us
    pallas_call x1, Pallas kernels, shards(): pl.pallas_call(early_kernel, out_shape=(shape((2, 4, 16, 16, 128)), shape...  2.58 us
    pallas_call x1, Pallas kernels, shards(): pl.pallas_call(widen_kernel, out_shape=(shape((768, 384)), shape((768, 38...  2.5 us
    pallas_call x1, Pallas kernels, shards(): pl.pallas_call(last_kernel, out_shape=shape((2, 64, 512)), in_specs=[SMEM...  2.46 us
    pallas_call x1, Pallas kernels, shards(): pl.pallas_call(pack_kernel, out_shape=(shape((2, 2, 2, 2) + ATOM), shape(...  1.18 us
  transfers between devices with their start and end apart: 15, of which 6 were waited for; matrix products, arithmetic and copies ran while one was open for 0% of the time, Pallas kernels for 21%

profile of v3, /device:TPU:1, one launch (start us, length us, event | category | flops | bytes accessed | tf_op | source)
XLA Modules:
  0.0 52.9 jit_solution(4932258669674408647)
XLA Ops:
  0.0 1.2 %shard_map.109 = (bf16[2,2,2,2,2,16,128]{6,5,4,3,2,1,0:T(8,128)(2,1)S(1)}, bf16[30,16,128]{2,1,0:T(8,128)(2,1)S(1)}) custom-call(bf16[2,64,512]{2,1,0:T(8,128)(2,1)} %features_hbm.1, bf16[27,16,128]{2,1,0:T(8,128)(2,1)} %w_coarse_hbm.1, bf16[16,64]{1,0:T(8,128)(2,1)} %w_project_hbm.1), custom_call_target="tpu_custom_call" | custom-call | flops 1150000000 | tf_op jit(solution)/shard_map/pallas_call | solution.py:519
  1.2 3.8 %collective-permute-start = (bf16[30,16,128]{2,1,0:T(8,128)(2,1)S(1)}, bf16[30,16,128]{2,1,0:T(8,128)(2,1)S(1)}, u32[]{:S(2)}, u32[]{:S(2)}) collective-permute-start(bf16[30,16,128]{2,1,0:T(8,128)(2,1)S(1)} %get-tuple-element.27.packet_ref), channel_id=1, source_target_pairs={{0,8},{1,9},{2,10},{3,11},{4,12},{5,13},{6,14},{7,15},{8,0},{9,1},... | collective-permute-start | bytes 368648 | tf_op jit(solution)/shard_map/ppermute | solution.py:62
  5.0 2.8 %collective-permute-done.got_ref = bf16[30,16,128]{2,1,0:T(8,128)(2,1)S(1)} collective-permute-done((bf16[30,16,128]{2,1,0:T(8,128)(2,1)S(1)}, bf16[30,16,128]{2,1,0:T(8,128)(2,1)S(1)}, u32[]{:S(2)}, u32[]{:S(2)}) %collective-permute-start) | collective-permute-done | bytes 122912 | tf_op jit(solution)/shard_map/ppermute | solution.py:62
  7.8 1.3 %collective-permute-start.1 = (bf16[52,16,128]{2,1,0:T(8,128)(2,1)S(1)}, bf16[52,16,128]{2,1,0:T(8,128)(2,1)S(1)}, u32[]{:S(2)}, u32[]{:S(2)}) collective-permute-start(bf16[52,16,128]{2,1,0:T(8,128)(2,1)S(1)} %get-tuple-element.28._.own_flip.own_ref), channel_id=1, source_target_pairs={{0,1},{1,0},{2,3},{3,2},{4,5},{5,4},{6,7},{7,6},{8,9},{9,8},{10,11... | collective-permute-start | bytes 638984 | tf_op jit(solution)/shard_map/ppermute | solution.py:62
  9.1 2.8 %collective-permute-start.2 = (bf16[52,16,128]{2,1,0:T(8,128)(2,1)S(1)}, bf16[52,16,128]{2,1,0:T(8,128)(2,1)S(1)}, u32[]{:S(2)}, u32[]{:S(2)}) collective-permute-start(bf16[52,16,128]{2,1,0:T(8,128)(2,1)S(1)} %get-tuple-element.29.own_flop), channel_id=1, source_target_pairs={{0,7},{1,2},{2,1},{3,4},{4,3},{5,6},{6,5},{7,0},{8,15},{9,10},{10,... | collective-permute-start | bytes 638984 | tf_op jit(solution)/shard_map/ppermute | solution.py:62
  12.0 2.5 %shard_map.111 = (bf16[768,384]{1,0:T(8,128)(2,1)S(1)}, bf16[768,384]{1,0:T(8,128)(2,1)S(1)}, bf16[768,768]{1,0:T(8,128)(2,1)S(1)}) custom-call(bf16[27,64,64]{2,1,0:T(8,128)(2,1)} %first_hbm.1, bf16[27,64,64]{2,1,0:T(8,128)(2,1)} %second_hbm.1, bf16[27,64,128]{2,1,0:T(8,128)(2,1)} %bitcast.17, bf16[52,16,128]{2,1,0:T(8,128)(2,1)S(1)} %get-tuple-element.28._.own_flip.own_ref), custom_call_target="tpu_custom_call" | custom-call | flops 2875000064 | tf_op jit(solution)/shard_map/pallas_call | solution.py:542
  14.5 0.0 collective-permute-done.1.got_flip
  14.5 1.5 %collective-permute-done.2.got_flop = bf16[52,16,128]{2,1,0:T(8,128)(2,1)S(1)} collective-permute-done((bf16[52,16,128]{2,1,0:T(8,128)(2,1)S(1)}, bf16[52,16,128]{2,1,0:T(8,128)(2,1)S(1)}, u32[]{:S(2)}, u32[]{:S(2)}) %collective-permute-start.2) | collective-permute-done | bytes 213024 | tf_op jit(solution)/shard_map/ppermute | solution.py:62
  16.0 3.1 %collective-permute-start.3 = (bf16[48,16,128]{2,1,0:T(8,128)(2,1)S(1)}, bf16[48,16,128]{2,1,0:T(8,128)(2,1)S(1)}, u32[]{:S(2)}, u32[]{:S(2)}) collective-permute-start(bf16[48,16,128]{2,1,0:T(8,128)(2,1)S(1)} %get-tuple-element.32.facing_flip), channel_id=1, source_target_pairs={{0,16},{1,17},{2,18},{3,19},{4,20},{5,21},{6,22},{7,23},{8,24},{9,... | collective-permute-start | bytes 589832 | tf_op jit(solution)/shard_map/ppermute | solution.py:62
  19.0 1.6 %collective-permute-start.4 = (bf16[48,16,128]{2,1,0:T(8,128)(2,1)S(1)}, bf16[48,16,128]{2,1,0:T(8,128)(2,1)S(1)}, u32[]{:S(2)}, u32[]{:S(2)}) collective-permute-start(bf16[48,16,128]{2,1,0:T(8,128)(2,1)S(1)} %get-tuple-element.33.facing_flop), channel_id=1, source_target_pairs={{0,112},{1,113},{2,114},{3,115},{4,116},{5,117},{6,118},{7,119},{8... | collective-permute-start | bytes 589832 | tf_op jit(solution)/shard_map/ppermute | solution.py:62
  20.6 2.6 %shard_map.113 = (bf16[2,4,16,16,128]{4,3,2,1,0:T(8,128)(2,1)S(1)}, bf16[2,3,14,16,128]{4,3,2,1,0:T(8,128)(2,1)S(1)}) custom-call(s32[2,27]{1,0:T(2,128)S(1)} %copy-done.1, bf16[48,16,128]{2,1,0:T(8,128)(2,1)S(1)} %get-tuple-element.32.facing_flip, bf16[48,16,128]{2,1,0:T(8,128)(2,1)S(1)} %get-tuple-element.33.facing_flop, ...), custom_call_target="tpu_custom_call" | custom-call | flops 2990000128 | tf_op jit(solution)/shard_map/pallas_call | solution.py:566
  23.2 0.1 shard_map.114
  23.3 1.9 %collective-permute-start.10 = (bf16[84,16,128]{2,1,0:T(8,128)(2,1)S(1)}, bf16[84,16,128]{2,1,0:T(8,128)(2,1)S(1)}, u32[]{:S(2)}, u32[]{:S(2)}) collective-permute-start(bf16[84,16,128]{2,1,0:T(8,128)(2,1)S(1)} %get-tuple-element.43), channel_id=1, source_target_pairs={{0,3},{1,4},{2,5},{3,6},{4,7},{5,0},{6,1},{7,2},{8,11},{9,12},{10,... | collective-permute-start | bytes 1032200 | tf_op jit(solution)/shard_map/ppermute | solution.py:62
  25.2 0.5 %collective-permute-start.11 = (bf16[56,16,128]{2,1,0:T(8,128)(2,1)S(1)}, bf16[56,16,128]{2,1,0:T(8,128)(2,1)S(1)}, u32[]{:S(2)}, u32[]{:S(2)}) collective-permute-start(bf16[56,16,128]{2,1,0:T(8,128)(2,1)S(1)} %get-tuple-element.42), channel_id=1, source_target_pairs={{0,5},{1,6},{2,7},{3,0},{4,1},{5,2},{6,3},{7,4},{8,13},{9,14},{10,... | collective-permute-start | bytes 688136 | tf_op jit(solution)/shard_map/ppermute | solution.py:62
  25.7 0.0 collective-permute-done.3.beside_flip
  25.7 0.0 collective-permute-done.4.beside_flop
  25.7 0.0 copy-start.2
  25.8 0.0 copy-start.3
  25.8 5.9 %shard_map.115 = (bf16[2,64,512]{2,1,0:T(8,128)(2,1)S(1)}, bf16[16,128]{1,0:T(8,128)(2,1)S(1)}) custom-call(s32[2,27]{1,0:T(2,128)S(1)} %copy-done.1, bf16[48,16,128]{2,1,0:T(8,128)(2,1)S(1)} %get-tuple-element.32.facing_flip, bf16[48,16,128]{2,1,0:T(8,128)(2,1)S(1)} %get-tuple-element.33.facing_flop, ...), custom_call_target="tpu_custom_call" | custom-call | flops 6899999744 | tf_op jit(solution)/shard_map/pallas_call | solution.py:589
  31.7 3.0 %collective-permute-start.5 = (bf16[16,128]{1,0:T(8,128)(2,1)S(1)}, bf16[16,128]{1,0:T(8,128)(2,1)S(1)}, u32[]{:S(2)}, u32[]{:S(2)}) collective-permute-start(bf16[16,128]{1,0:T(8,128)(2,1)S(1)} %get-tuple-element.41), channel_id=1, source_target_pairs={{0,8},{1,9},{2,10},{3,11},{4,12},{5,13},{6,14},{7,15},{8,0},{9,1},... | collective-permute-start | bytes 12296 | tf_op jit(solution)/shard_map/ppermute | solution.py:62
  34.7 1.4 %collective-permute-done.5 = bf16[16,128]{1,0:T(8,128)(2,1)S(1)} collective-permute-done((bf16[16,128]{1,0:T(8,128)(2,1)S(1)}, bf16[16,128]{1,0:T(8,128)(2,1)S(1)}, u32[]{:S(2)}, u32[]{:S(2)}) %collective-permute-start.5) | collective-permute-done | bytes 4128 | tf_op jit(solution)/shard_map/ppermute | solution.py:62
  36.2 3.8 %collective-permute-start.12 = (bf16[84,16,128]{2,1,0:T(8,128)(2,1)S(1)}, bf16[84,16,128]{2,1,0:T(8,128)(2,1)S(1)}, u32[]{:S(2)}, u32[]{:S(2)}) collective-permute-start(bf16[84,16,128]{2,1,0:T(8,128)(2,1)S(1)} %get-tuple-element.43), channel_id=1, source_target_pairs={{0,16},{1,17},{2,18},{3,19},{4,20},{5,21},{6,22},{7,23},{8,24},{9,... | collective-permute-start | bytes 1032200 | tf_op jit(solution)/shard_map/ppermute | solution.py:62
  40.0 0.0 collective-permute-done.10
  40.0 0.1 collective-permute-start.13
  40.1 0.4 collective-permute-start.14
  40.5 0.2 collective-permute-start.6
  40.7 3.0 %collective-permute-start.7 = (bf16[2,16,128]{2,1,0:T(8,128)(2,1)S(1)}, bf16[2,16,128]{2,1,0:T(8,128)(2,1)S(1)}, u32[]{:S(2)}, u32[]{:S(2)}) collective-permute-start(bf16[2,16,128]{2,1,0:T(8,128)(2,1)S(1)} %shard_map.116.refs_0_), channel_id=1, source_target_pairs={{0,7},{1,2},{2,1},{3,4},{4,3},{5,6},{6,5},{7,0},{8,15},{9,10},{10,... | collective-permute-start | bytes 24584 | tf_op jit(solution)/shard_map/ppermute | solution.py:62
  43.7 1.7 %collective-permute-done.7.refs_2_ = bf16[2,16,128]{2,1,0:T(8,128)(2,1)S(1)} collective-permute-done((bf16[2,16,128]{2,1,0:T(8,128)(2,1)S(1)}, bf16[2,16,128]{2,1,0:T(8,128)(2,1)S(1)}, u32[]{:S(2)}, u32[]{:S(2)}) %collective-permute-start.7) | collective-permute-done | bytes 8224 | tf_op jit(solution)/shard_map/ppermute | solution.py:62
  45.3 1.5 %collective-permute-start.8 = (bf16[6,16,128]{2,1,0:T(8,128)(2,1)S(1)}, bf16[6,16,128]{2,1,0:T(8,128)(2,1)S(1)}, u32[]{:S(2)}, u32[]{:S(2)}) collective-permute-start(bf16[6,16,128]{2,1,0:T(8,128)(2,1)S(1)} %shard_map.117.own), channel_id=1, source_target_pairs={{0,16},{1,17},{2,18},{3,19},{4,20},{5,21},{6,22},{7,23},{8,24},{9,... | collective-permute-start | bytes 73736 | tf_op jit(solution)/shard_map/ppermute | solution.py:62
  47.5 0.2 collective-permute-done.8.below
  47.7 2.7 %collective-permute-done.9.above = bf16[6,16,128]{2,1,0:T(8,128)(2,1)S(1)} collective-permute-done((bf16[6,16,128]{2,1,0:T(8,128)(2,1)S(1)}, bf16[6,16,128]{2,1,0:T(8,128)(2,1)S(1)}, u32[]{:S(2)}, u32[]{:S(2)}) %collective-permute-start.9) | collective-permute-done | bytes 24608 | tf_op jit(solution)/shard_map/ppermute | solution.py:62
  50.4 2.5 %shard_map.118 = bf16[2,64,512]{2,1,0:T(8,128)(2,1)} custom-call(s32[1]{0:T(128)S(6)} %copy.12.live_ref, s32[2,27]{1,0:T(2,128)S(1)} %copy-done.1, f32[2,432,27]{2,1,0:T(8,128)S(1)} %copy-done.2, f32[432,1]{1,0:T(8,128)S(1)} %copy-done.3, bf16[6,16,128]{2,1,0:T(8,128)(2,1)S(1)} %shard_map.117.own, bf16[6,16,128]{2,1,0:T(8,128)(2,1)S(1)} %collective-permute-done.8.below, ...), custom_call_target="tpu_custom_call" | custom-call | flops 2760000000 | tf_op jit(solution)/shard_map/pallas_call | solution.py:625
  (16 shorter events, 0.1 us)
Async XLA Ops:
  1.2 6.6 %collective-permute-start = (bf16[30,16,128]{2,1,0:T(8,128)(2,1)S(1)}, bf16[30,16,128]{2,1,0:T(8,128)(2,1)S(1)}, u32[]{:S(2)}, u32[]{:S(2)}) collective-permute-start(bf16[30,16,128]{2,1,0:T(8,128)(2,1)S(1)} %get-tuple-element.27.packet_ref), channel_id=1, source_target_pairs={{0,8},{1,9},{2,10},{3,11},{4,12},{5,13},{6,14},{7,15},{8,0},{9,1},... | collective-permute-start | bytes 368648 | tf_op jit(solution)/shard_map/ppermute | solution.py:62
  7.8 6.6 %collective-permute-start.1 = (bf16[52,16,128]{2,1,0:T(8,128)(2,1)S(1)}, bf16[52,16,128]{2,1,0:T(8,128)(2,1)S(1)}, u32[]{:S(2)}, u32[]{:S(2)}) collective-permute-start(bf16[52,16,128]{2,1,0:T(8,128)(2,1)S(1)} %get-tuple-element.28._.own_flip.own_ref), channel_id=1, source_target_pairs={{0,1},{1,0},{2,3},{3,2},{4,5},{5,4},{6,7},{7,6},{8,9},{9,8},{10,11... | collective-permute-start | bytes 638984 | tf_op jit(solution)/shard_map/ppermute | solution.py:62
  9.1 6.8 %collective-permute-start.2 = (bf16[52,16,128]{2,1,0:T(8,128)(2,1)S(1)}, bf16[52,16,128]{2,1,0:T(8,128)(2,1)S(1)}, u32[]{:S(2)}, u32[]{:S(2)}) collective-permute-start(bf16[52,16,128]{2,1,0:T(8,128)(2,1)S(1)} %get-tuple-element.29.own_flop), channel_id=1, source_target_pairs={{0,7},{1,2},{2,1},{3,4},{4,3},{5,6},{6,5},{7,0},{8,15},{9,10},{10,... | collective-permute-start | bytes 638984 | tf_op jit(solution)/shard_map/ppermute | solution.py:62
  12.0 8.7 %copy-start.1 = (s32[2,27]{1,0:T(2,128)S(1)}, s32[2,27]{1,0:T(2,128)}, u32[]{:S(2)}) copy-start(s32[2,27]{1,0:T(2,128)} %neighbour_ref.4) | copy-start | bytes 652
  16.0 9.8 %collective-permute-start.3 = (bf16[48,16,128]{2,1,0:T(8,128)(2,1)S(1)}, bf16[48,16,128]{2,1,0:T(8,128)(2,1)S(1)}, u32[]{:S(2)}, u32[]{:S(2)}) collective-permute-start(bf16[48,16,128]{2,1,0:T(8,128)(2,1)S(1)} %get-tuple-element.32.facing_flip), channel_id=1, source_target_pairs={{0,16},{1,17},{2,18},{3,19},{4,20},{5,21},{6,22},{7,23},{8,24},{9,... | collective-permute-start | bytes 589832 | tf_op jit(solution)/shard_map/ppermute | solution.py:62
  19.0 6.7 %collective-permute-start.4 = (bf16[48,16,128]{2,1,0:T(8,128)(2,1)S(1)}, bf16[48,16,128]{2,1,0:T(8,128)(2,1)S(1)}, u32[]{:S(2)}, u32[]{:S(2)}) collective-permute-start(bf16[48,16,128]{2,1,0:T(8,128)(2,1)S(1)} %get-tuple-element.33.facing_flop), channel_id=1, source_target_pairs={{0,112},{1,113},{2,114},{3,115},{4,116},{5,117},{6,118},{7,119},{8... | collective-permute-start | bytes 589832 | tf_op jit(solution)/shard_map/ppermute | solution.py:62
  23.3 16.7 %collective-permute-start.10 = (bf16[84,16,128]{2,1,0:T(8,128)(2,1)S(1)}, bf16[84,16,128]{2,1,0:T(8,128)(2,1)S(1)}, u32[]{:S(2)}, u32[]{:S(2)}) collective-permute-start(bf16[84,16,128]{2,1,0:T(8,128)(2,1)S(1)} %get-tuple-element.43), channel_id=1, source_target_pairs={{0,3},{1,4},{2,5},{3,6},{4,7},{5,0},{6,1},{7,2},{8,11},{9,12},{10,... | collective-permute-start | bytes 1032200 | tf_op jit(solution)/shard_map/ppermute | solution.py:62
  25.2 14.9 %collective-permute-start.11 = (bf16[56,16,128]{2,1,0:T(8,128)(2,1)S(1)}, bf16[56,16,128]{2,1,0:T(8,128)(2,1)S(1)}, u32[]{:S(2)}, u32[]{:S(2)}) collective-permute-start(bf16[56,16,128]{2,1,0:T(8,128)(2,1)S(1)} %get-tuple-element.42), channel_id=1, source_target_pairs={{0,5},{1,6},{2,7},{3,0},{4,1},{5,2},{6,3},{7,4},{8,13},{9,14},{10,... | collective-permute-start | bytes 688136 | tf_op jit(solution)/shard_map/ppermute | solution.py:62
  25.7 24.7 %copy-start = (bf16[64,128]{1,0:T(8,128)(2,1)S(1)}, bf16[64,128]{1,0:T(8,128)(2,1)}, u32[]{:S(2)}) copy-start(bf16[64,128]{1,0:T(8,128)(2,1)} %w_output.1) | copy-start | bytes 49156
  25.7 24.7 %copy-start.2 = (f32[2,432,27]{2,1,0:T(8,128)S(1)}, f32[2,432,27]{2,1,0:T(8,128)}, u32[]{:S(2)}) copy-start(f32[2,432,27]{2,1,0:T(8,128)} %constant.4.clone.taps_ref) | copy-start | bytes 279940
  25.8 24.7 %copy-start.3 = (f32[432,1]{1,0:T(8,128)S(1)}, f32[432,1]{1,0:T(8,128)}, u32[]{:S(2)}) copy-start(f32[432,1]{1,0:T(8,128)} %constant.5.clone.voxel_ref) | copy-start | bytes 5188
  31.7 4.4 %collective-permute-start.5 = (bf16[16,128]{1,0:T(8,128)(2,1)S(1)}, bf16[16,128]{1,0:T(8,128)(2,1)S(1)}, u32[]{:S(2)}, u32[]{:S(2)}) collective-permute-start(bf16[16,128]{1,0:T(8,128)(2,1)S(1)} %get-tuple-element.41), channel_id=1, source_target_pairs={{0,8},{1,9},{2,10},{3,11},{4,12},{5,13},{6,14},{7,15},{8,0},{9,1},... | collective-permute-start | bytes 12296 | tf_op jit(solution)/shard_map/ppermute | solution.py:62
  36.2 14.2 %collective-permute-start.12 = (bf16[84,16,128]{2,1,0:T(8,128)(2,1)S(1)}, bf16[84,16,128]{2,1,0:T(8,128)(2,1)S(1)}, u32[]{:S(2)}, u32[]{:S(2)}) collective-permute-start(bf16[84,16,128]{2,1,0:T(8,128)(2,1)S(1)} %get-tuple-element.43), channel_id=1, source_target_pairs={{0,16},{1,17},{2,18},{3,19},{4,20},{5,21},{6,22},{7,23},{8,24},{9,... | collective-permute-start | bytes 1032200 | tf_op jit(solution)/shard_map/ppermute | solution.py:62
  40.0 10.4 %collective-permute-start.13 = (bf16[84,16,128]{2,1,0:T(8,128)(2,1)S(1)}, bf16[84,16,128]{2,1,0:T(8,128)(2,1)S(1)}, u32[]{:S(2)}, u32[]{:S(2)}) collective-permute-start(bf16[84,16,128]{2,1,0:T(8,128)(2,1)S(1)} %collective-permute-done.10), channel_id=1, source_target_pairs={{0,16},{1,17},{2,18},{3,19},{4,20},{5,21},{6,22},{7,23},{8,24},{9,... | collective-permute-start | bytes 1032200 | tf_op jit(solution)/shard_map/ppermute | solution.py:62
  40.1 10.3 %collective-permute-start.14 = (bf16[56,16,128]{2,1,0:T(8,128)(2,1)S(1)}, bf16[56,16,128]{2,1,0:T(8,128)(2,1)S(1)}, u32[]{:S(2)}, u32[]{:S(2)}) collective-permute-start(bf16[56,16,128]{2,1,0:T(8,128)(2,1)S(1)} %collective-permute-done.11), channel_id=1, source_target_pairs={{0,16},{1,17},{2,18},{3,19},{4,20},{5,21},{6,22},{7,23},{8,24},{9,... | collective-permute-start | bytes 688136 | tf_op jit(solution)/shard_map/ppermute | solution.py:62
  40.5 3.2 %collective-permute-start.6 = (bf16[2,16,128]{2,1,0:T(8,128)(2,1)S(1)}, bf16[2,16,128]{2,1,0:T(8,128)(2,1)S(1)}, u32[]{:S(2)}, u32[]{:S(2)}) collective-permute-start(bf16[2,16,128]{2,1,0:T(8,128)(2,1)S(1)} %shard_map.116.refs_0_), channel_id=1, source_target_pairs={{0,1},{1,0},{2,3},{3,2},{4,5},{5,4},{6,7},{7,6},{8,9},{9,8},{10,11... | collective-permute-start | bytes 24584 | tf_op jit(solution)/shard_map/ppermute | solution.py:62
  40.7 4.6 %collective-permute-start.7 = (bf16[2,16,128]{2,1,0:T(8,128)(2,1)S(1)}, bf16[2,16,128]{2,1,0:T(8,128)(2,1)S(1)}, u32[]{:S(2)}, u32[]{:S(2)}) collective-permute-start(bf16[2,16,128]{2,1,0:T(8,128)(2,1)S(1)} %shard_map.116.refs_0_), channel_id=1, source_target_pairs={{0,7},{1,2},{2,1},{3,4},{4,3},{5,6},{6,5},{7,0},{8,15},{9,10},{10,... | collective-permute-start | bytes 24584 | tf_op jit(solution)/shard_map/ppermute | solution.py:62
  45.3 2.4 %collective-permute-start.8 = (bf16[6,16,128]{2,1,0:T(8,128)(2,1)S(1)}, bf16[6,16,128]{2,1,0:T(8,128)(2,1)S(1)}, u32[]{:S(2)}, u32[]{:S(2)}) collective-permute-start(bf16[6,16,128]{2,1,0:T(8,128)(2,1)S(1)} %shard_map.117.own), channel_id=1, source_target_pairs={{0,16},{1,17},{2,18},{3,19},{4,20},{5,21},{6,22},{7,23},{8,24},{9,... | collective-permute-start | bytes 73736 | tf_op jit(solution)/shard_map/ppermute | solution.py:62
  46.8 3.5 %collective-permute-start.9 = (bf16[6,16,128]{2,1,0:T(8,128)(2,1)S(1)}, bf16[6,16,128]{2,1,0:T(8,128)(2,1)S(1)}, u32[]{:S(2)}, u32[]{:S(2)}) collective-permute-start(bf16[6,16,128]{2,1,0:T(8,128)(2,1)S(1)} %shard_map.117.own), channel_id=1, source_target_pairs={{0,112},{1,113},{2,114},{3,115},{4,116},{5,117},{6,118},{7,119},{8... | collective-permute-start | bytes 73736 | tf_op jit(solution)/shard_map/ppermute | solution.py:62

commit v4 on v3

--- a/solution.py
+++ b/solution.py
@@ -151,15 +151,15 @@
         packet_ref[29] = jnp.concatenate([project, jnp.zeros_like(project)], axis=1).astype(BF)
 
 
-def merge_kernel(atoms_ref, packet_ref, got_ref, flip_ref, flop_ref):
+def merge_kernel(atoms_ref, packet_ref, got_ref, _, flip_ref, flop_ref, share_ref):
     j = position()[2]
     upper = 1 - (j & 1)
     for yh, out in ((upper, flip_ref), (1 - upper, flop_ref)):
         for zh in range(2):
             out[zh * 12 : zh * 12 + 8] = atoms_ref[zh, yh].reshape(8, 16, 128)
             out[zh * 12 + 8 : zh * 12 + 12] = got_ref[pl.ds((zh * 2 + yh) * 4, 4)]
-        out[24:38] = packet_ref[16:30]
-        out[38:52] = got_ref[16:30]
+    share_ref[0:14] = packet_ref[16:30]
+    share_ref[14:28] = got_ref[16:30]
 
 
 def widen_kernel(
@@ -220,20 +220,20 @@
             out[n * 12 : n * 12 + 12] = source[pl.ds(zh * 12, 12)]
 
 
-def gather_kernel(own_ref, got_flip, got_flop, three_ref, two_ref):
+def gather_kernel(own_ref, got_flip, got_flop, _, three_ref, two_ref):
     j = position()[2]
-    three_ref[0:28] = got_flip[24:52]
-    three_ref[28:56] = own_ref[24:52]
-    three_ref[56:84] = got_flop[24:52]
-    two_ref[28:56] = own_ref[24:52]
+    three_ref[0:28] = got_flip[...]
+    three_ref[28:56] = own_ref[...]
+    three_ref[56:84] = got_flop[...]
+    two_ref[28:56] = own_ref[...]
 
     @pl.when((j & 1) == 1)
     def _():
-        two_ref[0:28] = got_flip[24:52]
+        two_ref[0:28] = got_flip[...]
 
     @pl.when((j & 1) == 0)
     def _():
-        two_ref[0:28] = got_flop[24:52]
+        two_ref[0:28] = got_flop[...]
 
 
 def leaf_conv(source, b, k, n, length, weight_ref):
@@ -326,24 +326,8 @@
     )
 
 
-def early_kernel(neighbour_ref, facing_flip, facing_flop, w1, wide, first, table, sems):
-    copies = own_copies(facing_flip, facing_flop, table, sems)
-    rows = atom_rows(neighbour_ref, (1, 2))
-    table[2 * ABSENT : 2 * ABSENT + 2] = jnp.zeros(ATOM, BF)
-    for copy in copies:
-        copy.wait()
-    for b in range(2):
-        for z in (1, 2):
-            assemble(table, rows, b, z, wide, b, 2 * z - 2)
-    for b in range(2):
-        mask = [mask_tile(neighbour_ref, b, dx, 1) for dx in range(3)]
-        value = gelu(leaf_conv(wide, b, 0, 3, 14, w1)).reshape(3, 14 * 16, 128)
-        for i in range(3):
-            first[b, i] = over_x(value[i], mask, 3).astype(BF)
-
-
 def main_kernel(
-    neighbour_ref, facing_flip, facing_flop, beside_flip, beside_flop, wide_mid, first_mid,
+    neighbour_ref, facing_flip, facing_flop, beside_flip, beside_flop,
     w1, w2, w3,
     skip_ref, coarse_ref,
     table, wide, first, second, masks, rows_a, middle_in, rows_b, turned, sems,
@@ -355,7 +339,7 @@
         )
         copies[-1].start()
     table[2 * ABSENT : 2 * ABSENT + 2] = jnp.zeros(ATOM, BF)
-    rows = atom_rows(neighbour_ref, (0, 3))
+    rows = atom_rows(neighbour_ref, (0, 1, 2, 3))
 
     low = halves(128)
     for b in range(2):
@@ -366,26 +350,23 @@
             masks[b, 2, dx] = of_z[1]
             masks[b, 3, dx] = jnp.where(low, of_z[1], of_z[2])
             masks[b, 4, dx] = of_z[2]
-        first[b, 2:5] = first_mid[b]
-        wide[2 * b, 2] = wide_mid[b, 0]
-        wide[2 * b + 1, 0] = wide_mid[b, 3]
 
     for copy in copies:
         copy.wait()
 
     for b in range(2):
-        assemble(table, rows, b, 0, wide, 2 * b, 0)
-        assemble(table, rows, b, 3, wide, 2 * b + 1, 1)
+        for z in range(4):
+            assemble(table, rows, b, z, wide, b, 2 * z)
 
     def masked(value, b, pattern, edge):
         return over_x(value, [masks[b, pattern, dx] for dx in range(3)], edge)
 
     for b in range(2):
-        for side in range(2):
-            value = gelu(leaf_conv(wide, 2 * b + side, 0, 2, 14, w1)).reshape(2, 14 * 16, 128)
-            for i in range(2):
-                pattern = ((0, 1), (3, 4))[side][i]
-                first[b, 5 * side + i] = masked(value[i], b, pattern, 3).astype(BF)
+        for k, n in ((0, 2), (2, 2), (4, 2), (6, 1)):
+            value = gelu(leaf_conv(wide, b, k, n, 14, w1)).reshape(n, 14 * 16, 128)
+            for i in range(n):
+                pattern = (0, 1, 2, 2, 2, 3, 4)[k + i]
+                first[b, k + i] = masked(value[i], b, pattern, 3).astype(BF)
     for b in range(2):
         for k, n in ((0, 2), (2, 2), (4, 2)):
             value = gelu(leaf_conv(first, b, k, n, 12, w2)).reshape(n, 12 * 16, 128)
@@ -531,14 +512,7 @@
         cost_estimate=cost(1),
         compiler_params=params(8),
     )(in_hbm(features), in_hbm(w_coarse), in_hbm(w_project))
-    own_flip, own_flop = pl.pallas_call(
-        merge_kernel,
-        out_shape=(shape((52, 16, 128)),) * 2,
-        in_specs=[VMEM] * 3,
-        out_specs=(VMEM,) * 2,
-        cost_estimate=cost(0.1),
-        compiler_params=params(8),
-    )(atoms, packet, to_x(packet))
+    beside = to_x(packet)
     w1, w2, w3 = pl.pallas_call(
         widen_kernel,
         out_shape=(shape((768, 384)), shape((768, 384)), shape((768, 768))),
@@ -552,34 +526,34 @@
         ],
         cost_estimate=cost(2.5),
         compiler_params=params(8),
-    )(in_hbm(w_first), in_hbm(w_second), in_hbm(jnp.swapaxes(w_middle, 1, 2)), own_flip)
+    )(in_hbm(w_first), in_hbm(w_second), in_hbm(jnp.swapaxes(w_middle, 1, 2)), packet)
+    own_flip, own_flop, share = pl.pallas_call(
+        merge_kernel,
+        out_shape=(shape((24, 16, 128)),) * 2 + (shape((28, 16, 128)),),
+        in_specs=[VMEM] * 3 + [ANY],
+        out_specs=(VMEM,) * 3,
+        cost_estimate=cost(0.1),
+        compiler_params=params(8),
+    )(atoms, packet, beside, w1)
     got_flip, got_flop = to_y(own_flip, flip), to_y(own_flop, flop)
+    share_flip, share_flop = to_y(share, flip), to_y(share, flop)
     facing_flip, facing_flop = pl.pallas_call(
         stack_kernel,
         out_shape=(shape((48, 16, 128)),) * 2,
         in_specs=[VMEM] * 4,
         out_specs=(VMEM,) * 2,
-        cost_estimate=cost(0.05),
+        cost_estimate=cost(2),
         compiler_params=params(8),
-    )(own_flip, own_flop, after(got_flip, w1), got_flop)
+    )(own_flip, own_flop, got_flip, got_flop)
     beside_flip, beside_flop = to_z(facing_flip, flip), to_z(facing_flop, flop)
-    wide_mid, first_mid = pl.pallas_call(
-        early_kernel,
-        out_shape=(shape((2, 4, 16, 16, 128)), shape((2, 3, 14, 16, 128))),
-        in_specs=[SMEM, ANY, ANY, VMEM],
-        out_specs=(VMEM,) * 2,
-        scratch_shapes=[pltpu.VMEM((194, 16, 128), BF), pltpu.SemaphoreType.DMA((2,))],
-        cost_estimate=cost(2.6),
-        compiler_params=params(14),
-    )(neighbours, facing_flip, facing_flop, w1)
     three, two = pl.pallas_call(
         gather_kernel,
         out_shape=(shape((84, 16, 128)), shape((56, 16, 128))),
-        in_specs=[VMEM] * 3,
+        in_specs=[VMEM] * 3 + [ANY],
         out_specs=(VMEM,) * 2,
-        cost_estimate=cost(0.05),
+        cost_estimate=cost(3),
         compiler_params=params(8),
-    )(own_flip, after(got_flip, wide_mid), got_flop)
+    )(share, share_flip, share_flop, facing_flop)
     mine = (
         three,
         to_y(three, lambda j, n: (j + 3) % n),
@@ -589,11 +563,11 @@
     skip, coarse = pl.pallas_call(
         main_kernel,
         out_shape=(shape((2, 64, 512)), shape((16, 128))),
-        in_specs=[SMEM] + [ANY] * 4 + [VMEM] * 5,
+        in_specs=[SMEM] + [ANY] * 4 + [VMEM] * 3,
         out_specs=(VMEM, VMEM),
         scratch_shapes=[
             pltpu.VMEM((194, 16, 128), BF),
-            pltpu.VMEM((4, 3, 16, 16, 128), BF),
+            pltpu.VMEM((2, 8, 16, 16, 128), BF),
             pltpu.VMEM((2, 7, 14, 16, 128), BF),
             pltpu.VMEM((2, 6, 12, 16, 128), BF),
             pltpu.VMEM((2, 5, 3, 16, 128), F32),
@@ -603,7 +577,7 @@
             pltpu.VMEM((512, 128), F32),
             pltpu.SemaphoreType.DMA((4,)),
         ],
-        cost_estimate=cost(6),
+        cost_estimate=cost(7),
         compiler_params=params(20),
     )(
         after(neighbours, three),
@@ -611,8 +585,6 @@
         facing_flop,
         beside_flip,
         beside_flop,
-        wide_mid,
-        first_mid,
         w1,
         w2,
         w3,

time: 53 us -> 49.7 us (0.938)
  waiting for transfers between devices: 10.2 us -> 7.95 us
  Pallas kernels: 14.8 us -> 13.4 us
    pallas_call x2 -> x1, Pallas kernels: 2.63 us -> 0.02 us  [shards(): pl.pallas_call(merge_kernel, out_shape=(shape((24, 16, 128)),) * 2 + (sha...]
    ppermute x15 -> x17, waiting for transfers between devices: 10.2 us -> 7.95 us  [permuted(): return lax.ppermute(value, AXES, pairs)]
    pallas_call x1, Pallas kernels: 5.93 us -> 7.21 us  [shards(): pl.pallas_call(main_kernel, out_shape=(shape((2, 64, 512)), shape((16, 12...]
    ppermute x15 -> x17, starting transfers between devices: 27.1 us -> 27.1 us  [permuted(): return lax.ppermute(value, AXES, pairs)]
  transfers between devices with their start and end apart: 15 -> 17, of which waited for: 6 -> 7; matrix products, arithmetic and copies ran while one was open for 0% -> 0% of each run, Pallas kernels for 21% -> 20%
where the time goes in v4:
time: 49.7 us; the launch traced here: 49.2 us
  starting transfers between devices  27.1 us (55%)
  Pallas kernels  13.4 us (27%)
  waiting for transfers between devices  7.95 us (16%)
  between operations  0.77 us (2%)
    ppermute x17, starting transfers between devices, permuted(): return lax.ppermute(value, AXES, pairs)  27.1 us
    ppermute x17, waiting for transfers between devices, permuted(): return lax.ppermute(value, AXES, pairs)  7.95 us
    pallas_call x1, Pallas kernels, shards(): pl.pallas_call(main_kernel, out_shape=(shape((2, 64, 512)), shape((16, 12...  7.21 us
    pallas_call x1, Pallas kernels, shards(): pl.pallas_call(widen_kernel, out_shape=(shape((768, 384)), shape((768, 38...  2.49 us
    pallas_call x1, Pallas kernels, shards(): pl.pallas_call(last_kernel, out_shape=shape((2, 64, 512)), in_specs=[SMEM...  2.45 us
    pallas_call x1, Pallas kernels, shards(): pl.pallas_call(pack_kernel, out_shape=(shape((2, 2, 2, 2) + ATOM), shape(...  1.18 us
  transfers between devices with their start and end apart: 17, of which 7 were waited for; matrix products, arithmetic and copies ran while one was open for 0% of the time, Pallas kernels for 20%

profile of v4, /device:TPU:1, one launch (start us, length us, event | category | flops | bytes accessed | tf_op | source)
XLA Modules:
  0.0 49.2 jit_solution(7798735957783469155)
XLA Ops:
  0.0 1.2 %shard_map.109 = (bf16[2,2,2,2,2,16,128]{6,5,4,3,2,1,0:T(8,128)(2,1)S(1)}, bf16[30,16,128]{2,1,0:T(8,128)(2,1)S(1)}) custom-call(bf16[2,64,512]{2,1,0:T(8,128)(2,1)} %features_hbm.1, bf16[27,16,128]{2,1,0:T(8,128)(2,1)} %w_coarse_hbm.1, bf16[16,64]{1,0:T(8,128)(2,1)} %w_project_hbm.1), custom_call_target="tpu_custom_call" | custom-call | flops 1150000000 | tf_op jit(solution)/shard_map/pallas_call | solution.py:500
  1.2 3.8 %collective-permute-start = (bf16[30,16,128]{2,1,0:T(8,128)(2,1)S(1)}, bf16[30,16,128]{2,1,0:T(8,128)(2,1)S(1)}, u32[]{:S(2)}, u32[]{:S(2)}) collective-permute-start(bf16[30,16,128]{2,1,0:T(8,128)(2,1)S(1)} %get-tuple-element.24._.packet_ref), channel_id=1, source_target_pairs={{0,8},{1,9},{2,10},{3,11},{4,12},{5,13},{6,14},{7,15},{8,0},{9,1},... | collective-permute-start | bytes 368648 | tf_op jit(solution)/shard_map/ppermute | solution.py:62
  5.0 2.5 %shard_map.110 = (bf16[768,384]{1,0:T(8,128)(2,1)S(1)}, bf16[768,384]{1,0:T(8,128)(2,1)S(1)}, bf16[768,768]{1,0:T(8,128)(2,1)S(1)}) custom-call(bf16[27,64,64]{2,1,0:T(8,128)(2,1)} %first_hbm.1, bf16[27,64,64]{2,1,0:T(8,128)(2,1)} %second_hbm.1, bf16[27,64,128]{2,1,0:T(8,128)(2,1)} %bitcast.17, bf16[30,16,128]{2,1,0:T(8,128)(2,1)S(1)} %get-tuple-element.24._.packet_ref), custom_call_target="tpu_custom_call" | custom-call | flops 2875000064 | tf_op jit(solution)/shard_map/pallas_call | solution.py:516
  7.5 0.3 collective-permute-done.got_ref
  7.8 1.3 %collective-permute-start.3 = (bf16[24,16,128]{2,1,0:T(8,128)(2,1)S(1)}, bf16[24,16,128]{2,1,0:T(8,128)(2,1)S(1)}, u32[]{:S(2)}, u32[]{:S(2)}) collective-permute-start(bf16[24,16,128]{2,1,0:T(8,128)(2,1)S(1)} %get-tuple-element.27.own_flip), channel_id=1, source_target_pairs={{0,1},{1,0},{2,3},{3,2},{4,5},{5,4},{6,7},{7,6},{8,9},{9,8},{10,11... | collective-permute-start | bytes 294920 | tf_op jit(solution)/shard_map/ppermute | solution.py:62
  9.1 2.8 %collective-permute-start.4 = (bf16[24,16,128]{2,1,0:T(8,128)(2,1)S(1)}, bf16[24,16,128]{2,1,0:T(8,128)(2,1)S(1)}, u32[]{:S(2)}, u32[]{:S(2)}) collective-permute-start(bf16[24,16,128]{2,1,0:T(8,128)(2,1)S(1)} %get-tuple-element.28.own_flop), channel_id=1, source_target_pairs={{0,7},{1,2},{2,1},{3,4},{4,3},{5,6},{6,5},{7,0},{8,15},{9,10},{10,... | collective-permute-start | bytes 294920 | tf_op jit(solution)/shard_map/ppermute | solution.py:62
  11.9 0.9 %collective-permute-start.2 = (bf16[28,16,128]{2,1,0:T(8,128)(2,1)S(1)}, bf16[28,16,128]{2,1,0:T(8,128)(2,1)S(1)}, u32[]{:S(2)}, u32[]{:S(2)}) collective-permute-start(bf16[28,16,128]{2,1,0:T(8,128)(2,1)S(1)} %get-tuple-element.26.own_ref), channel_id=1, source_target_pairs={{0,7},{1,2},{2,1},{3,4},{4,3},{5,6},{6,5},{7,0},{8,15},{9,10},{10,... | collective-permute-start | bytes 344072 | tf_op jit(solution)/shard_map/ppermute | solution.py:62
  12.9 0.0 collective-permute-done.3.got_flip
  12.9 1.8 %collective-permute-done.4.got_flop = bf16[24,16,128]{2,1,0:T(8,128)(2,1)S(1)} collective-permute-done((bf16[24,16,128]{2,1,0:T(8,128)(2,1)S(1)}, bf16[24,16,128]{2,1,0:T(8,128)(2,1)S(1)}, u32[]{:S(2)}, u32[]{:S(2)}) %collective-permute-start.4) | collective-permute-done | bytes 98336 | tf_op jit(solution)/shard_map/ppermute | solution.py:62
  14.7 5.1 %collective-permute-start.6 = (bf16[48,16,128]{2,1,0:T(8,128)(2,1)S(1)}, bf16[48,16,128]{2,1,0:T(8,128)(2,1)S(1)}, u32[]{:S(2)}, u32[]{:S(2)}) collective-permute-start(bf16[48,16,128]{2,1,0:T(8,128)(2,1)S(1)} %get-tuple-element.29._.facing_flop), channel_id=1, source_target_pairs={{0,112},{1,113},{2,114},{3,115},{4,116},{5,117},{6,118},{7,119},{8... | collective-permute-start | bytes 589832 | tf_op jit(solution)/shard_map/ppermute | solution.py:62
  19.9 0.0 collective-permute-start.5
  19.9 0.0 collective-permute-done.1.got_flip
  19.9 0.0 collective-permute-done.2.got_flop
  19.9 0.1 shard_map.113
  19.9 2.1 %collective-permute-start.12 = (bf16[84,16,128]{2,1,0:T(8,128)(2,1)S(1)}, bf16[84,16,128]{2,1,0:T(8,128)(2,1)S(1)}, u32[]{:S(2)}, u32[]{:S(2)}) collective-permute-start(bf16[84,16,128]{2,1,0:T(8,128)(2,1)S(1)} %get-tuple-element.37), channel_id=1, source_target_pairs={{0,3},{1,4},{2,5},{3,6},{4,7},{5,0},{6,1},{7,2},{8,11},{9,12},{10,... | collective-permute-start | bytes 1032200 | tf_op jit(solution)/shard_map/ppermute | solution.py:62
  22.1 0.3 collective-permute-start.13
  22.4 1.1 %collective-permute-done.6.beside_flop = bf16[48,16,128]{2,1,0:T(8,128)(2,1)S(1)} collective-permute-done((bf16[48,16,128]{2,1,0:T(8,128)(2,1)S(1)}, bf16[48,16,128]{2,1,0:T(8,128)(2,1)S(1)}, u32[]{:S(2)}, u32[]{:S(2)}) %collective-permute-start.6) | collective-permute-done | bytes 196640 | tf_op jit(solution)/shard_map/ppermute | solution.py:62
  23.5 0.0 copy-start.2
  23.5 0.0 copy-start.3
  23.5 7.2 %shard_map.114 = (bf16[2,64,512]{2,1,0:T(8,128)(2,1)S(1)}, bf16[16,128]{1,0:T(8,128)(2,1)S(1)}) custom-call(s32[2,27]{1,0:T(2,128)S(1)} %copy-done.1, bf16[48,16,128]{2,1,0:T(8,128)(2,1)S(1)} %get-tuple-element.32.facing_flip, bf16[48,16,128]{2,1,0:T(8,128)(2,1)S(1)} %get-tuple-element.29._.facing_flop, ...), custom_call_target="tpu_custom_call" | custom-call | flops 8049999872 | tf_op jit(solution)/shard_map/pallas_call | solution.py:563
  30.8 3.2 %collective-permute-start.7 = (bf16[16,128]{1,0:T(8,128)(2,1)S(1)}, bf16[16,128]{1,0:T(8,128)(2,1)S(1)}, u32[]{:S(2)}, u32[]{:S(2)}) collective-permute-start(bf16[16,128]{1,0:T(8,128)(2,1)S(1)} %get-tuple-element.35), channel_id=1, source_target_pairs={{0,8},{1,9},{2,10},{3,11},{4,12},{5,13},{6,14},{7,15},{8,0},{9,1},... | collective-permute-start | bytes 12296 | tf_op jit(solution)/shard_map/ppermute | solution.py:62
  34.0 1.0 %collective-permute-done.7 = bf16[16,128]{1,0:T(8,128)(2,1)S(1)} collective-permute-done((bf16[16,128]{1,0:T(8,128)(2,1)S(1)}, bf16[16,128]{1,0:T(8,128)(2,1)S(1)}, u32[]{:S(2)}, u32[]{:S(2)}) %collective-permute-start.7) | collective-permute-done | bytes 4128 | tf_op jit(solution)/shard_map/ppermute | solution.py:62
  35.0 2.1 %collective-permute-start.14 = (bf16[84,16,128]{2,1,0:T(8,128)(2,1)S(1)}, bf16[84,16,128]{2,1,0:T(8,128)(2,1)S(1)}, u32[]{:S(2)}, u32[]{:S(2)}) collective-permute-start(bf16[84,16,128]{2,1,0:T(8,128)(2,1)S(1)} %get-tuple-element.37), channel_id=1, source_target_pairs={{0,16},{1,17},{2,18},{3,19},{4,20},{5,21},{6,22},{7,23},{8,24},{9,... | collective-permute-start | bytes 1032200 | tf_op jit(solution)/shard_map/ppermute | solution.py:62
  37.1 0.1 collective-permute-start.15
  37.2 0.4 collective-permute-start.16
  37.6 2.3 %collective-permute-start.9 = (bf16[2,16,128]{2,1,0:T(8,128)(2,1)S(1)}, bf16[2,16,128]{2,1,0:T(8,128)(2,1)S(1)}, u32[]{:S(2)}, u32[]{:S(2)}) collective-permute-start(bf16[2,16,128]{2,1,0:T(8,128)(2,1)S(1)} %shard_map.115.refs_0_), channel_id=1, source_target_pairs={{0,7},{1,2},{2,1},{3,4},{4,3},{5,6},{6,5},{7,0},{8,15},{9,10},{10,... | collective-permute-start | bytes 24584 | tf_op jit(solution)/shard_map/ppermute | solution.py:62
  39.9 0.3 collective-permute-done.8.refs_1_
  40.1 2.1 %collective-permute-done.9.refs_2_ = bf16[2,16,128]{2,1,0:T(8,128)(2,1)S(1)} collective-permute-done((bf16[2,16,128]{2,1,0:T(8,128)(2,1)S(1)}, bf16[2,16,128]{2,1,0:T(8,128)(2,1)S(1)}, u32[]{:S(2)}, u32[]{:S(2)}) %collective-permute-start.9) | collective-permute-done | bytes 8224 | tf_op jit(solution)/shard_map/ppermute | solution.py:62
  42.3 1.2 %collective-permute-start.10 = (bf16[6,16,128]{2,1,0:T(8,128)(2,1)S(1)}, bf16[6,16,128]{2,1,0:T(8,128)(2,1)S(1)}, u32[]{:S(2)}, u32[]{:S(2)}) collective-permute-start(bf16[6,16,128]{2,1,0:T(8,128)(2,1)S(1)} %shard_map.116.own), channel_id=1, source_target_pairs={{0,16},{1,17},{2,18},{3,19},{4,20},{5,21},{6,22},{7,23},{8,24},{9,... | collective-permute-start | bytes 73736 | tf_op jit(solution)/shard_map/ppermute | solution.py:62
  43.5 1.3 %collective-permute-start.11 = (bf16[6,16,128]{2,1,0:T(8,128)(2,1)S(1)}, bf16[6,16,128]{2,1,0:T(8,128)(2,1)S(1)}, u32[]{:S(2)}, u32[]{:S(2)}) collective-permute-start(bf16[6,16,128]{2,1,0:T(8,128)(2,1)S(1)} %shard_map.116.own), channel_id=1, source_target_pairs={{0,112},{1,113},{2,114},{3,115},{4,116},{5,117},{6,118},{7,119},{8... | collective-permute-start | bytes 73736 | tf_op jit(solution)/shard_map/ppermute | solution.py:62
  45.4 1.3 %collective-permute-done.11.above = bf16[6,16,128]{2,1,0:T(8,128)(2,1)S(1)} collective-permute-done((bf16[6,16,128]{2,1,0:T(8,128)(2,1)S(1)}, bf16[6,16,128]{2,1,0:T(8,128)(2,1)S(1)}, u32[]{:S(2)}, u32[]{:S(2)}) %collective-permute-start.11) | collective-permute-done | bytes 24608 | tf_op jit(solution)/shard_map/ppermute | solution.py:62
  46.8 2.5 %shard_map.117 = bf16[2,64,512]{2,1,0:T(8,128)(2,1)} custom-call(s32[1]{0:T(128)S(6)} %copy.12.live_ref, s32[2,27]{1,0:T(2,128)S(1)} %copy-done.1, f32[2,432,27]{2,1,0:T(8,128)S(1)} %copy-done.2, f32[432,1]{1,0:T(8,128)S(1)} %copy-done.3, bf16[6,16,128]{2,1,0:T(8,128)(2,1)S(1)} %shard_map.116.own, bf16[6,16,128]{2,1,0:T(8,128)(2,1)S(1)} %collective-permute-done.10.below, ...), custom_call_target="tpu_custom_call" | custom-call | flops 2760000000 | tf_op jit(solution)/shard_map/pallas_call | solution.py:597
  (19 shorter events, 0.1 us)
Async XLA Ops:
  1.2 6.6 %collective-permute-start = (bf16[30,16,128]{2,1,0:T(8,128)(2,1)S(1)}, bf16[30,16,128]{2,1,0:T(8,128)(2,1)S(1)}, u32[]{:S(2)}, u32[]{:S(2)}) collective-permute-start(bf16[30,16,128]{2,1,0:T(8,128)(2,1)S(1)} %get-tuple-element.24._.packet_ref), channel_id=1, source_target_pairs={{0,8},{1,9},{2,10},{3,11},{4,12},{5,13},{6,14},{7,15},{8,0},{9,1},... | collective-permute-start | bytes 368648 | tf_op jit(solution)/shard_map/ppermute | solution.py:62
  7.8 5.1 %collective-permute-start.3 = (bf16[24,16,128]{2,1,0:T(8,128)(2,1)S(1)}, bf16[24,16,128]{2,1,0:T(8,128)(2,1)S(1)}, u32[]{:S(2)}, u32[]{:S(2)}) collective-permute-start(bf16[24,16,128]{2,1,0:T(8,128)(2,1)S(1)} %get-tuple-element.27.own_flip), channel_id=1, source_target_pairs={{0,1},{1,0},{2,3},{3,2},{4,5},{5,4},{6,7},{7,6},{8,9},{9,8},{10,11... | collective-permute-start | bytes 294920 | tf_op jit(solution)/shard_map/ppermute | solution.py:62
  9.1 5.6 %collective-permute-start.4 = (bf16[24,16,128]{2,1,0:T(8,128)(2,1)S(1)}, bf16[24,16,128]{2,1,0:T(8,128)(2,1)S(1)}, u32[]{:S(2)}, u32[]{:S(2)}) collective-permute-start(bf16[24,16,128]{2,1,0:T(8,128)(2,1)S(1)} %get-tuple-element.28.own_flop), channel_id=1, source_target_pairs={{0,7},{1,2},{2,1},{3,4},{4,3},{5,6},{6,5},{7,0},{8,15},{9,10},{10,... | collective-permute-start | bytes 294920 | tf_op jit(solution)/shard_map/ppermute | solution.py:62
  11.9 7.9 %collective-permute-start.1 = (bf16[28,16,128]{2,1,0:T(8,128)(2,1)S(1)}, bf16[28,16,128]{2,1,0:T(8,128)(2,1)S(1)}, u32[]{:S(2)}, u32[]{:S(2)}) collective-permute-start(bf16[28,16,128]{2,1,0:T(8,128)(2,1)S(1)} %get-tuple-element.26.own_ref), channel_id=1, source_target_pairs={{0,1},{1,0},{2,3},{3,2},{4,5},{5,4},{6,7},{7,6},{8,9},{9,8},{10,11... | collective-permute-start | bytes 344072 | tf_op jit(solution)/shard_map/ppermute | solution.py:62
  11.9 7.9 %collective-permute-start.2 = (bf16[28,16,128]{2,1,0:T(8,128)(2,1)S(1)}, bf16[28,16,128]{2,1,0:T(8,128)(2,1)S(1)}, u32[]{:S(2)}, u32[]{:S(2)}) collective-permute-start(bf16[28,16,128]{2,1,0:T(8,128)(2,1)S(1)} %get-tuple-element.26.own_ref), channel_id=1, source_target_pairs={{0,7},{1,2},{2,1},{3,4},{4,3},{5,6},{6,5},{7,0},{8,15},{9,10},{10,... | collective-permute-start | bytes 344072 | tf_op jit(solution)/shard_map/ppermute | solution.py:62
  14.7 8.8 %collective-permute-start.6 = (bf16[48,16,128]{2,1,0:T(8,128)(2,1)S(1)}, bf16[48,16,128]{2,1,0:T(8,128)(2,1)S(1)}, u32[]{:S(2)}, u32[]{:S(2)}) collective-permute-start(bf16[48,16,128]{2,1,0:T(8,128)(2,1)S(1)} %get-tuple-element.29._.facing_flop), channel_id=1, source_target_pairs={{0,112},{1,113},{2,114},{3,115},{4,116},{5,117},{6,118},{7,119},{8... | collective-permute-start | bytes 589832 | tf_op jit(solution)/shard_map/ppermute | solution.py:62
  19.9 3.7 %copy-start.1 = (s32[2,27]{1,0:T(2,128)S(1)}, s32[2,27]{1,0:T(2,128)}, u32[]{:S(2)}) copy-start(s32[2,27]{1,0:T(2,128)} %neighbour_ref.2) | copy-start | bytes 652
  19.9 3.7 %collective-permute-start.5 = (bf16[48,16,128]{2,1,0:T(8,128)(2,1)S(1)}, bf16[48,16,128]{2,1,0:T(8,128)(2,1)S(1)}, u32[]{:S(2)}, u32[]{:S(2)}) collective-permute-start(bf16[48,16,128]{2,1,0:T(8,128)(2,1)S(1)} %get-tuple-element.32.facing_flip), channel_id=1, source_target_pairs={{0,16},{1,17},{2,18},{3,19},{4,20},{5,21},{6,22},{7,23},{8,24},{9,... | collective-permute-start | bytes 589832 | tf_op jit(solution)/shard_map/ppermute | solution.py:62
  19.9 17.2 %collective-permute-start.12 = (bf16[84,16,128]{2,1,0:T(8,128)(2,1)S(1)}, bf16[84,16,128]{2,1,0:T(8,128)(2,1)S(1)}, u32[]{:S(2)}, u32[]{:S(2)}) collective-permute-start(bf16[84,16,128]{2,1,0:T(8,128)(2,1)S(1)} %get-tuple-element.37), channel_id=1, source_target_pairs={{0,3},{1,4},{2,5},{3,6},{4,7},{5,0},{6,1},{7,2},{8,11},{9,12},{10,... | collective-permute-start | bytes 1032200 | tf_op jit(solution)/shard_map/ppermute | solution.py:62
  22.1 15.1 %collective-permute-start.13 = (bf16[56,16,128]{2,1,0:T(8,128)(2,1)S(1)}, bf16[56,16,128]{2,1,0:T(8,128)(2,1)S(1)}, u32[]{:S(2)}, u32[]{:S(2)}) collective-permute-start(bf16[56,16,128]{2,1,0:T(8,128)(2,1)S(1)} %get-tuple-element.36), channel_id=1, source_target_pairs={{0,5},{1,6},{2,7},{3,0},{4,1},{5,2},{6,3},{7,4},{8,13},{9,14},{10,... | collective-permute-start | bytes 688136 | tf_op jit(solution)/shard_map/ppermute | solution.py:62
  23.5 23.2 %copy-start = (bf16[64,128]{1,0:T(8,128)(2,1)S(1)}, bf16[64,128]{1,0:T(8,128)(2,1)}, u32[]{:S(2)}) copy-start(bf16[64,128]{1,0:T(8,128)(2,1)} %w_output.1) | copy-start | bytes 49156
  23.5 23.2 %copy-start.2 = (f32[2,432,27]{2,1,0:T(8,128)S(1)}, f32[2,432,27]{2,1,0:T(8,128)}, u32[]{:S(2)}) copy-start(f32[2,432,27]{2,1,0:T(8,128)} %constant.4.clone.taps_ref) | copy-start | bytes 279940
  23.5 23.2 %copy-start.3 = (f32[432,1]{1,0:T(8,128)S(1)}, f32[432,1]{1,0:T(8,128)}, u32[]{:S(2)}) copy-start(f32[432,1]{1,0:T(8,128)} %constant.5.clone.voxel_ref) | copy-start | bytes 5188
  30.8 4.2 %collective-permute-start.7 = (bf16[16,128]{1,0:T(8,128)(2,1)S(1)}, bf16[16,128]{1,0:T(8,128)(2,1)S(1)}, u32[]{:S(2)}, u32[]{:S(2)}) collective-permute-start(bf16[16,128]{1,0:T(8,128)(2,1)S(1)} %get-tuple-element.35), channel_id=1, source_target_pairs={{0,8},{1,9},{2,10},{3,11},{4,12},{5,13},{6,14},{7,15},{8,0},{9,1},... | collective-permute-start | bytes 12296 | tf_op jit(solution)/shard_map/ppermute | solution.py:62
  35.0 11.7 %collective-permute-start.14 = (bf16[84,16,128]{2,1,0:T(8,128)(2,1)S(1)}, bf16[84,16,128]{2,1,0:T(8,128)(2,1)S(1)}, u32[]{:S(2)}, u32[]{:S(2)}) collective-permute-start(bf16[84,16,128]{2,1,0:T(8,128)(2,1)S(1)} %get-tuple-element.37), channel_id=1, source_target_pairs={{0,16},{1,17},{2,18},{3,19},{4,20},{5,21},{6,22},{7,23},{8,24},{9,... | collective-permute-start | bytes 1032200 | tf_op jit(solution)/shard_map/ppermute | solution.py:62
  37.1 9.6 %collective-permute-start.15 = (bf16[84,16,128]{2,1,0:T(8,128)(2,1)S(1)}, bf16[84,16,128]{2,1,0:T(8,128)(2,1)S(1)}, u32[]{:S(2)}, u32[]{:S(2)}) collective-permute-start(bf16[84,16,128]{2,1,0:T(8,128)(2,1)S(1)} %collective-permute-done.12), channel_id=1, source_target_pairs={{0,16},{1,17},{2,18},{3,19},{4,20},{5,21},{6,22},{7,23},{8,24},{9,... | collective-permute-start | bytes 1032200 | tf_op jit(solution)/shard_map/ppermute | solution.py:62
  37.2 9.5 %collective-permute-start.16 = (bf16[56,16,128]{2,1,0:T(8,128)(2,1)S(1)}, bf16[56,16,128]{2,1,0:T(8,128)(2,1)S(1)}, u32[]{:S(2)}, u32[]{:S(2)}) collective-permute-start(bf16[56,16,128]{2,1,0:T(8,128)(2,1)S(1)} %collective-permute-done.13), channel_id=1, source_target_pairs={{0,16},{1,17},{2,18},{3,19},{4,20},{5,21},{6,22},{7,23},{8,24},{9,... | collective-permute-start | bytes 688136 | tf_op jit(solution)/shard_map/ppermute | solution.py:62
  37.6 2.5 %collective-permute-start.8 = (bf16[2,16,128]{2,1,0:T(8,128)(2,1)S(1)}, bf16[2,16,128]{2,1,0:T(8,128)(2,1)S(1)}, u32[]{:S(2)}, u32[]{:S(2)}) collective-permute-start(bf16[2,16,128]{2,1,0:T(8,128)(2,1)S(1)} %shard_map.115.refs_0_), channel_id=1, source_target_pairs={{0,1},{1,0},{2,3},{3,2},{4,5},{5,4},{6,7},{7,6},{8,9},{9,8},{10,11... | collective-permute-start | bytes 24584 | tf_op jit(solution)/shard_map/ppermute | solution.py:62
  37.6 4.6 %collective-permute-start.9 = (bf16[2,16,128]{2,1,0:T(8,128)(2,1)S(1)}, bf16[2,16,128]{2,1,0:T(8,128)(2,1)S(1)}, u32[]{:S(2)}, u32[]{:S(2)}) collective-permute-start(bf16[2,16,128]{2,1,0:T(8,128)(2,1)S(1)} %shard_map.115.refs_0_), channel_id=1, source_target_pairs={{0,7},{1,2},{2,1},{3,4},{4,3},{5,6},{6,5},{7,0},{8,15},{9,10},{10,... | collective-permute-start | bytes 24584 | tf_op jit(solution)/shard_map/ppermute | solution.py:62
  42.3 3.1 %collective-permute-start.10 = (bf16[6,16,128]{2,1,0:T(8,128)(2,1)S(1)}, bf16[6,16,128]{2,1,0:T(8,128)(2,1)S(1)}, u32[]{:S(2)}, u32[]{:S(2)}) collective-permute-start(bf16[6,16,128]{2,1,0:T(8,128)(2,1)S(1)} %shard_map.116.own), channel_id=1, source_target_pairs={{0,16},{1,17},{2,18},{3,19},{4,20},{5,21},{6,22},{7,23},{8,24},{9,... | collective-permute-start | bytes 73736 | tf_op jit(solution)/shard_map/ppermute | solution.py:62
  43.5 3.3 %collective-permute-start.11 = (bf16[6,16,128]{2,1,0:T(8,128)(2,1)S(1)}, bf16[6,16,128]{2,1,0:T(8,128)(2,1)S(1)}, u32[]{:S(2)}, u32[]{:S(2)}) collective-permute-start(bf16[6,16,128]{2,1,0:T(8,128)(2,1)S(1)} %shard_map.116.own), channel_id=1, source_target_pairs={{0,112},{1,113},{2,114},{3,115},{4,116},{5,117},{6,118},{7,119},{8... | collective-permute-start | bytes 73736 | tf_op jit(solution)/shard_map/ppermute | solution.py:62

commit v5 on v4

--- a/solution.py
+++ b/solution.py
@@ -424,11 +424,8 @@
     skip_ref[...] = turned[...].T.astype(BF).reshape(2, 64, 512)
 
 
-def last_kernel(
-    live_ref, neighbour_ref, taps_ref, voxel_ref, own, below, above, mine_a, mine_b, mine_c,
-    theirs_a, theirs_b, theirs_c, w_output, skip_ref, out_ref, coarse_ref,
-):
-    g, h, j, core = position()
+def choose_kernel(neighbour_ref, taps_ref, voxel_ref, chosen_ref):
+    g, h, j, _ = position()
     entry = neighbour_ref[...]
     apart_g = (entry >> 5) ^ g
     apart_j = ((entry >> 1) & 7) ^ j
@@ -440,9 +437,16 @@
     code = jnp.where(entry >= 0, code, -4096).astype(F32)
     rows = jnp.sum(taps_ref[0] * code[0:1] + taps_ref[1] * code[1:2], axis=1, keepdims=True)
     rows = (rows + voxel_ref[...]).astype(jnp.int32)
+    chosen_ref[...] = (rows == lax.broadcasted_iota(jnp.int32, (432, 288), 1)).astype(F32).astype(BF)
+
+
+def last_kernel(
+    live_ref, chosen_ref, own, below, above, mine_a, mine_b, mine_c,
+    theirs_a, theirs_b, theirs_c, w_output, skip_ref, out_ref, coarse_ref,
+):
+    core = position()[3]
     tiles = jnp.concatenate([r[...].reshape(96, 128) for r in (own, below, above)], axis=0)
-    chosen = (rows == lax.broadcasted_iota(jnp.int32, (432, 288), 1)).astype(F32).astype(BF)
-    taps = dot(chosen, tiles).astype(BF)
+    taps = dot(chosen_ref[...], tiles).astype(BF)
 
     def weight(parts, t):
         chosen = [part[:, t % 14] for part in parts]
@@ -590,6 +594,14 @@
         w3,
     )
 
+    chosen = pl.pallas_call(
+        choose_kernel,
+        out_shape=shape((432, 288)),
+        in_specs=[VMEM] * 3,
+        out_specs=VMEM,
+        cost_estimate=cost(0.5),
+        compiler_params=params(8),
+    )(neighbours, *(jnp.asarray(a) for a in tap_table()))
     both = joined(coarse[None], to_x(coarse)[None])
     theirs = [to_z(after(part, both), flip) for part in mine]
     layer = joined(both, to_y(both, flip), to_y(both, flop))
@@ -597,7 +609,7 @@
     return pl.pallas_call(
         last_kernel,
         out_shape=shape((2, 64, 512)),
-        in_specs=[SMEM] + [VMEM] * 14,
+        in_specs=[SMEM] + [VMEM] * 12,
         out_specs=VMEM,
         scratch_shapes=[
             pltpu.VMEM((16, 128), F32),
@@ -606,8 +618,7 @@
         compiler_params=params(8),
     )(
         live_counts,
-        neighbours,
-        *(jnp.asarray(a) for a in tap_table()),
+        chosen,
         layer,
         below,
         above,

time: 49.7 us -> 49.5 us (level)
  transfers between devices with their start and end apart: 17 -> 17, of which waited for: 7 -> 7; matrix products, arithmetic and copies ran while one was open for 0% -> 0% of each run, Pallas kernels for 20% -> 21%
where the time goes in v5:
time: 49.5 us; the launch traced here: 49 us
  starting transfers between devices  27.1 us (55%)
  Pallas kernels  13.5 us (27%)
  waiting for transfers between devices  7.67 us (15%)
  between operations  0.76 us (2%)
    ppermute x17, starting transfers between devices, permuted(): return lax.ppermute(value, AXES, pairs)  27.1 us
    ppermute x17, waiting for transfers between devices, permuted(): return lax.ppermute(value, AXES, pairs)  7.67 us
    pallas_call x1, Pallas kernels, shards(): pl.pallas_call(main_kernel, out_shape=(shape((2, 64, 512)), shape((16, 12...  7.31 us
    pallas_call x1, Pallas kernels, shards(): pl.pallas_call(widen_kernel, out_shape=(shape((768, 384)), shape((768, 38...  2.49 us
    pallas_call x1, Pallas kernels, shards(): pl.pallas_call(last_kernel, out_shape=shape((2, 64, 512)), in_specs=[SMEM...  2.16 us
    pallas_call x1, Pallas kernels, shards(): pl.pallas_call(pack_kernel, out_shape=(shape((2, 2, 2, 2) + ATOM), shape(...  1.18 us
  transfers between devices with their start and end apart: 17, of which 7 were waited for; matrix products, arithmetic and copies ran while one was open for 0% of the time, Pallas kernels for 21%

profile of v5, /device:TPU:1, one launch (start us, length us, event | category | flops | bytes accessed | tf_op | source)
XLA Modules:
  0.0 49.0 jit_solution(10755592524277082747)
XLA Ops:
  0.0 1.2 %shard_map.110 = (bf16[2,2,2,2,2,16,128]{6,5,4,3,2,1,0:T(8,128)(2,1)S(1)}, bf16[30,16,128]{2,1,0:T(8,128)(2,1)S(1)}) custom-call(bf16[2,64,512]{2,1,0:T(8,128)(2,1)} %features_hbm.1, bf16[27,16,128]{2,1,0:T(8,128)(2,1)} %w_coarse_hbm.1, bf16[16,64]{1,0:T(8,128)(2,1)} %w_project_hbm.1), custom_call_target="tpu_custom_call" | custom-call | flops 1150000000 | tf_op jit(solution)/shard_map/pallas_call | solution.py:504
  1.2 3.8 %collective-permute-start = (bf16[30,16,128]{2,1,0:T(8,128)(2,1)S(1)}, bf16[30,16,128]{2,1,0:T(8,128)(2,1)S(1)}, u32[]{:S(2)}, u32[]{:S(2)}) collective-permute-start(bf16[30,16,128]{2,1,0:T(8,128)(2,1)S(1)} %get-tuple-element.24._.packet_ref), channel_id=1, source_target_pairs={{0,8},{1,9},{2,10},{3,11},{4,12},{5,13},{6,14},{7,15},{8,0},{9,1},... | collective-permute-start | bytes 368648 | tf_op jit(solution)/shard_map/ppermute | solution.py:62
  5.0 2.5 %shard_map.111 = (bf16[768,384]{1,0:T(8,128)(2,1)S(1)}, bf16[768,384]{1,0:T(8,128)(2,1)S(1)}, bf16[768,768]{1,0:T(8,128)(2,1)S(1)}) custom-call(bf16[27,64,64]{2,1,0:T(8,128)(2,1)} %first_hbm.1, bf16[27,64,64]{2,1,0:T(8,128)(2,1)} %second_hbm.1, bf16[27,64,128]{2,1,0:T(8,128)(2,1)} %bitcast.17, bf16[30,16,128]{2,1,0:T(8,128)(2,1)S(1)} %get-tuple-element.24._.packet_ref), custom_call_target="tpu_custom_call" | custom-call | flops 2875000064 | tf_op jit(solution)/shard_map/pallas_call | solution.py:520
  7.5 0.3 collective-permute-done.got_ref
  7.8 1.3 %collective-permute-start.3 = (bf16[24,16,128]{2,1,0:T(8,128)(2,1)S(1)}, bf16[24,16,128]{2,1,0:T(8,128)(2,1)S(1)}, u32[]{:S(2)}, u32[]{:S(2)}) collective-permute-start(bf16[24,16,128]{2,1,0:T(8,128)(2,1)S(1)} %get-tuple-element.27.own_flip), channel_id=1, source_target_pairs={{0,1},{1,0},{2,3},{3,2},{4,5},{5,4},{6,7},{7,6},{8,9},{9,8},{10,11... | collective-permute-start | bytes 294920 | tf_op jit(solution)/shard_map/ppermute | solution.py:62
  9.1 2.8 %collective-permute-start.4 = (bf16[24,16,128]{2,1,0:T(8,128)(2,1)S(1)}, bf16[24,16,128]{2,1,0:T(8,128)(2,1)S(1)}, u32[]{:S(2)}, u32[]{:S(2)}) collective-permute-start(bf16[24,16,128]{2,1,0:T(8,128)(2,1)S(1)} %get-tuple-element.28.own_flop), channel_id=1, source_target_pairs={{0,7},{1,2},{2,1},{3,4},{4,3},{5,6},{6,5},{7,0},{8,15},{9,10},{10,... | collective-permute-start | bytes 294920 | tf_op jit(solution)/shard_map/ppermute | solution.py:62
  11.9 0.9 %collective-permute-start.2 = (bf16[28,16,128]{2,1,0:T(8,128)(2,1)S(1)}, bf16[28,16,128]{2,1,0:T(8,128)(2,1)S(1)}, u32[]{:S(2)}, u32[]{:S(2)}) collective-permute-start(bf16[28,16,128]{2,1,0:T(8,128)(2,1)S(1)} %get-tuple-element.26.own_ref), channel_id=1, source_target_pairs={{0,7},{1,2},{2,1},{3,4},{4,3},{5,6},{6,5},{7,0},{8,15},{9,10},{10,... | collective-permute-start | bytes 344072 | tf_op jit(solution)/shard_map/ppermute | solution.py:62
  12.9 0.0 collective-permute-done.3.got_flip
  12.9 1.8 %collective-permute-done.4.got_flop = bf16[24,16,128]{2,1,0:T(8,128)(2,1)S(1)} collective-permute-done((bf16[24,16,128]{2,1,0:T(8,128)(2,1)S(1)}, bf16[24,16,128]{2,1,0:T(8,128)(2,1)S(1)}, u32[]{:S(2)}, u32[]{:S(2)}) %collective-permute-start.4) | collective-permute-done | bytes 98336 | tf_op jit(solution)/shard_map/ppermute | solution.py:62
  14.7 5.1 %collective-permute-start.6 = (bf16[48,16,128]{2,1,0:T(8,128)(2,1)S(1)}, bf16[48,16,128]{2,1,0:T(8,128)(2,1)S(1)}, u32[]{:S(2)}, u32[]{:S(2)}) collective-permute-start(bf16[48,16,128]{2,1,0:T(8,128)(2,1)S(1)} %get-tuple-element.29._.facing_flop), channel_id=1, source_target_pairs={{0,112},{1,113},{2,114},{3,115},{4,116},{5,117},{6,118},{7,119},{8... | collective-permute-start | bytes 589832 | tf_op jit(solution)/shard_map/ppermute | solution.py:62
  19.9 0.0 collective-permute-start.5
  19.9 0.0 collective-permute-done.1.got_flip
  19.9 0.1 shard_map.114
  19.9 2.1 %collective-permute-start.12 = (bf16[84,16,128]{2,1,0:T(8,128)(2,1)S(1)}, bf16[84,16,128]{2,1,0:T(8,128)(2,1)S(1)}, u32[]{:S(2)}, u32[]{:S(2)}) collective-permute-start(bf16[84,16,128]{2,1,0:T(8,128)(2,1)S(1)} %get-tuple-element.37), channel_id=1, source_target_pairs={{0,3},{1,4},{2,5},{3,6},{4,7},{5,0},{6,1},{7,2},{8,11},{9,12},{10,... | collective-permute-start | bytes 1032200 | tf_op jit(solution)/shard_map/ppermute | solution.py:62
  22.1 0.3 collective-permute-start.13
  22.4 1.1 %collective-permute-done.6.beside_flop = bf16[48,16,128]{2,1,0:T(8,128)(2,1)S(1)} collective-permute-done((bf16[48,16,128]{2,1,0:T(8,128)(2,1)S(1)}, bf16[48,16,128]{2,1,0:T(8,128)(2,1)S(1)}, u32[]{:S(2)}, u32[]{:S(2)}) %collective-permute-start.6) | collective-permute-done | bytes 196640 | tf_op jit(solution)/shard_map/ppermute | solution.py:62
  23.5 0.0 collective-permute-done.5.beside_flip
  23.5 0.0 copy-start.3
  23.5 7.3 %shard_map.115 = (bf16[2,64,512]{2,1,0:T(8,128)(2,1)S(1)}, bf16[16,128]{1,0:T(8,128)(2,1)S(1)}) custom-call(s32[2,27]{1,0:T(2,128)S(1)} %copy-done.1, bf16[48,16,128]{2,1,0:T(8,128)(2,1)S(1)} %get-tuple-element.32.facing_flip, bf16[48,16,128]{2,1,0:T(8,128)(2,1)S(1)} %get-tuple-element.29._.facing_flop, ...), custom_call_target="tpu_custom_call" | custom-call | flops 8049999872 | tf_op jit(solution)/shard_map/pallas_call | solution.py:567
  30.9 3.2 %collective-permute-start.7 = (bf16[16,128]{1,0:T(8,128)(2,1)S(1)}, bf16[16,128]{1,0:T(8,128)(2,1)S(1)}, u32[]{:S(2)}, u32[]{:S(2)}) collective-permute-start(bf16[16,128]{1,0:T(8,128)(2,1)S(1)} %get-tuple-element.35), channel_id=1, source_target_pairs={{0,8},{1,9},{2,10},{3,11},{4,12},{5,13},{6,14},{7,15},{8,0},{9,1},... | collective-permute-start | bytes 12296 | tf_op jit(solution)/shard_map/ppermute | solution.py:62
  34.1 1.0 %collective-permute-done.7 = bf16[16,128]{1,0:T(8,128)(2,1)S(1)} collective-permute-done((bf16[16,128]{1,0:T(8,128)(2,1)S(1)}, bf16[16,128]{1,0:T(8,128)(2,1)S(1)}, u32[]{:S(2)}, u32[]{:S(2)}) %collective-permute-start.7) | collective-permute-done | bytes 4128 | tf_op jit(solution)/shard_map/ppermute | solution.py:62
  35.1 2.1 %collective-permute-start.14 = (bf16[84,16,128]{2,1,0:T(8,128)(2,1)S(1)}, bf16[84,16,128]{2,1,0:T(8,128)(2,1)S(1)}, u32[]{:S(2)}, u32[]{:S(2)}) collective-permute-start(bf16[84,16,128]{2,1,0:T(8,128)(2,1)S(1)} %get-tuple-element.37), channel_id=1, source_target_pairs={{0,16},{1,17},{2,18},{3,19},{4,20},{5,21},{6,22},{7,23},{8,24},{9,... | collective-permute-start | bytes 1032200 | tf_op jit(solution)/shard_map/ppermute | solution.py:62
  37.2 0.1 collective-permute-start.15
  37.3 0.4 collective-permute-start.16
  37.7 2.3 %collective-permute-start.9 = (bf16[2,16,128]{2,1,0:T(8,128)(2,1)S(1)}, bf16[2,16,128]{2,1,0:T(8,128)(2,1)S(1)}, u32[]{:S(2)}, u32[]{:S(2)}) collective-permute-start(bf16[2,16,128]{2,1,0:T(8,128)(2,1)S(1)} %shard_map.116.refs_0_), channel_id=1, source_target_pairs={{0,7},{1,2},{2,1},{3,4},{4,3},{5,6},{6,5},{7,0},{8,15},{9,10},{10,... | collective-permute-start | bytes 24584 | tf_op jit(solution)/shard_map/ppermute | solution.py:62
  40.0 0.2 collective-permute-done.8.refs_1_
  40.2 2.1 %collective-permute-done.9.refs_2_ = bf16[2,16,128]{2,1,0:T(8,128)(2,1)S(1)} collective-permute-done((bf16[2,16,128]{2,1,0:T(8,128)(2,1)S(1)}, bf16[2,16,128]{2,1,0:T(8,128)(2,1)S(1)}, u32[]{:S(2)}, u32[]{:S(2)}) %collective-permute-start.9) | collective-permute-done | bytes 8224 | tf_op jit(solution)/shard_map/ppermute | solution.py:62
  42.3 1.2 %collective-permute-start.10 = (bf16[6,16,128]{2,1,0:T(8,128)(2,1)S(1)}, bf16[6,16,128]{2,1,0:T(8,128)(2,1)S(1)}, u32[]{:S(2)}, u32[]{:S(2)}) collective-permute-start(bf16[6,16,128]{2,1,0:T(8,128)(2,1)S(1)} %shard_map.117.own), channel_id=1, source_target_pairs={{0,16},{1,17},{2,18},{3,19},{4,20},{5,21},{6,22},{7,23},{8,24},{9,... | collective-permute-start | bytes 73736 | tf_op jit(solution)/shard_map/ppermute | solution.py:62
  43.6 1.3 %collective-permute-start.11 = (bf16[6,16,128]{2,1,0:T(8,128)(2,1)S(1)}, bf16[6,16,128]{2,1,0:T(8,128)(2,1)S(1)}, u32[]{:S(2)}, u32[]{:S(2)}) collective-permute-start(bf16[6,16,128]{2,1,0:T(8,128)(2,1)S(1)} %shard_map.117.own), channel_id=1, source_target_pairs={{0,112},{1,113},{2,114},{3,115},{4,116},{5,117},{6,118},{7,119},{8... | collective-permute-start | bytes 73736 | tf_op jit(solution)/shard_map/ppermute | solution.py:62
  44.8 0.3 shard_map.109.chosen_ref
  45.8 1.1 %collective-permute-done.11.above = bf16[6,16,128]{2,1,0:T(8,128)(2,1)S(1)} collective-permute-done((bf16[6,16,128]{2,1,0:T(8,128)(2,1)S(1)}, bf16[6,16,128]{2,1,0:T(8,128)(2,1)S(1)}, u32[]{:S(2)}, u32[]{:S(2)}) %collective-permute-start.11) | collective-permute-done | bytes 24608 | tf_op jit(solution)/shard_map/ppermute | solution.py:62
  46.8 2.2 %shard_map.118 = bf16[2,64,512]{2,1,0:T(8,128)(2,1)} custom-call(s32[1]{0:T(128)S(6)} %copy.12.live_ref, bf16[432,288]{1,0:T(8,128)(2,1)S(1)} %shard_map.109.chosen_ref, bf16[6,16,128]{2,1,0:T(8,128)(2,1)S(1)} %shard_map.117.own, bf16[6,16,128]{2,1,0:T(8,128)(2,1)S(1)} %collective-permute-done.10.below, ...), custom_call_target="tpu_custom_call" | custom-call | flops 2760000000 | tf_op jit(solution)/shard_map/pallas_call | solution.py:609
  (20 shorter events, 0.1 us)
Async XLA Ops:
  1.2 6.6 %collective-permute-start = (bf16[30,16,128]{2,1,0:T(8,128)(2,1)S(1)}, bf16[30,16,128]{2,1,0:T(8,128)(2,1)S(1)}, u32[]{:S(2)}, u32[]{:S(2)}) collective-permute-start(bf16[30,16,128]{2,1,0:T(8,128)(2,1)S(1)} %get-tuple-element.24._.packet_ref), channel_id=1, source_target_pairs={{0,8},{1,9},{2,10},{3,11},{4,12},{5,13},{6,14},{7,15},{8,0},{9,1},... | collective-permute-start | bytes 368648 | tf_op jit(solution)/shard_map/ppermute | solution.py:62
  7.8 5.1 %collective-permute-start.3 = (bf16[24,16,128]{2,1,0:T(8,128)(2,1)S(1)}, bf16[24,16,128]{2,1,0:T(8,128)(2,1)S(1)}, u32[]{:S(2)}, u32[]{:S(2)}) collective-permute-start(bf16[24,16,128]{2,1,0:T(8,128)(2,1)S(1)} %get-tuple-element.27.own_flip), channel_id=1, source_target_pairs={{0,1},{1,0},{2,3},{3,2},{4,5},{5,4},{6,7},{7,6},{8,9},{9,8},{10,11... | collective-permute-start | bytes 294920 | tf_op jit(solution)/shard_map/ppermute | solution.py:62
  9.1 5.6 %collective-permute-start.4 = (bf16[24,16,128]{2,1,0:T(8,128)(2,1)S(1)}, bf16[24,16,128]{2,1,0:T(8,128)(2,1)S(1)}, u32[]{:S(2)}, u32[]{:S(2)}) collective-permute-start(bf16[24,16,128]{2,1,0:T(8,128)(2,1)S(1)} %get-tuple-element.28.own_flop), channel_id=1, source_target_pairs={{0,7},{1,2},{2,1},{3,4},{4,3},{5,6},{6,5},{7,0},{8,15},{9,10},{10,... | collective-permute-start | bytes 294920 | tf_op jit(solution)/shard_map/ppermute | solution.py:62
  11.9 7.9 %collective-permute-start.1 = (bf16[28,16,128]{2,1,0:T(8,128)(2,1)S(1)}, bf16[28,16,128]{2,1,0:T(8,128)(2,1)S(1)}, u32[]{:S(2)}, u32[]{:S(2)}) collective-permute-start(bf16[28,16,128]{2,1,0:T(8,128)(2,1)S(1)} %get-tuple-element.26.own_ref), channel_id=1, source_target_pairs={{0,1},{1,0},{2,3},{3,2},{4,5},{5,4},{6,7},{7,6},{8,9},{9,8},{10,11... | collective-permute-start | bytes 344072 | tf_op jit(solution)/shard_map/ppermute | solution.py:62
  11.9 7.9 %collective-permute-start.2 = (bf16[28,16,128]{2,1,0:T(8,128)(2,1)S(1)}, bf16[28,16,128]{2,1,0:T(8,128)(2,1)S(1)}, u32[]{:S(2)}, u32[]{:S(2)}) collective-permute-start(bf16[28,16,128]{2,1,0:T(8,128)(2,1)S(1)} %get-tuple-element.26.own_ref), channel_id=1, source_target_pairs={{0,7},{1,2},{2,1},{3,4},{4,3},{5,6},{6,5},{7,0},{8,15},{9,10},{10,... | collective-permute-start | bytes 344072 | tf_op jit(solution)/shard_map/ppermute | solution.py:62
  14.7 8.8 %collective-permute-start.6 = (bf16[48,16,128]{2,1,0:T(8,128)(2,1)S(1)}, bf16[48,16,128]{2,1,0:T(8,128)(2,1)S(1)}, u32[]{:S(2)}, u32[]{:S(2)}) collective-permute-start(bf16[48,16,128]{2,1,0:T(8,128)(2,1)S(1)} %get-tuple-element.29._.facing_flop), channel_id=1, source_target_pairs={{0,112},{1,113},{2,114},{3,115},{4,116},{5,117},{6,118},{7,119},{8... | collective-permute-start | bytes 589832 | tf_op jit(solution)/shard_map/ppermute | solution.py:62
  19.9 3.7 %copy-start.1 = (s32[2,27]{1,0:T(2,128)S(1)}, s32[2,27]{1,0:T(2,128)}, u32[]{:S(2)}) copy-start(s32[2,27]{1,0:T(2,128)} %neighbour_ref.2) | copy-start | bytes 652
  19.9 3.7 %collective-permute-start.5 = (bf16[48,16,128]{2,1,0:T(8,128)(2,1)S(1)}, bf16[48,16,128]{2,1,0:T(8,128)(2,1)S(1)}, u32[]{:S(2)}, u32[]{:S(2)}) collective-permute-start(bf16[48,16,128]{2,1,0:T(8,128)(2,1)S(1)} %get-tuple-element.32.facing_flip), channel_id=1, source_target_pairs={{0,16},{1,17},{2,18},{3,19},{4,20},{5,21},{6,22},{7,23},{8,24},{9,... | collective-permute-start | bytes 589832 | tf_op jit(solution)/shard_map/ppermute | solution.py:62
  19.9 17.2 %collective-permute-start.12 = (bf16[84,16,128]{2,1,0:T(8,128)(2,1)S(1)}, bf16[84,16,128]{2,1,0:T(8,128)(2,1)S(1)}, u32[]{:S(2)}, u32[]{:S(2)}) collective-permute-start(bf16[84,16,128]{2,1,0:T(8,128)(2,1)S(1)} %get-tuple-element.37), channel_id=1, source_target_pairs={{0,3},{1,4},{2,5},{3,6},{4,7},{5,0},{6,1},{7,2},{8,11},{9,12},{10,... | collective-permute-start | bytes 1032200 | tf_op jit(solution)/shard_map/ppermute | solution.py:62
  22.1 15.2 %collective-permute-start.13 = (bf16[56,16,128]{2,1,0:T(8,128)(2,1)S(1)}, bf16[56,16,128]{2,1,0:T(8,128)(2,1)S(1)}, u32[]{:S(2)}, u32[]{:S(2)}) collective-permute-start(bf16[56,16,128]{2,1,0:T(8,128)(2,1)S(1)} %get-tuple-element.36), channel_id=1, source_target_pairs={{0,5},{1,6},{2,7},{3,0},{4,1},{5,2},{6,3},{7,4},{8,13},{9,14},{10,... | collective-permute-start | bytes 688136 | tf_op jit(solution)/shard_map/ppermute | solution.py:62
  23.5 21.3 %copy-start.2 = (f32[2,432,27]{2,1,0:T(8,128)S(1)}, f32[2,432,27]{2,1,0:T(8,128)}, u32[]{:S(2)}) copy-start(f32[2,432,27]{2,1,0:T(8,128)} %constant.4.clone.taps_ref) | copy-start | bytes 279940
  23.5 21.3 %copy-start.3 = (f32[432,1]{1,0:T(8,128)S(1)}, f32[432,1]{1,0:T(8,128)}, u32[]{:S(2)}) copy-start(f32[432,1]{1,0:T(8,128)} %constant.5.clone.voxel_ref) | copy-start | bytes 5188
  30.9 4.2 %collective-permute-start.7 = (bf16[16,128]{1,0:T(8,128)(2,1)S(1)}, bf16[16,128]{1,0:T(8,128)(2,1)S(1)}, u32[]{:S(2)}, u32[]{:S(2)}) collective-permute-start(bf16[16,128]{1,0:T(8,128)(2,1)S(1)} %get-tuple-element.35), channel_id=1, source_target_pairs={{0,8},{1,9},{2,10},{3,11},{4,12},{5,13},{6,14},{7,15},{8,0},{9,1},... | collective-permute-start | bytes 12296 | tf_op jit(solution)/shard_map/ppermute | solution.py:62
  35.1 11.8 %copy-start = (bf16[64,128]{1,0:T(8,128)(2,1)S(1)}, bf16[64,128]{1,0:T(8,128)(2,1)}, u32[]{:S(2)}) copy-start(bf16[64,128]{1,0:T(8,128)(2,1)} %w_output.1) | copy-start | bytes 49156
  35.1 11.7 %collective-permute-start.14 = (bf16[84,16,128]{2,1,0:T(8,128)(2,1)S(1)}, bf16[84,16,128]{2,1,0:T(8,128)(2,1)S(1)}, u32[]{:S(2)}, u32[]{:S(2)}) collective-permute-start(bf16[84,16,128]{2,1,0:T(8,128)(2,1)S(1)} %get-tuple-element.37), channel_id=1, source_target_pairs={{0,16},{1,17},{2,18},{3,19},{4,20},{5,21},{6,22},{7,23},{8,24},{9,... | collective-permute-start | bytes 1032200 | tf_op jit(solution)/shard_map/ppermute | solution.py:62
  37.2 9.6 %collective-permute-start.15 = (bf16[84,16,128]{2,1,0:T(8,128)(2,1)S(1)}, bf16[84,16,128]{2,1,0:T(8,128)(2,1)S(1)}, u32[]{:S(2)}, u32[]{:S(2)}) collective-permute-start(bf16[84,16,128]{2,1,0:T(8,128)(2,1)S(1)} %collective-permute-done.12), channel_id=1, source_target_pairs={{0,16},{1,17},{2,18},{3,19},{4,20},{5,21},{6,22},{7,23},{8,24},{9,... | collective-permute-start | bytes 1032200 | tf_op jit(solution)/shard_map/ppermute | solution.py:62
  37.3 9.5 %collective-permute-start.16 = (bf16[56,16,128]{2,1,0:T(8,128)(2,1)S(1)}, bf16[56,16,128]{2,1,0:T(8,128)(2,1)S(1)}, u32[]{:S(2)}, u32[]{:S(2)}) collective-permute-start(bf16[56,16,128]{2,1,0:T(8,128)(2,1)S(1)} %collective-permute-done.13), channel_id=1, source_target_pairs={{0,16},{1,17},{2,18},{3,19},{4,20},{5,21},{6,22},{7,23},{8,24},{9,... | collective-permute-start | bytes 688136 | tf_op jit(solution)/shard_map/ppermute | solution.py:62
  37.7 2.5 %collective-permute-start.8 = (bf16[2,16,128]{2,1,0:T(8,128)(2,1)S(1)}, bf16[2,16,128]{2,1,0:T(8,128)(2,1)S(1)}, u32[]{:S(2)}, u32[]{:S(2)}) collective-permute-start(bf16[2,16,128]{2,1,0:T(8,128)(2,1)S(1)} %shard_map.116.refs_0_), channel_id=1, source_target_pairs={{0,1},{1,0},{2,3},{3,2},{4,5},{5,4},{6,7},{7,6},{8,9},{9,8},{10,11... | collective-permute-start | bytes 24584 | tf_op jit(solution)/shard_map/ppermute | solution.py:62
  37.7 4.6 %collective-permute-start.9 = (bf16[2,16,128]{2,1,0:T(8,128)(2,1)S(1)}, bf16[2,16,128]{2,1,0:T(8,128)(2,1)S(1)}, u32[]{:S(2)}, u32[]{:S(2)}) collective-permute-start(bf16[2,16,128]{2,1,0:T(8,128)(2,1)S(1)} %shard_map.116.refs_0_), channel_id=1, source_target_pairs={{0,7},{1,2},{2,1},{3,4},{4,3},{5,6},{6,5},{7,0},{8,15},{9,10},{10,... | collective-permute-start | bytes 24584 | tf_op jit(solution)/shard_map/ppermute | solution.py:62
  42.3 3.4 %collective-permute-start.10 = (bf16[6,16,128]{2,1,0:T(8,128)(2,1)S(1)}, bf16[6,16,128]{2,1,0:T(8,128)(2,1)S(1)}, u32[]{:S(2)}, u32[]{:S(2)}) collective-permute-start(bf16[6,16,128]{2,1,0:T(8,128)(2,1)S(1)} %shard_map.117.own), channel_id=1, source_target_pairs={{0,16},{1,17},{2,18},{3,19},{4,20},{5,21},{6,22},{7,23},{8,24},{9,... | collective-permute-start | bytes 73736 | tf_op jit(solution)/shard_map/ppermute | solution.py:62
  43.6 3.3 %collective-permute-start.11 = (bf16[6,16,128]{2,1,0:T(8,128)(2,1)S(1)}, bf16[6,16,128]{2,1,0:T(8,128)(2,1)S(1)}, u32[]{:S(2)}, u32[]{:S(2)}) collective-permute-start(bf16[6,16,128]{2,1,0:T(8,128)(2,1)S(1)} %shard_map.117.own), channel_id=1, source_target_pairs={{0,112},{1,113},{2,114},{3,115},{4,116},{5,117},{6,118},{7,119},{8... | collective-permute-start | bytes 73736 | tf_op jit(solution)/shard_map/ppermute | solution.py:62
